TPU v7x, 1024 devices: a whole 4x8x16 slice. The times are simulated.
1024 devices in a mesh: dp: 32 (over x, z_lo), tensor: 32 (over z_hi, y, core).
Axes of the slice: x: 4, y: 8, z: 16 (z_hi: 2, z_lo: 8; z = z_hi * 8 + z_lo), core: 2. Of those that a mesh axis runs over, the one named last changes fastest.
Arguments:
- x_source: bfloat16 [2048, 4096], P('dp', 'tensor'), may hold values from -6 to 6
- grad_out: bfloat16 [4096, 4096], P('dp'), may hold values from -6 to 6
- w_query: bfloat16 [4096, 4096], P(None, 'tensor'), may hold values from -0.09375 to 0.09375
- w_kv: bfloat16 [4096, 1024], P(None, 'tensor'), may hold values from -0.09375 to 0.09375
- w_out: bfloat16 [4096, 4096], P('tensor'), may hold values from -0.5 to 0.5
- lengths: int32 [32, 4], replicated, may hold values from 1 to 32, 64 in all within a row
- dest: int32 [32, 4], replicated, may hold values from 0 to 31, as said below
Outputs:
- grad_input: bfloat16 [4096, 4096], P('dp', 'tensor')
- grad_query: float32 [4096, 4096], P('dp', 'tensor')
- grad_kv: float32 [4096, 1024], P('dp', 'tensor')
- grad_wout: float32 [4096, 4096], P('tensor', 'dp')
Inputs may be any that keep to these rules, and one draw needn't show every extreme that they name: `dest`: sequence j of every group g goes to group (g + c_j) mod 32 for 4 distinct shifts c_j, so each group receives exactly 4 sequences, at most one from any group. Each group's 4 lengths sum to 64, and the longest of all is 32.
All inputs are finite; a program needn't handle non-finite values.
Results may differ from a plain program's by a relative error of at most 0.034.
Values may be sent and summed in bfloat16 or wider, within the bound.
No kernel may reach another device: no remote copies, remote signals or barrier semaphores. Data moves between devices by JAX's collectives and lax.ppermute only.
A program may use at most 32 MiB of HBM per device.

v0:
```python
import math

import jax
import jax.numpy as jnp
from jax import lax
from jax.sharding import PartitionSpec as P


def rope_tables(positions, head_dim):
    half_dim = head_dim // 2
    frequency = jnp.exp(
        jnp.arange(half_dim, dtype=jnp.float32) * (-2.0 * math.log(1000000.0) / head_dim)
    )
    angles = positions.astype(jnp.float32)[..., None] * frequency
    cosine = jnp.cos(angles)
    sine = jnp.sin(angles)
    return (jnp.concatenate([cosine, cosine], -1), jnp.concatenate([sine, sine], -1))


def rotate(vectors, cosine, sine):
    half_dim = vectors.shape[-1] // 2
    leading = vectors[..., :half_dim]
    trailing = vectors[..., half_dim:]
    turned = jnp.concatenate([-trailing, leading], -1)
    return vectors * cosine + turned * sine


def arrangement(lengths, dest):
    groups = dest.shape[0]
    seq_total = dest.shape[1]
    starts = jnp.cumsum(lengths, axis=1) - lengths
    targets = jnp.arange(groups, dtype=jnp.int32)
    matches = (dest[None, :, :] == targets[:, None, None]).astype(jnp.int32)
    is_live = jnp.sum(matches, axis=2)
    ranking = (1 - is_live) * groups + targets[None, :]
    senders = jnp.argsort(ranking, axis=1)[:, :seq_total]
    picked = jnp.take_along_axis(matches, senders[:, :, None], axis=1)
    seq_choice = jnp.sum(picked * jnp.arange(seq_total, dtype=jnp.int32), axis=2)
    return (senders, starts, lengths[senders, seq_choice])


def contract_rows(left, right):
    return lax.dot_general(
        left, right, (((0,), (0,)), ((), ())), preferred_element_type=jnp.float32
    )


def contract_cols(left, right):
    return lax.dot_general(
        left, right, (((1,), (1,)), ((), ())), preferred_element_type=jnp.float32
    )


def block_pass(xblock, grad_block, is_valid, cosine, sine, w_query, w_kv, w_out):
    seq_count, longest, width = xblock.shape
    row_count = seq_count * longest
    head_dim = w_query.shape[1]
    flat_rows = xblock.reshape(row_count, width)
    queries = jnp.dot(flat_rows, w_query, preferred_element_type=jnp.float32).astype(jnp.bfloat16)
    queries = rotate(
        queries.reshape(seq_count, longest, head_dim).astype(jnp.float32), cosine, sine
    ).astype(jnp.bfloat16)
    kv_part = jnp.dot(flat_rows, w_kv, preferred_element_type=jnp.float32).astype(jnp.bfloat16)
    kv_all = lax.all_gather(kv_part, "tensor", axis=1, tiled=True)
    kv_heads = kv_all.shape[1] // (2 * head_dim)
    group_size = lax.axis_size("tensor") // kv_heads
    own_head = lax.axis_index("tensor") // group_size
    kv_own = lax.dynamic_slice_in_dim(kv_all, own_head * 2 * head_dim, 2 * head_dim, 1)
    kv_own = kv_own.reshape(seq_count, longest, 2, head_dim)
    key_rot = rotate(kv_own[:, :, 0].astype(jnp.float32), cosine, sine).astype(jnp.bfloat16)
    values = kv_own[:, :, 1]
    inv_scale = 1.0 / math.sqrt(head_dim)
    position_in = jnp.arange(longest)
    scores = (
        jnp.einsum("sqd,skd->sqk", queries, key_rot, preferred_element_type=jnp.float32) * inv_scale
    )
    allowed = (position_in[:, None] >= position_in[None, :]) & is_valid[:, None, :]
    scores = jnp.where(allowed, scores, -1e30)
    highest = jnp.max(scores, axis=-1, keepdims=True)
    weights = jnp.exp(scores - highest) * allowed.astype(jnp.float32)
    attn_probs = (
        weights
        / jnp.sum(weights, axis=-1, keepdims=True)
        * is_valid[:, :, None].astype(jnp.float32)
    )
    probs_low = attn_probs.astype(jnp.bfloat16)
    outputs = jnp.einsum(
        "sqk,skd->sqd", probs_low, values, preferred_element_type=jnp.float32
    ).astype(jnp.bfloat16)
    grad_att = (
        contract_cols(grad_block, w_out).astype(jnp.bfloat16).reshape(seq_count, longest, head_dim)
    )
    grad_probs = jnp.einsum("sqd,skd->sqk", grad_att, values, preferred_element_type=jnp.float32)
    centre = jnp.sum(attn_probs * grad_probs, axis=-1, keepdims=True)
    grad_scores = (attn_probs * (grad_probs - centre) * inv_scale).astype(jnp.bfloat16)
    grad_qrot = jnp.einsum("sqk,skd->sqd", grad_scores, key_rot, preferred_element_type=jnp.float32)
    grad_krot = jnp.einsum("sqk,sqd->skd", grad_scores, queries, preferred_element_type=jnp.float32)
    grad_values = jnp.einsum(
        "sqk,sqd->skd", probs_low, grad_att, preferred_element_type=jnp.float32
    )
    grad_queries = (
        rotate(grad_qrot, cosine, -sine).astype(jnp.bfloat16).reshape(row_count, head_dim)
    )
    grad_keys = rotate(grad_krot, cosine, -sine)
    kv_term = jnp.stack([grad_keys, grad_values], axis=2).reshape(row_count, 2 * head_dim)
    selector = (jnp.arange(kv_heads) == own_head).astype(jnp.float32)
    spread = (kv_term[:, None, :] * selector[None, :, None]).reshape(
        row_count, kv_heads * 2 * head_dim
    )
    kv_grad = lax.psum_scatter(
        spread.astype(jnp.bfloat16), "tensor", scatter_dimension=1, tiled=True
    )
    partial_value = contract_cols(grad_queries, w_query) + contract_cols(kv_grad, w_kv)
    grad_input = lax.psum_scatter(
        partial_value.astype(jnp.bfloat16), "tensor", scatter_dimension=1, tiled=True
    )
    grad_wq = contract_rows(flat_rows, grad_queries)
    grad_wkv = contract_rows(flat_rows, kv_grad)
    grad_wo = contract_rows(outputs.reshape(row_count, head_dim), grad_block)
    return (grad_input, grad_wq, grad_wkv, grad_wo)


def body(x_source, grad_out, w_query, w_kv, w_out, lengths, dest):
    groups = lax.axis_size("dp")
    seq_total = dest.shape[1]
    longest = grad_out.shape[0] // seq_total
    own_group = lax.axis_index("dp")
    senders, starts, seq_len = arrangement(lengths, dest)
    own_dest = lax.dynamic_index_in_dim(dest, own_group, 0, keepdims=False)
    own_start = lax.dynamic_index_in_dim(starts, own_group, 0, keepdims=False)
    own_len = lax.dynamic_index_in_dim(lengths, own_group, 0, keepdims=False)
    targets = jnp.arange(groups, dtype=jnp.int32)
    matches = (own_dest[None, :] == targets[:, None]).astype(jnp.int32)
    first_row = jnp.sum(matches * own_start[None, :], axis=1)
    seq_count = jnp.sum(matches * own_len[None, :], axis=1)
    position_in = jnp.arange(longest, dtype=jnp.int32)
    is_live = position_in[None, :] < seq_count[:, None]
    row_index = jnp.where(is_live, first_row[:, None] + position_in[None, :], 0)
    outgoing = jnp.where(is_live[:, :, None], x_source[row_index], jnp.zeros((), x_source.dtype))
    received = lax.all_to_all(outgoing, "dp", split_axis=0, concat_axis=0, tiled=True)
    my_senders = lax.dynamic_index_in_dim(senders, own_group, 0, keepdims=False)
    my_len = lax.dynamic_index_in_dim(seq_len, own_group, 0, keepdims=False)
    xslice = received[my_senders]
    xblock = lax.all_gather(xslice, "tensor", axis=2, tiled=True)
    is_valid = position_in[None, :] < my_len[:, None]
    positions = jnp.broadcast_to(position_in[None, :], (seq_total, longest))
    cosine, sine = rope_tables(positions, w_query.shape[1])
    grad_input, grad_wq, grad_wkv, grad_wo = block_pass(
        xblock, grad_out, is_valid, cosine, sine, w_query, w_kv, w_out
    )
    grad_query, grad_kv, grad_wout = (
        lax.psum_scatter(
            grad_wq.astype(jnp.bfloat16), "dp", scatter_dimension=0, tiled=True
        ).astype(jnp.float32),
        lax.psum_scatter(
            grad_wkv.astype(jnp.bfloat16), "dp", scatter_dimension=0, tiled=True
        ).astype(jnp.float32),
        lax.psum_scatter(
            grad_wo.astype(jnp.bfloat16), "dp", scatter_dimension=1, tiled=True
        ).astype(jnp.float32),
    )
    return (grad_input, grad_query, grad_kv, grad_wout)


def solution(mesh):
    placed = (
        P("dp", "tensor"),
        P("dp", None),
        P(None, "tensor"),
        P(None, "tensor"),
        P("tensor", None),
        P(),
        P(),
    )
    return jax.shard_map(
        body,
        mesh=mesh,
        in_specs=placed,
        out_specs=(P("dp", "tensor"), P("dp", "tensor"), P("dp", "tensor"), P("tensor", "dp")),
        check_vma=False,
    )
```

profile of v0, /device:TPU:6, one launch (start us, length us, event | category | flops | bytes accessed | tf_op | source)
XLA Modules:
  0.0 1247.2 jit_solution(12772076607426129679)
XLA Ops:
  12.4 3.6 gather_fusion.1
  16.9 18.8 %all-to-all-start = ((bf16[32,32,128]{2,1,0:T(8,128)(2,1)}), bf16[32,32,128]{2,1,0:T(8,128)(2,1)S(1)}, u32[]{:S(2)}, u32[]{:S(2)}) async-start(bf16[32,32,128]{2,1,0:T(8,128)(2,1)} %broadcast_select_fusion), calls=%async_computation | async-start | bytes 524288 | tf_op jit(solution)/shard_map/all_to_all | solution.py:140
  35.9 17.2 %all-to-all-done = bf16[32,32,128]{2,1,0:T(8,128)(2,1)S(1)} async-done(((bf16[32,32,128]{2,1,0:T(8,128)(2,1)}), bf16[32,32,128]{2,1,0:T(8,128)(2,1)S(1)}, u32[]{:S(2)}, u32[]{:S(2)}) %all-to-all-start) | async-done | bytes 262176 | tf_op jit(solution)/shard_map/all_to_all | solution.py:140
  53.1 1.2 gather_fusion.2
  54.8 1.2 gather_fusion.3
  57.0 1.5 gather_fusion
  59.6 1.7 convolution_convert_fusion.3
  61.3 101.2 %all-gather.3.cloned.1.call-done = bf16[4,32,4096]{2,1,0:T(8,128)(2,1)} async-done(((bf16[4,32,128]{2,1,0:T(8,128)(2,1)}), bf16[4,32,4096]{2,1,0:T(8,128)(2,1)}) %all-gather.3.cloned.1.call-update) | async-done | bytes 1048592 | tf_op jit(solution)/shard_map/all_gather | solution.py:144
  162.5 1.7 convolution_convert_fusion.4
  165.4 66.7 %all_gather.7 = bf16[128,1024]{0,1:T(8,128)(2,1)S(1)} all-gather(bf16[128,32]{0,1:T(8,128)(2,1)S(1)} %convolution_convert_fusion.5), channel_id=1, replica_groups=mesh['dp'=32,'tensor'=32] {'tensor'}, dimensions={1}, use_global_device_ids=true | all-gather | bytes 270336 | tf_op jit(solution)/shard_map/all_gather | solution.py:64
  233.2 1.7 fusion.21
  241.3 144.2 %reduce-scatter.16.cloned.1.call-done = bf16[32,128]{1,0:T(8,128)(2,1)} async-done(((bf16[1024,128]{1,0:T(8,128)(2,1)}), bf16[32,128]{1,0:T(8,128)(2,1)}) %reduce-scatter.16.cloned.1.call-update) | async-done | bytes 8208
  386.5 1.3 copy.56
  388.8 1.4 fusion.2
  390.3 2.3 copy.54
  392.9 1.4 convolution_convert_fusion
  394.3 2.3 copy.58
  396.7 1.5 fusion.3
  398.1 207.3 %reduce-scatter.20.cloned.1.call-done = bf16[128,32]{1,0:T(8,128)(2,1)} async-done(((bf16[4096,32]{1,0:T(8,128)(2,1)}), bf16[128,32]{1,0:T(8,128)(2,1)}) %reduce-scatter.20.cloned.1.call-update) | async-done | bytes 8208
  606.9 172.0 %reduce-scatter.18.cloned.1.call-done = bf16[128,128]{1,0:T(8,128)(2,1)} async-done(((bf16[4096,128]{1,0:T(8,128)(2,1)}), bf16[128,128]{1,0:T(8,128)(2,1)}) %reduce-scatter.18.cloned.1.call-update) | async-done | bytes 32784
  778.9 1.5 copy.55
  780.4 218.0 %reduce-scatter.22.cloned.1.call-done = bf16[128,128]{1,0:T(8,128)(2,1)} async-done(((bf16[4096,128]{1,0:T(8,128)(2,1)}), bf16[128,128]{1,0:T(8,128)(2,1)}) %reduce-scatter.22.cloned.1.call-update) | async-done | bytes 32784
  999.9 239.0 %reduce-scatter.14.cloned.1.call-done = bf16[128,128]{1,0:T(8,128)(2,1)} async-done(((bf16[4096,128]{1,0:T(8,128)(2,1)}), bf16[128,128]{1,0:T(8,128)(2,1)}) %reduce-scatter.14.cloned.1.call-update) | async-done | bytes 32784 | tf_op jit(solution)/shard_map/reduce_scatter | solution.py:152
  1238.9 1.4 convert_element_type.112
  (108 shorter events, 22.4 us)
Async XLA Ops:
  7.2 155.3 %copy-start = (bf16[4096,128]{1,0:T(8,128)(2,1)S(1)}, bf16[4096,128]{1,0:T(8,128)(2,1)}, u32[]{:S(2)}) copy-start(bf16[4096,128]{1,0:T(8,128)(2,1)} %param.9) | copy-start | bytes 3145732
  12.4 44.6 %copy-start.1 = (s32[32,4]{0,1:T(4,128)S(1)}, s32[32,4]{0,1:T(4,128)}, u32[]{:S(2)}) copy-start(s32[32,4]{0,1:T(4,128)} %param.12) | copy-start | bytes 1540
  16.9 36.1 %all-to-all-start = ((bf16[32,32,128]{2,1,0:T(8,128)(2,1)}), bf16[32,32,128]{2,1,0:T(8,128)(2,1)S(1)}, u32[]{:S(2)}, u32[]{:S(2)}) async-start(bf16[32,32,128]{2,1,0:T(8,128)(2,1)} %broadcast_select_fusion), calls=%async_computation | async-start | bytes 524288 | tf_op jit(solution)/shard_map/all_to_all | solution.py:140
  35.8 126.7 %all-gather.3.cloned.1.call-start = ((), (), s32[]{:S(2)}) async-start(), calls=%async_computation.7 | async-start | bytes 1081344 | tf_op jit(solution)/shard_map/all_gather | solution.py:144
  54.3 331.3 %reduce-scatter.16.cloned.1.call-start = ((), (), s32[]{:S(2)}) async-start(), calls=%async_computation.8 | async-start | bytes 270336
  57.0 2.5 copy-start.3
  59.6 105.3 %copy-start.4 = (bf16[4096,32]{0,1:T(8,128)(2,1)S(1)}, bf16[4096,32]{0,1:T(8,128)(2,1)}, u32[]{:S(2)}) copy-start(bf16[4096,32]{0,1:T(8,128)(2,1)} %param.10) | copy-start | bytes 786436
  162.4 2.4 copy-start.2
  165.3 74.5 %copy-start.6 = (f32[4,32,64]{2,1,0:T(8,128)S(1)}, f32[4,32,64]{2,1,0:T(8,128)}, u32[]{:S(2)}) copy-start(f32[4,32,64]{2,1,0:T(8,128)} %get-tuple-element.21) | copy-start | bytes 98308
  235.8 0.6 copy-start.8
  235.8 4.5 copy-start.10
  241.3 364.2 %reduce-scatter.20.cloned.1.call-start = ((), (), s32[]{:S(2)}) async-start(), calls=%async_computation.10 | async-start | bytes 1081344
  387.9 0.9 copy-start.5
  387.9 1.0 copy-start.7
  387.9 391.0 %reduce-scatter.18.cloned.1.call-start = ((), (), s32[]{:S(2)}) async-start(), calls=%async_computation.9 | async-start | bytes 1081344
  390.3 2.4 copy-start.9
  390.3 2.4 copy-start.11
  392.6 605.8 %reduce-scatter.22.cloned.1.call-start = ((), (), s32[]{:S(2)}) async-start(), calls=%async_computation.11 | async-start | bytes 1081344
  396.6 842.3 %reduce-scatter.14.cloned.1.call-start = ((), (), s32[]{:S(2)}) async-start(), calls=%async_computation.6 | async-start | bytes 1081344 | tf_op jit(solution)/shard_map/reduce_scatter | solution.py:152
Sparse Core Ops, SparseCore 0:
  54.4 108.0 all-gather.2
  241.4 144.1 reduce-scatter.15
  389.3 216.1 reduce-scatter.19
  611.1 167.7 reduce-scatter.17
  782.1 216.2 reduce-scatter.21
  1002.0 236.9 reduce-scatter.13
where the time goes:
time: 1270 us; the launch traced here: 1250 us
  waiting for transfers between devices  1100 us (87%)
  blocking collectives  66.7 us (5%)
  local copies, waits for them, and re-layouts  22.5 us (2%)
  starting transfers between devices  19.1 us (2%)
  matrix products  14.7 us (1%)
  between operations  14.5 us (1%)
    unnamed x10, waiting for transfers between devices  742 us
    reduce_scatter x1, waiting for transfers between devices, body(): lax.psum_scatter(grad_wq.astype(jnp.bfloat16), 'dp', scatter_dimension=0,...  239 us
    all_gather x1, waiting for transfers between devices, body(): xblock = lax.all_gather(xslice, 'tensor', axis=2, tiled=True)  101 us
    all_gather x1, blocking collectives, block_pass(): kv_all = lax.all_gather(kv_part, 'tensor', axis=1, tiled=True)  66.7 us
  transfers between devices with their start and end apart: 7, of which 7 were waited for; matrix products, arithmetic and copies ran while one was open for 2% of the time, Pallas kernels for 0%

commit v1 on v0

v1 whole, which is shorter than its diff:
```python
import math

import jax
import jax.numpy as jnp
import numpy as np
from jax import lax
from jax.experimental import pallas as pl
from jax.experimental.pallas import tpu as pltpu
from jax.sharding import Mesh
from jax.sharding import PartitionSpec as P

DP = ("x", "zl")
YY = ("yh", "yl")
TP = ("zh", "yh", "yl", "c")
PEERS = ("yl", "c")
F32 = jnp.float32
BF16 = jnp.bfloat16


def dot(left, right, dims):
    return lax.dot_general(left, right, (dims, ((), ())), preferred_element_type=F32)


def tables(longest, seq_total, head_dim):
    frequency = np.exp(
        np.arange(head_dim // 2, dtype=np.float32) * np.float32(-2.0 * math.log(1000000.0) / head_dim)
    ).astype(np.float32)
    angles = (np.arange(longest, dtype=np.float32)[:, None] * frequency).astype(np.float32)
    cosine, sine = np.cos(angles), np.sin(angles)
    cosine = np.tile(np.concatenate([cosine, cosine], -1), (seq_total, 1)).astype(np.float32)
    signed = np.tile(np.concatenate([-sine, sine], -1), (seq_total, 1)).astype(np.float32)
    return cosine, signed


def block_at(zh, y, c):
    return zh * 16 + y * 2 + c


def project_kernel(x_ref, wq_ref, wkv_ref, q_ref, kv_ref):
    rows = x_ref.shape[3]
    q = jnp.zeros((rows, 128), F32)
    kv = jnp.zeros((32, rows), F32)
    for c in range(2):
        for y in range(8):
            for zh in range(2):
                xb = x_ref[c, y, zh]
                cut = pl.ds(block_at(zh, y, c) * 128, 128)
                q = q + dot(xb, wq_ref[cut, :], ((1,), (0,)))
                kv = kv + dot(wkv_ref[cut, :], xb, ((0,), (1,)))
    q_ref[...] = q.astype(BF16)
    kv_ref[...] = kv.astype(BF16)


def attention_kernel(longest, len_ref, q_ref, kv_ref, ga_ref, cos_ref, sin_ref, cost_ref, sint_ref,
                     o_ref, gq_ref, kvg_ref):
    rows, hd = q_ref.shape
    inv_scale = 1.0 / math.sqrt(hd)

    def turn(v):
        return jnp.concatenate([v[:, hd // 2:], v[:, : hd // 2]], 1)

    def turn_t(v):
        return jnp.concatenate([v[hd // 2:], v[: hd // 2]], 0)

    cosine, sine, cosine_t, sine_t = cos_ref[...], sin_ref[...], cost_ref[...], sint_ref[...]
    q = q_ref[...].astype(F32)
    q = (q * cosine + turn(q) * sine).astype(BF16)
    k = kv_ref[:hd, :].astype(F32)
    k = (k * cosine_t + turn_t(k) * sine_t).astype(BF16)
    v = kv_ref[hd:, :]
    ga = ga_ref[...]
    qi = lax.broadcasted_iota(jnp.int32, (rows, rows), 0)
    ki = lax.broadcasted_iota(jnp.int32, (rows, rows), 1)
    ends = jnp.zeros((rows, rows), jnp.int32)
    starts = jnp.zeros((rows, rows), jnp.int32)
    for slot in range(rows // longest):
        here = (qi >= slot * longest) & (qi < (slot + 1) * longest)
        starts = jnp.where(here, slot * longest, starts)
        ends = jnp.where(here, slot * longest + len_ref[slot], ends)
    allowed = (ki >= starts) & (ki <= qi) & (ki < ends)
    scores = jnp.where(allowed, dot(q, k, ((1,), (0,))) * inv_scale, -1e30)
    highest = jnp.max(scores, axis=1, keepdims=True)
    weights = jnp.where(allowed, jnp.exp(scores - highest), 0.0)
    probs = weights / jnp.sum(weights, axis=1, keepdims=True)
    probs = jnp.where(qi < ends, probs, 0.0)
    low = probs.astype(BF16)
    o_ref[...] = dot(low, v, ((1,), (1,))).astype(BF16)
    gp = dot(ga, v, ((1,), (0,)))
    centre = jnp.sum(probs * gp, axis=1, keepdims=True)
    gs = (probs * (gp - centre) * inv_scale).astype(BF16)
    gq = dot(gs, k, ((1,), (1,)))
    gq_ref[...] = (gq * cosine - turn(gq) * sine).astype(BF16)
    gk = dot(q, gs, ((0,), (0,)))
    kvg_ref[:hd, :] = (gk * cosine_t - turn_t(gk) * sine_t).astype(BF16)
    kvg_ref[hd:, :] = dot(ga, low, ((0,), (0,))).astype(BF16)


def product_kernel(own_ref, x_ref, go_ref, wq_ref, wkv_ref, o_ref, gq_ref, kvg_ref, gw_ref, mine_ref, other_ref):
    gq = gq_ref[...]
    out = o_ref[...]
    kvg = kvg_ref[...]
    for zh in range(2):
        for y in range(8):
            for c in range(2):
                block = block_at(zh, y, c)
                cut = pl.ds(block * 128, 128)
                xb = x_ref[c, y, zh]
                to = (block // 8, block % 8)
                gw_ref[to[0], to[1], 0:128, :] = dot(xb, gq, ((0,), (0,))).astype(BF16)
                gw_ref[to[0], to[1], 128:256, :] = dot(out, go_ref[:, cut], ((0,), (0,))).astype(BF16)
                gw_ref[to[0], to[1], 256:288, :] = dot(kvg, xb, ((1,), (0,))).astype(BF16)
    own = own_ref[0]
    for c in range(2):
        for y in range(8):
            for zh in range(2):
                cut = pl.ds(block_at(zh, y, c) * 128, 128)
                part = dot(gq, wq_ref[cut, :], ((1,), (1,))) + dot(kvg, wkv_ref[cut, :], ((0,), (1,)))
                part = part.astype(BF16)

                @pl.when(own == c)
                def _():
                    mine_ref[y, zh] = part

                @pl.when(own != c)
                def _():
                    other_ref[y, zh] = part


def body(x_source, grad_out, w_query, w_kv, w_out, lengths, dest):
    groups, seq_total = dest.shape
    rows = grad_out.shape[0]
    longest = rows // seq_total
    group = lax.axis_index(DP)
    own_zh = lax.axis_index("zh")
    own_c = lax.axis_index("c")
    swap = [(0, 1), (1, 0)]
    vmem = pl.BlockSpec(memory_space=pltpu.VMEM)
    smem = pl.BlockSpec(memory_space=pltpu.SMEM)
    params = pltpu.CompilerParams(vmem_limit_bytes=40 * 1024 * 1024)
    shape = jax.ShapeDtypeStruct

    shifts = dest[0]
    own_len = lax.dynamic_index_in_dim(lengths, group, 0, keepdims=False)
    own_start = jnp.cumsum(own_len) - own_len
    own_dest = (group + shifts) % groups
    slot = jnp.arange(groups, dtype=jnp.int32)[:, None, None, None]
    place = jnp.arange(longest, dtype=jnp.int32)[None, :, None, None]
    token = jnp.arange(x_source.shape[0], dtype=jnp.int32)[None, None, :, None]
    chosen = (slot == own_dest) & (place < own_len) & (token == own_start + place)
    chosen = jnp.any(chosen, axis=3).astype(BF16).reshape(groups * longest, -1)
    outgoing = dot(chosen, x_source, ((1,), (0,))).astype(BF16).reshape(groups, longest, -1)
    received = lax.all_to_all(outgoing, DP, 0, 0, tiled=True)

    sender = (group - shifts) % groups
    length = jnp.sum(
        jnp.where(jnp.arange(groups)[:, None] == sender[None, :], lengths, 0), axis=0
    )
    rank = jnp.sum((sender[None, :] < sender[:, None]).astype(jnp.int32), axis=1)
    pick = rank[None, :] == jnp.arange(seq_total)[:, None]
    my_senders = jnp.sum(jnp.where(pick, sender[None, :], 0), axis=1)
    my_len = jnp.sum(jnp.where(pick, length[None, :], 0), axis=1)
    xs = received[my_senders].reshape(rows, -1)

    xo = lax.ppermute(xs, "zh", swap)
    pair = jnp.where(own_zh == 0, jnp.stack([xs, xo]), jnp.stack([xo, xs]))
    wide = lax.all_to_all(jnp.broadcast_to(pair[None], (8,) + pair.shape), YY, 0, 0, tiled=True)
    xall = lax.all_gather(wide, "c", axis=0)

    q, kv = pl.pallas_call(
        project_kernel,
        out_shape=(shape((rows, 128), BF16), shape((32, rows), BF16)),
        in_specs=[vmem] * 3,
        out_specs=(vmem, vmem),
        compiler_params=params,
    )(xall, w_query, w_kv)
    kv = lax.all_to_all(jnp.broadcast_to(kv[None], (8,) + kv.shape), PEERS, 0, 0, tiled=True)
    kv = kv.reshape(256, rows)
    grad_att = dot(grad_out, w_out, ((1,), (1,))).astype(BF16)
    cosine, sine = tables(longest, seq_total, 128)
    out, gq, kvt = pl.pallas_call(
        lambda *refs: attention_kernel(longest, *refs),
        out_shape=(shape((rows, 128), BF16), shape((rows, 128), BF16), shape((256, rows), BF16)),
        in_specs=[smem] + [vmem] * 7,
        out_specs=(vmem,) * 3,
        compiler_params=params,
    )(my_len, q, kv, grad_att, cosine, sine, cosine.T.copy(), sine.T.copy())
    kvt = lax.all_to_all(kvt.reshape(8, 32, rows), PEERS, 0, 0, tiled=True)
    kvg = jnp.sum(kvt.astype(F32), axis=0).astype(BF16)

    gw, mine, other = pl.pallas_call(
        product_kernel,
        out_shape=(shape((4, 8, 288, 128), BF16), shape((8, 2, rows, 128), BF16), shape((8, 2, rows, 128), BF16)),
        in_specs=[smem] + [vmem] * 7,
        out_specs=(vmem,) * 3,
        compiler_params=params,
    )(own_c[None].astype(jnp.int32), xall, grad_out, w_query, w_kv, out, gq, kvg)

    theirs = lax.ppermute(other, "c", swap)
    half = (mine.astype(F32) + theirs.astype(F32)).astype(BF16)
    half = lax.all_to_all(half, YY, 0, 0, tiled=True)
    half = jnp.sum(half.astype(F32), axis=0)
    keep = jnp.where(own_zh == 0, half[0], half[1])
    send = jnp.where(own_zh == 0, half[1], half[0]).astype(BF16)
    grad_input = (keep + lax.ppermute(send, "zh", swap).astype(F32)).astype(BF16)

    gw = lax.all_to_all(gw, "x", 0, 0, tiled=True)
    gw = jnp.sum(gw.astype(F32), axis=0).astype(BF16)
    gw = lax.all_to_all(gw, "zl", 0, 0, tiled=True)
    gw = jnp.sum(gw.astype(F32), axis=0)
    return grad_input, gw[:128], gw[256:].T, gw[128:256]


def solution(mesh):
    fine = Mesh(mesh.devices.reshape(4, 8, 2, 2, 4, 2), ("x", "zl", "zh", "yh", "yl", "c"))
    placed = (P(DP, TP), P(DP, None), P(None, TP), P(None, TP), P(TP, None), P(), P())
    return jax.shard_map(
        body,
        mesh=fine,
        in_specs=placed,
        out_specs=(P(DP, TP), P(DP, TP), P(DP, TP), P(TP, DP)),
        check_vma=False,
    )
```

time: 1270 us -> 250 us (0.20); the launches traced: 1250 us -> 249 us
  waiting for transfers between devices: 1100 us -> 109 us
  starting transfers between devices: 19.1 us -> 68.3 us
  blocking collectives: 66.7 us -> 22.3 us
    unnamed x10 -> x1, waiting for transfers between devices: 742 us -> 0.02 us
    reduce_scatter x1 -> x0, waiting for transfers between devices: 239 us -> none  [body(): lax.psum_scatter(grad_wq.astype(jnp.bfloat16), 'dp', scatter_dimension=0,...]
    all_gather x1, waiting for transfers between devices: 101 us -> 17 us  [body(): xall = lax.all_gather(wide, 'c', axis=0)]
    all_gather x1 -> x0, blocking collectives: 66.7 us -> none  [block_pass(): kv_all = lax.all_gather(kv_part, 'tensor', axis=1, tiled=True)]
    all_to_all x1 -> x6, waiting for transfers between devices: 17.2 us -> 78.4 us  [the longest x1 22.5 us: body(): gw = lax.all_to_all(gw, 'x', 0, 0, tiled=True)]
    all_to_all x1 -> x6, starting transfers between devices: 18.8 us -> 48 us  [the longest x1 18.8 us: body(): received = lax.all_to_all(outgoing, DP, 0, 0, tiled=True)]
    all_to_all x0 -> x1, blocking collectives: none -> 22.3 us  [body(): lax.all_to_all(jnp.broadcast_to(pair[None], (8,) + pair.shape), YY, 0, 0,...]
    ppermute x0 -> x3, starting transfers between devices: none -> 20.2 us  [the longest x1 11.9 us: body(): xo = lax.ppermute(xs, 'zh', swap)]
  transfers between devices with their start and end apart: 7 -> 10, of which waited for: 7 -> 10; matrix products, arithmetic and copies ran while one was open for 2% -> 3% of each run, Pallas kernels for 0% -> 0%
where the time goes in v1:
time: 250 us; the launch traced here: 249 us
  waiting for transfers between devices  109 us (44%)
  starting transfers between devices  68.3 us (27%)
  blocking collectives  22.3 us (9%)
  between operations  14.3 us (6%)
  local copies, waits for them, and re-layouts  13.5 us (5%)
  Pallas kernels  10 us (4%)
  other arithmetic  8.13 us (3%)
  matrix products  3.37 us (1%)
    all_to_all x1, waiting for transfers between devices, body(): gw = lax.all_to_all(gw, 'x', 0, 0, tiled=True)  22.5 us
    all_to_all x1, blocking collectives, body(): lax.all_to_all(jnp.broadcast_to(pair[None], (8,) + pair.shape), YY, 0, 0,...  22.3 us
    all_to_all x1, starting transfers between devices, body(): received = lax.all_to_all(outgoing, DP, 0, 0, tiled=True)  18.8 us
    all_gather x1, waiting for transfers between devices, body(): xall = lax.all_gather(wide, 'c', axis=0)  17 us
    all_to_all x1, waiting for transfers between devices, body(): gw = lax.all_to_all(gw, 'zl', 0, 0, tiled=True)  16.3 us
    all_to_all x1, waiting for transfers between devices, body(): received = lax.all_to_all(outgoing, DP, 0, 0, tiled=True)  16 us
    all_to_all x1, waiting for transfers between devices, body(): half = lax.all_to_all(half, YY, 0, 0, tiled=True)  13.5 us
    ppermute x1, starting transfers between devices, body(): xo = lax.ppermute(xs, 'zh', swap)  11.9 us
  transfers between devices with their start and end apart: 10, of which 10 were waited for; matrix products, arithmetic and copies ran while one was open for 3% of the time, Pallas kernels for 0%

profile of v1, /device:TPU:6, one launch (start us, length us, event | category | flops | bytes accessed | tf_op | source)
XLA Modules:
  0.0 248.7 jit_solution(5125675603912457544)
XLA Ops:
  10.4 1.7 convolution_convert_fusion
  12.1 18.8 %all-to-all-start = ((bf16[32,32,128]{2,1,0:T(8,128)(2,1)}), bf16[32,32,128]{2,1,0:T(8,128)(2,1)S(1)}, u32[]{:S(2)}, u32[]{:S(2)}) async-start(bf16[32,32,128]{2,1,0:T(8,128)(2,1)} %bitcast.3), calls=%async_computation | async-start | bytes 524288 | tf_op jit(solution)/shard_map/all_to_all | solution.py:152
  32.2 16.0 %all-to-all-done = bf16[32,32,128]{2,1,0:T(8,128)(2,1)S(1)} async-done(((bf16[32,32,128]{2,1,0:T(8,128)(2,1)}), bf16[32,32,128]{2,1,0:T(8,128)(2,1)S(1)}, u32[]{:S(2)}, u32[]{:S(2)}) %all-to-all-start) | async-done | bytes 262176 | tf_op jit(solution)/shard_map/all_to_all | solution.py:152
  48.8 11.9 %collective-permute-start = (bf16[128,128]{1,0:T(8,128)(2,1)S(1)}, bf16[128,128]{1,0:T(8,128)(2,1)S(1)}, u32[]{:S(2)}, u32[]{:S(2)}) collective-permute-start(bf16[128,128]{1,0:T(8,128)(2,1)S(1)} %bitcast.32), channel_id=1, source_target_pairs={{0,16},{16,0},{1,17},{17,1},{2,18},{18,2},{3,19},{19,3},{4,20},{20... | collective-permute-start | bytes 98312 | tf_op jit(solution)/shard_map/ppermute | solution.py:164
  60.7 2.6 %collective-permute-done = bf16[128,128]{1,0:T(8,128)(2,1)S(1)} collective-permute-done((bf16[128,128]{1,0:T(8,128)(2,1)S(1)}, bf16[128,128]{1,0:T(8,128)(2,1)S(1)}, u32[]{:S(2)}, u32[]{:S(2)}) %collective-permute-start) | collective-permute-done | bytes 32800 | tf_op jit(solution)/shard_map/ppermute | solution.py:164
  63.4 22.3 %all_to_all.35 = bf16[8,2,128,128]{3,2,1,0:T(8,128)(2,1)} all-to-all(bf16[8,2,128,128]{3,2,1,0:T(8,128)(2,1)S(1)} %broadcast_in_dim.28), channel_id=1, replica_groups=mesh['x'=4,'zl'=8,'zh'=2,'yh'=2,'yl'=4,'c'=2] {'yh','yl'}, dimensions={0} | all-to-all | bytes 1048576 | tf_op jit(solution)/shard_map/all_to_all | solution.py:166
  86.3 17.0 %all-gather.3.cloned.1.call-done = bf16[16,2,128,128]{3,2,1,0:T(8,128)(2,1)} async-done(((bf16[8,2,128,128]{3,2,1,0:T(8,128)(2,1)}), bf16[16,2,128,128]{3,2,1,0:T(8,128)(2,1)}) %all-gather.3.cloned.1.call-update) | async-done | bytes 1048592 | tf_op jit(solution)/shard_map/all_gather | solution.py:167
  106.8 4.6 %all-to-all-start.2 = ((bf16[8,32,128]{2,1,0:T(8,128)(2,1)}), bf16[8,32,128]{2,1,0:T(8,128)(2,1)S(1)}, u32[]{:S(2)}, u32[]{:S(2)}) async-start(bf16[8,32,128]{2,1,0:T(8,128)(2,1)} %broadcast_in_dim.31), calls=%async_computation.2 | async-start | bytes 131072 | tf_op jit(solution)/shard_map/all_to_all | solution.py:176
  113.1 4.2 %all-to-all-done.2 = bf16[8,32,128]{2,1,0:T(8,128)(2,1)S(1)} async-done(((bf16[8,32,128]{2,1,0:T(8,128)(2,1)}), bf16[8,32,128]{2,1,0:T(8,128)(2,1)S(1)}, u32[]{:S(2)}, u32[]{:S(2)}) %all-to-all-start.2) | async-done | bytes 65568 | tf_op jit(solution)/shard_map/all_to_all | solution.py:176
  118.1 1.8 shard_map.139
  120.5 3.4 %all-to-all-start.3 = ((bf16[8,32,128]{2,1,0:T(8,128)(2,1)}), bf16[8,32,128]{2,1,0:T(8,128)(2,1)S(1)}, u32[]{:S(2)}, u32[]{:S(2)}) async-start(bf16[8,32,128]{2,1,0:T(8,128)(2,1)} %bitcast.11), calls=%async_computation.3 | async-start | bytes 131072 | tf_op jit(solution)/shard_map/all_to_all | solution.py:187
  123.8 5.8 %all-to-all-done.3 = bf16[8,32,128]{2,1,0:T(8,128)(2,1)S(1)} async-done(((bf16[8,32,128]{2,1,0:T(8,128)(2,1)}), bf16[8,32,128]{2,1,0:T(8,128)(2,1)S(1)}, u32[]{:S(2)}, u32[]{:S(2)}) %all-to-all-start.3) | async-done | bytes 65568 | tf_op jit(solution)/shard_map/all_to_all | solution.py:187
  132.9 7.3 %shard_map.140 = (bf16[4,8,288,128]{3,2,1,0:T(8,128)(2,1)S(1)}, bf16[8,2,128,128]{3,2,1,0:T(8,128)(2,1)S(1)}, bf16[8,2,128,128]{3,2,1,0:T(8,128)(2,1)S(1)}) custom-call(s32[1]{0:T(128)} %bitcast.own_ref, bf16[2,8,2,128,128]{4,3,2,1,0:T(8,128)(2,1)S(1)} %bitcast.29, bf16[128,4096]{1,0:T(8,128)(2,1)S(1)} %copy-done.4, bf16[4096,128]{1,0:T(8,128)(2,1)S(1)} %copy-done.1, ...), custom_call_target="tpu_custom_call" | custom-call | tf_op jit(solution)/shard_map/pallas_call | solution.py:190
  143.2 6.3 %all-to-all-start.5 = ((bf16[4,8,288,128]{3,2,1,0:T(8,128)(2,1)}), bf16[4,8,288,128]{3,2,1,0:T(8,128)(2,1)}, u32[]{:S(2)}, u32[]{:S(2)}) async-start(bf16[4,8,288,128]{3,2,1,0:T(8,128)(2,1)} %copy-done.5), calls=%async_computation.5 | async-start | bytes 4718592 | tf_op jit(solution)/shard_map/all_to_all | solution.py:206
  149.5 1.9 collective-permute-start.1
  151.4 1.9 collective-permute-done.1
  154.3 22.5 %all-to-all-done.5 = bf16[4,8,288,128]{3,2,1,0:T(8,128)(2,1)} async-done(((bf16[4,8,288,128]{3,2,1,0:T(8,128)(2,1)}), bf16[4,8,288,128]{3,2,1,0:T(8,128)(2,1)}, u32[]{:S(2)}, u32[]{:S(2)}) %all-to-all-start.5) | async-done | bytes 2359328 | tf_op jit(solution)/shard_map/all_to_all | solution.py:206
  176.8 4.3 %all-to-all-start.4 = ((bf16[8,2,128,128]{3,2,1,0:T(8,128)(2,1)}), bf16[8,2,128,128]{3,2,1,0:T(8,128)(2,1)S(1)}, u32[]{:S(2)}, u32[]{:S(2)}) async-start(bf16[8,2,128,128]{3,2,1,0:T(8,128)(2,1)} %add_convert_fusion), calls=%async_computation.4 | async-start | bytes 1048576 | tf_op jit(solution)/shard_map/all_to_all | solution.py:200
  181.1 3.0 %reduce_sum.87 = bf16[8,288,128]{2,1,0:T(8,128)(2,1)} reduce(bf16[4,8,288,128]{3,2,1,0:T(8,128)(2,1)} %all-to-all-done.5, bf16[]{:T(256)} %constant.67.clone.1), dimensions={0}, to_apply=%region_8.9 | reduce | flops 884736 | bytes 2949122 | tf_op jit(solution)/shard_map/reduce_sum | solution.py:207
  184.1 13.5 %all-to-all-done.4 = bf16[8,2,128,128]{3,2,1,0:T(8,128)(2,1)S(1)} async-done(((bf16[8,2,128,128]{3,2,1,0:T(8,128)(2,1)}), bf16[8,2,128,128]{3,2,1,0:T(8,128)(2,1)S(1)}, u32[]{:S(2)}, u32[]{:S(2)}) %all-to-all-start.4) | async-done | bytes 524320 | tf_op jit(solution)/shard_map/all_to_all | solution.py:200
  197.5 10.6 %all-to-all-start.6 = ((bf16[8,288,128]{2,1,0:T(8,128)(2,1)}), bf16[8,288,128]{2,1,0:T(8,128)(2,1)S(1)}, u32[]{:S(2)}, u32[]{:S(2)}) async-start(bf16[8,288,128]{2,1,0:T(8,128)(2,1)} %reduce_sum.87), calls=%async_computation.6 | async-start | bytes 1179648 | tf_op jit(solution)/shard_map/all_to_all | solution.py:208
  208.2 6.5 %collective-permute-start.2 = (bf16[128,128]{1,0:T(8,128)(2,1)S(1)}, bf16[128,128]{1,0:T(8,128)(2,1)S(1)}, u32[]{:S(2)}, u32[]{:S(2)}) collective-permute-start(bf16[128,128]{1,0:T(8,128)(2,1)S(1)} %fusion.1), channel_id=1, source_target_pairs={{0,16},{16,0},{1,17},{17,1},{2,18},{18,2},{3,19},{19,3},{4,20},{20... | collective-permute-start | bytes 98312 | tf_op jit(solution)/shard_map/ppermute | solution.py:204
  214.7 8.9 %collective-permute-done.2 = bf16[128,128]{1,0:T(8,128)(2,1)S(1)} collective-permute-done((bf16[128,128]{1,0:T(8,128)(2,1)S(1)}, bf16[128,128]{1,0:T(8,128)(2,1)S(1)}, u32[]{:S(2)}, u32[]{:S(2)}) %collective-permute-start.2) | collective-permute-done | bytes 32800 | tf_op jit(solution)/shard_map/ppermute | solution.py:204
  224.2 16.3 %all-to-all-done.6 = bf16[8,288,128]{2,1,0:T(8,128)(2,1)S(1)} async-done(((bf16[8,288,128]{2,1,0:T(8,128)(2,1)}), bf16[8,288,128]{2,1,0:T(8,128)(2,1)S(1)}, u32[]{:S(2)}, u32[]{:S(2)}) %all-to-all-start.6) | async-done | bytes 589856 | tf_op jit(solution)/shard_map/all_to_all | solution.py:208
  (71 shorter events, 21.4 us)
Async XLA Ops:
  7.2 104.2 %copy-start = (bf16[128,4096]{1,0:T(8,128)(2,1)S(1)}, bf16[128,4096]{1,0:T(8,128)(2,1)}, u32[]{:S(2)}) copy-start(bf16[128,4096]{1,0:T(8,128)(2,1)} %param.15) | copy-start | bytes 3145732
  7.2 78.6 %copy-start.18 = (bf16[4096,32]{0,1:T(8,128)(2,1)S(1)}, bf16[4096,32]{0,1:T(8,128)(2,1)}, u32[]{:S(2)}) copy-start(bf16[4096,32]{0,1:T(8,128)(2,1)} %param.14) | copy-start | bytes 786436
  10.4 92.9 %copy-start.1 = (bf16[4096,128]{1,0:T(8,128)(2,1)S(1)}, bf16[4096,128]{1,0:T(8,128)(2,1)}, u32[]{:S(2)}) copy-start(bf16[4096,128]{1,0:T(8,128)(2,1)} %wq_ref.3) | copy-start | bytes 3145732
  12.1 36.1 %all-to-all-start = ((bf16[32,32,128]{2,1,0:T(8,128)(2,1)}), bf16[32,32,128]{2,1,0:T(8,128)(2,1)S(1)}, u32[]{:S(2)}, u32[]{:S(2)}) async-start(bf16[32,32,128]{2,1,0:T(8,128)(2,1)} %bitcast.3), calls=%async_computation | async-start | bytes 524288 | tf_op jit(solution)/shard_map/all_to_all | solution.py:152
  30.9 72.4 %all-gather.3.cloned.1.call-start = ((), (), s32[]{:S(2)}) async-start(), calls=%async_computation.7 | async-start | bytes 1572864 | tf_op jit(solution)/shard_map/all_gather | solution.py:167
  48.8 14.5 %collective-permute-start = (bf16[128,128]{1,0:T(8,128)(2,1)S(1)}, bf16[128,128]{1,0:T(8,128)(2,1)S(1)}, u32[]{:S(2)}, u32[]{:S(2)}) collective-permute-start(bf16[128,128]{1,0:T(8,128)(2,1)S(1)} %bitcast.32), channel_id=1, source_target_pairs={{0,16},{16,0},{1,17},{17,1},{2,18},{18,2},{3,19},{19,3},{4,20},{20... | collective-permute-start | bytes 98312 | tf_op jit(solution)/shard_map/ppermute | solution.py:164
  103.3 1.2 copy-start.2
  104.5 12.8 %copy-start.8 = (f32[128,128]{1,0:T(8,128)S(1)}, f32[128,128]{1,0:T(8,128)}, u32[]{:S(2)}) copy-start(f32[128,128]{1,0:T(8,128)} %constant.69.clone.refs_4_) | copy-start | bytes 196612
  104.5 12.8 %copy-start.9 = (f32[128,128]{1,0:T(8,128)S(1)}, f32[128,128]{1,0:T(8,128)}, u32[]{:S(2)}) copy-start(f32[128,128]{1,0:T(8,128)} %constant.70.clone.refs_5_) | copy-start | bytes 196612
  104.5 12.8 %copy-start.10 = (f32[128,128]{1,0:T(8,128)S(1)}, f32[128,128]{1,0:T(8,128)}, u32[]{:S(2)}) copy-start(f32[128,128]{1,0:T(8,128)} %constant.71.clone.refs_6_) | copy-start | bytes 196612
  104.5 12.8 %copy-start.11 = (f32[128,128]{1,0:T(8,128)S(1)}, f32[128,128]{1,0:T(8,128)}, u32[]{:S(2)}) copy-start(f32[128,128]{1,0:T(8,128)} %constant.72.clone.refs_7_) | copy-start | bytes 196612
  106.8 10.5 %all-to-all-start.2 = ((bf16[8,32,128]{2,1,0:T(8,128)(2,1)}), bf16[8,32,128]{2,1,0:T(8,128)(2,1)S(1)}, u32[]{:S(2)}, u32[]{:S(2)}) async-start(bf16[8,32,128]{2,1,0:T(8,128)(2,1)} %broadcast_in_dim.31), calls=%async_computation.2 | async-start | bytes 131072 | tf_op jit(solution)/shard_map/all_to_all | solution.py:176
  120.5 9.2 %all-to-all-start.3 = ((bf16[8,32,128]{2,1,0:T(8,128)(2,1)}), bf16[8,32,128]{2,1,0:T(8,128)(2,1)S(1)}, u32[]{:S(2)}, u32[]{:S(2)}) async-start(bf16[8,32,128]{2,1,0:T(8,128)(2,1)} %bitcast.11), calls=%async_computation.3 | async-start | bytes 131072 | tf_op jit(solution)/shard_map/all_to_all | solution.py:187
  129.7 1.2 copy-start.3
  130.9 1.2 copy-start.4
  140.2 1.4 copy-start.5
  142.4 0.8 copy-start.16
  143.2 6.3 %copy-start.17 = (bf16[8,2,128,128]{3,2,1,0:T(8,128)(2,1)S(1)}, bf16[8,2,128,128]{3,2,1,0:T(8,128)(2,1)}, u32[]{:S(2)}) copy-start(bf16[8,2,128,128]{3,2,1,0:T(8,128)(2,1)} %copy-done.16) | copy-start | bytes 1572868
  143.2 10.1 %copy-start.7 = (bf16[8,2,128,128]{3,2,1,0:T(8,128)(2,1)S(1)}, bf16[8,2,128,128]{3,2,1,0:T(8,128)(2,1)}, u32[]{:S(2)}) copy-start(bf16[8,2,128,128]{3,2,1,0:T(8,128)(2,1)} %copy-done.6) | copy-start | bytes 1572868
  143.2 33.6 %all-to-all-start.5 = ((bf16[4,8,288,128]{3,2,1,0:T(8,128)(2,1)}), bf16[4,8,288,128]{3,2,1,0:T(8,128)(2,1)}, u32[]{:S(2)}, u32[]{:S(2)}) async-start(bf16[4,8,288,128]{3,2,1,0:T(8,128)(2,1)} %copy-done.5), calls=%async_computation.5 | async-start | bytes 4718592 | tf_op jit(solution)/shard_map/all_to_all | solution.py:206
  149.5 3.8 %collective-permute-start.1 = (bf16[8,2,128,128]{3,2,1,0:T(8,128)(2,1)S(1)}, bf16[8,2,128,128]{3,2,1,0:T(8,128)(2,1)S(1)}, u32[]{:S(2)}, u32[]{:S(2)}) collective-permute-start(bf16[8,2,128,128]{3,2,1,0:T(8,128)(2,1)S(1)} %copy-done.17), channel_id=1, source_target_pairs={{0,1},{1,0},{2,3},{3,2},{4,5},{5,4},{6,7},{7,6},{8,9},{9,8},{10,11... | collective-permute-start | bytes 1572872 | tf_op jit(solution)/shard_map/ppermute | solution.py:198
  176.8 20.7 %all-to-all-start.4 = ((bf16[8,2,128,128]{3,2,1,0:T(8,128)(2,1)}), bf16[8,2,128,128]{3,2,1,0:T(8,128)(2,1)S(1)}, u32[]{:S(2)}, u32[]{:S(2)}) async-start(bf16[8,2,128,128]{3,2,1,0:T(8,128)(2,1)} %add_convert_fusion), calls=%async_computation.4 | async-start | bytes 1048576 | tf_op jit(solution)/shard_map/all_to_all | solution.py:200
  197.5 42.9 %all-to-all-start.6 = ((bf16[8,288,128]{2,1,0:T(8,128)(2,1)}), bf16[8,288,128]{2,1,0:T(8,128)(2,1)S(1)}, u32[]{:S(2)}, u32[]{:S(2)}) async-start(bf16[8,288,128]{2,1,0:T(8,128)(2,1)} %reduce_sum.87), calls=%async_computation.6 | async-start | bytes 1179648 | tf_op jit(solution)/shard_map/all_to_all | solution.py:208
  208.2 15.3 %collective-permute-start.2 = (bf16[128,128]{1,0:T(8,128)(2,1)S(1)}, bf16[128,128]{1,0:T(8,128)(2,1)S(1)}, u32[]{:S(2)}, u32[]{:S(2)}) collective-permute-start(bf16[128,128]{1,0:T(8,128)(2,1)S(1)} %fusion.1), channel_id=1, source_target_pairs={{0,16},{16,0},{1,17},{17,1},{2,18},{18,2},{3,19},{19,3},{4,20},{20... | collective-permute-start | bytes 98312 | tf_op jit(solution)/shard_map/ppermute | solution.py:204
  (5 other events, 3.6 us)
Sparse Core Ops, SparseCore 0:
  85.9 17.3 all-gather.2

commit v2 on v1

v2 whole, which is shorter than its diff:
```python
import math

import jax
import jax.numpy as jnp
import numpy as np
from jax import lax
from jax.experimental import pallas as pl
from jax.experimental.pallas import tpu as pltpu
from jax.sharding import Mesh
from jax.sharding import PartitionSpec as P

AXES = ("x", "zb", "za", "zh", "yh", "yl", "c")
SIZES = (4, 2, 4, 2, 2, 4, 2)
DP = ("x", "zb", "za")
YY = ("yh", "yl")
TP = ("zh", "yh", "yl", "c")
PEERS = ("yl", "c")
F32 = jnp.float32
BF16 = jnp.bfloat16
SWAP = [(0, 1), (1, 0)]
G, OX, OC, OYL = 0, 1, 2, 3


def dot(left, right, dims):
    return lax.dot_general(left, right, (dims, ((), ())), preferred_element_type=F32)


def tables(longest, seq_total, head_dim):
    frequency = np.exp(
        np.arange(head_dim // 2, dtype=np.float32) * np.float32(-2.0 * math.log(1000000.0) / head_dim)
    ).astype(np.float32)
    angles = (np.arange(longest, dtype=np.float32)[:, None] * frequency).astype(np.float32)
    cosine, sine = np.cos(angles), np.sin(angles)
    cosine = np.tile(np.concatenate([cosine, cosine], -1), (seq_total, 1)).astype(np.float32)
    signed = np.tile(np.concatenate([-sine, sine], -1), (seq_total, 1)).astype(np.float32)
    return cosine, signed


def aligned(index, size):
    return pl.ds(pl.multiple_of(index * size, size), size)


def incoming(ids_ref, dest_ref):
    groups, seq_total = dest_ref.shape
    senders = [lax.rem(ids_ref[G] + groups - dest_ref[0, j], groups) for j in range(seq_total)]
    ranks = []
    for j in range(seq_total):
        rank = jnp.int32(0)
        for i in range(seq_total):
            rank = rank + (senders[i] < senders[j]).astype(jnp.int32)
        ranks.append(rank)
    return senders, ranks


def outgoing_kernel(ids_ref, len_ref, dest_ref, x_ref, out_ref):
    groups, seq_total = dest_ref.shape
    longest = out_ref.shape[1]
    tokens = x_ref.shape[0]
    group = ids_ref[G]
    out_ref[...] = jnp.zeros_like(out_ref)
    place = lax.broadcasted_iota(jnp.int32, (longest, tokens), 0)
    token = lax.broadcasted_iota(jnp.int32, (longest, tokens), 1)
    start = jnp.int32(0)
    for j in range(seq_total):
        size = len_ref[group, j]
        chosen = jnp.where((token == place + start) & (place < size), 1.0, 0.0).astype(BF16)
        to = lax.rem(group + dest_ref[0, j], groups)
        out_ref[to] = dot(chosen, x_ref[...], ((1,), (0,))).astype(BF16)
        start = start + size


def incoming_kernel(ids_ref, dest_ref, x_ref, *refs):
    out_ref = refs[-1]
    longest = x_ref.shape[1]
    senders, ranks = incoming(ids_ref, dest_ref)
    for sender, rank in zip(senders, ranks):
        rows = x_ref[sender]
        for i in range(out_ref.shape[0]):
            out_ref[i, aligned(rank, longest), :] = rows


def head_kernel(ids_ref, *refs):
    out_ref = refs[-1]
    for rel in range(4):
        for flip in range(2):
            peer = (ids_ref[OYL] ^ rel) * 2 + (ids_ref[OC] ^ flip)
            source = refs[rel] if flip == 0 else refs[4].at[rel]
            out_ref[aligned(peer, 32), :] = source[...]


def attention_kernel(longest, ids_ref, len_ref, dest_ref, xm_ref, xt_ref, wq_ref, wh_ref, ga_ref,
                     cos_ref, sin_ref, cost_ref, sint_ref, o_ref, gq_ref, kvg_ref, gap_ref):
    rows, hd = ga_ref.shape
    inv_scale = 1.0 / math.sqrt(hd)

    def turn(v):
        return jnp.concatenate([v[:, hd // 2:], v[:, : hd // 2]], 1)

    def turn_t(v):
        return jnp.concatenate([v[hd // 2:], v[: hd // 2]], 0)

    q = jnp.zeros((rows, hd), F32)
    kv = jnp.zeros((2 * hd, rows), F32)
    for x_ref, c in ((xm_ref, ids_ref[OC]), (xt_ref, 1 - ids_ref[OC])):
        for i in range(16):
            cut = aligned(i * 2 + c, 128)
            q = q + dot(x_ref[i], wq_ref[cut, :], ((1,), (0,)))
            kv = kv + dot(wh_ref[:, cut], x_ref[i], ((1,), (1,)))
    cosine, sine, cosine_t, sine_t = cos_ref[...], sin_ref[...], cost_ref[...], sint_ref[...]
    q = q.astype(BF16).astype(F32)
    q = (q * cosine + turn(q) * sine).astype(BF16)
    kv = kv.astype(BF16)
    k = kv[:hd].astype(F32)
    k = (k * cosine_t + turn_t(k) * sine_t).astype(BF16)
    v = kv[hd:]
    ga = ga_ref[...]
    qi = lax.broadcasted_iota(jnp.int32, (rows, rows), 0)
    ki = lax.broadcasted_iota(jnp.int32, (rows, rows), 1)
    ends = jnp.zeros((rows, rows), jnp.int32)
    starts = jnp.zeros((rows, rows), jnp.int32)
    senders, ranks = incoming(ids_ref, dest_ref)
    for j in range(rows // longest):
        first = ranks[j] * longest
        here = (qi >= first) & (qi < first + longest)
        starts = jnp.where(here, first, starts)
        ends = jnp.where(here, first + len_ref[senders[j], j], ends)
    allowed = (ki >= starts) & (ki <= qi) & (ki < ends)
    scores = jnp.where(allowed, dot(q, k, ((1,), (0,))) * inv_scale, -1e30)
    highest = jnp.max(scores, axis=1, keepdims=True)
    weights = jnp.where(allowed, jnp.exp(scores - highest), 0.0)
    probs = weights / jnp.sum(weights, axis=1, keepdims=True)
    probs = jnp.where(qi < ends, probs, 0.0)
    low = probs.astype(BF16)
    o_ref[...] = dot(low, v, ((1,), (1,))).astype(BF16)
    gp = dot(ga, v, ((1,), (0,)))
    centre = jnp.sum(probs * gp, axis=1, keepdims=True)
    gs = (probs * (gp - centre) * inv_scale).astype(BF16)
    gq = dot(gs, k, ((1,), (1,)))
    gq_ref[...] = (gq * cosine - turn(gq) * sine).astype(BF16)
    gk = dot(q, gs, ((0,), (0,)))
    gk = (gk * cosine_t - turn_t(gk) * sine_t).astype(BF16)
    gv = dot(ga, low, ((0,), (0,))).astype(BF16)
    kvg_ref[:hd, :] = gk
    kvg_ref[hd:, :] = gv
    gap_ref[:, :hd] = gk.astype(F32).T.astype(BF16)
    gap_ref[:, hd:] = gv.astype(F32).T.astype(BF16)


def input_kernel(ids_ref, wq_ref, wh_ref, gq_ref, kvt_ref, mine_ref, other_ref):
    gq, kvt = gq_ref[...], kvt_ref[...]
    for out_ref, c in ((other_ref, 1 - ids_ref[OC]), (mine_ref, ids_ref[OC])):
        for y in range(8):
            for zh in range(2):
                cut = aligned(zh * 16 + y * 2 + c, 128)
                part = dot(gq, wq_ref[cut, :], ((1,), (1,))) + dot(kvt, wh_ref[:, cut], ((1,), (0,)))
                out_ref[y, zh] = part.astype(BF16)


def row_of(yl, c):
    return ((yl & 1) * 2 + c) * 2 + (yl >> 1)


def weight_kernel(ids_ref, xm_ref, xt_ref, go_ref, o_ref, gq_ref, *out_refs):
    gq, out = gq_ref[...], o_ref[...]
    for s in (1, 2, 3, 0):
        x = (ids_ref[OX] + s) & 3
        for x_ref, c in ((xm_ref, ids_ref[OC]), (xt_ref, 1 - ids_ref[OC])):
            for yl in range(4):
                row = row_of(yl, c)
                out_refs[s][row, 0:128, :] = dot(x_ref[x * 4 + yl], gq, ((0,), (0,))).astype(BF16)
                cut = aligned(x * 8 + yl * 2 + c, 128)
                out_refs[s][row, 128:256, :] = dot(out, go_ref[:, cut], ((0,), (0,))).astype(BF16)


def half_kernel(mine_ref, theirs_ref, after_ref, out_ref):
    out_ref[...] = (mine_ref[...].astype(F32) + theirs_ref[...].astype(F32)).astype(BF16)


def kv_kernel(ids_ref, xm_ref, xt_ref, kvt_ref, *out_refs):
    kvg = jnp.sum(kvt_ref[...].astype(F32), axis=0).astype(BF16)
    for s in (1, 2, 3, 0):
        x = (ids_ref[OX] + s) & 3
        for x_ref, c in ((xm_ref, ids_ref[OC]), (xt_ref, 1 - ids_ref[OC])):
            for yl in range(4):
                part = dot(kvg, x_ref[x * 4 + yl], ((1,), (0,)))
                out_refs[s][row_of(yl, c)] = part.astype(BF16)


def sum_kernel(*refs):
    out_ref = refs[-1]
    out_ref[:, 0:256, :] = sum(ref[...].astype(F32) for ref in refs[:4]).astype(BF16)
    out_ref[:, 256:288, :] = sum(ref[...].astype(F32) for ref in refs[4:8]).astype(BF16)


def body(x_source, grad_out, w_query, w_kv, w_out, lengths, dest):
    groups, seq_total = dest.shape
    rows = grad_out.shape[0]
    longest = rows // seq_total
    vmem = pl.BlockSpec(memory_space=pltpu.VMEM)
    smem = pl.BlockSpec(memory_space=pltpu.SMEM)
    anyw = pl.BlockSpec(memory_space=pl.ANY)
    params = pltpu.CompilerParams(vmem_limit_bytes=32 * 1024 * 1024)
    shape = jax.ShapeDtypeStruct
    own_x, own_c, own_yl = lax.axis_index("x"), lax.axis_index("c"), lax.axis_index("yl")
    own_zh, own_zb = lax.axis_index("zh"), lax.axis_index("zb")
    ids = jnp.stack([lax.axis_index(DP), own_x, own_c, own_yl]).astype(jnp.int32)

    def call(kernel, ins, outs, out_shape, **extra):
        return pl.pallas_call(
            kernel, out_shape=out_shape, in_specs=ins, out_specs=outs, compiler_params=params, **extra
        )

    outgoing = call(outgoing_kernel, [smem] * 3 + [vmem], vmem, shape((groups, longest, 128), BF16))(
        ids, lengths, dest, x_source
    )
    received = lax.all_to_all(outgoing, DP, 0, 0, tiled=True)
    w_own = w_kv.T
    w_parts = [w_own] + [lax.ppermute(w_own, "yl", [(i, i ^ s) for i in range(4)]) for s in (1, 2, 3)]
    w_there = lax.ppermute(jnp.stack(w_parts), "c", SWAP)
    w_head = call(head_kernel, [smem] + [vmem] * 5, vmem, shape((256, w_kv.shape[0]), BF16))(
        ids, *w_parts, w_there
    )
    grad_att = dot(grad_out, w_out, ((1,), (1,))).astype(BF16)

    spread = call(incoming_kernel, [smem] * 2 + [vmem] + [anyw] * 3, vmem, shape((16, rows, 128), BF16))(
        ids, dest, received, *w_parts[1:]
    )
    x_mine = lax.all_to_all(spread, ("zh",) + YY, 0, 0, tiled=True)
    x_there = lax.ppermute(x_mine, "c", SWAP)

    cosine, sine = tables(longest, seq_total, 128)
    out, gq, kv_term, kv_turned = call(
        lambda *refs: attention_kernel(longest, *refs),
        [smem] * 3 + [vmem] * 9,
        (vmem,) * 4,
        (shape((rows, 128), BF16), shape((rows, 128), BF16), shape((256, rows), BF16), shape((rows, 256), BF16)),
    )(ids, lengths, dest, x_mine, x_there, w_query, w_head, grad_att, cosine, sine, cosine.T.copy(), sine.T.copy())
    kv_terms = lax.all_to_all(kv_term.reshape(8, 32, rows), PEERS, 0, 0, tiled=True)

    half = shape((8, 2, rows, 128), BF16)
    mine, other = call(input_kernel, [smem] + [vmem] * 4, (vmem,) * 2, (half, half))(
        ids, w_query, w_head, gq, kv_turned
    )
    theirs = lax.ppermute(other, "c", SWAP)
    gw = call(weight_kernel, [smem] + [vmem] * 5, (vmem,) * 4, (shape((8, 256, 128), BF16),) * 4)(
        ids, x_mine, x_there, grad_out, out, gq
    )
    part = call(half_kernel, [vmem] * 2 + [anyw], vmem, half)(mine, theirs, gw[0])
    gkv = call(kv_kernel, [smem] + [vmem] * 3, (vmem,) * 4, (shape((8, 32, 128), BF16),) * 4)(
        ids, x_mine, x_there, kv_terms
    )
    part = lax.all_to_all(part, YY, 0, 0, tiled=True)
    part = jnp.sum(part.astype(F32), axis=0)
    keep = jnp.where(own_zh == 0, part[0], part[1])
    send = jnp.where(own_zh == 0, part[1], part[0]).astype(BF16)
    grad_input = (keep + lax.ppermute(send, "zh", SWAP).astype(F32)).astype(BF16)

    around = [[(i, (i + s) % 4) for i in range(4)] for s in range(4)]
    gw = [gw[0]] + [lax.ppermute(gw[s], "x", around[s]) for s in (1, 2, 3)]
    gkv = [gkv[0]] + [lax.ppermute(gkv[s], "x", around[s]) for s in (1, 2, 3)]
    total = call(sum_kernel, [vmem] * 8, vmem, shape((8, 288, 128), BF16))(*gw, *gkv)
    total = lax.all_to_all(total.reshape(4, 576, 128), "za", 0, 0, tiled=True)
    total = jnp.sum(total.astype(F32), axis=0).reshape(2, 288, 128)
    keep = jnp.where(own_zb == 0, total[0], total[1])
    send = jnp.where(own_zb == 0, total[1], total[0]).astype(BF16)
    total = keep + lax.ppermute(send, "zb", SWAP).astype(F32)
    return grad_input, total[:128], total[256:].T, total[128:256]


def solution(mesh):
    fine = Mesh(mesh.devices.reshape(SIZES), AXES)
    placed = (P(DP, TP), P(DP, None), P(None, TP), P(None, TP), P(TP, None), P(), P())
    return jax.shard_map(
        body,
        mesh=fine,
        in_specs=placed,
        out_specs=(P(DP, TP), P(DP, TP), P(DP, TP), P(TP, DP)),
        check_vma=False,
    )
```

time: 250 us -> 210 us (0.84)
  waiting for transfers between devices: 109 us -> 63 us
  starting transfers between devices: 68.3 us -> 114 us
  blocking collectives: 22.3 us -> 0 us
  between operations: 14.3 us -> 1.03 us
  Pallas kernels: 10 us -> 14.9 us
  other arithmetic: 8.13 us -> 4.02 us
  local copies, waits for them, and re-layouts: 13.5 us -> 10.3 us
  matrix products: 3.37 us -> 0.54 us
    all_to_all x5 -> x4, waiting for transfers between devices: 62.3 us -> 26.7 us  [the longest x1 15.8 us: body(): x_mine = lax.all_to_all(spread, ('zh',) + YY, 0, 0, tiled=True)]
    ppermute x3 -> x14, starting transfers between devices: 20.2 us -> 50.1 us  [the longest x1 12.6 us: body(): total = keep + lax.ppermute(send, 'zb', SWAP).astype(F32)]
    ppermute x3 -> x14, waiting for transfers between devices: 13.4 us -> 36.2 us  [the longest x3 17.2 us: body(): gkv = [gkv[0]] + [lax.ppermute(gkv[s], 'x', around[s]) for s in (1, 2, 3)]]
    all_to_all x1 -> x0, blocking collectives: 22.3 us -> none  [body(): lax.all_to_all(jnp.broadcast_to(pair[None], (8,) + pair.shape), YY, 0, 0,...]
    all_gather x1 -> x0, waiting for transfers between devices: 17 us -> none  [body(): xall = lax.all_gather(wide, 'c', axis=0)]
    all_to_all x1, waiting for transfers between devices: 16 us -> 0.01 us  [body(): received = lax.all_to_all(outgoing, DP, 0, 0, tiled=True)]
    all_to_all x5 -> x4, starting transfers between devices: 29.1 us -> 44.9 us  [the longest x1 18.5 us: body(): x_mine = lax.all_to_all(spread, ('zh',) + YY, 0, 0, tiled=True)]
    pallas_call x3 -> x9, Pallas kernels: 10 us -> 14.9 us  [the longest x1 3.52 us: body(): call(lambda *refs: attention_kernel(longest, *refs), [smem] * 3 + [vmem]...]
  transfers between devices with their start and end apart: 10 -> 19, of which waited for: 10 -> 8; matrix products, arithmetic and copies ran while one was open for 3% -> 2% of each run, Pallas kernels for 0% -> 3%
where the time goes in v2:
time: 210 us; the launch traced here: 208 us
  starting transfers between devices  114 us (54%)
  waiting for transfers between devices  63 us (30%)
  Pallas kernels  14.9 us (7%)
  local copies, waits for them, and re-layouts  10.3 us (5%)
  other arithmetic  4.02 us (2%)
    all_to_all x1, starting transfers between devices, body(): received = lax.all_to_all(outgoing, DP, 0, 0, tiled=True)  18.8 us
    all_to_all x1, starting transfers between devices, body(): x_mine = lax.all_to_all(spread, ('zh',) + YY, 0, 0, tiled=True)  18.5 us
    ppermute x3, waiting for transfers between devices, body(): gkv = [gkv[0]] + [lax.ppermute(gkv[s], 'x', around[s]) for s in (1, 2, 3)]  17.2 us
    ppermute x3, waiting for transfers between devices, body(): lax.ppermute(w_own, 'yl', [(i, i ^ s) for i in range(4)])  16.7 us
    all_to_all x1, starting transfers between devices, body(): total = lax.all_to_all(total.reshape(4, 576, 128), 'za', 0, 0, tiled=True)  16.2 us
    all_to_all x1, waiting for transfers between devices, body(): x_mine = lax.all_to_all(spread, ('zh',) + YY, 0, 0, tiled=True)  15.8 us
    ppermute x1, starting transfers between devices, body(): total = keep + lax.ppermute(send, 'zb', SWAP).astype(F32)  12.6 us
    all_to_all x1, waiting for transfers between devices, body(): total = lax.all_to_all(total.reshape(4, 576, 128), 'za', 0, 0, tiled=True)  11 us
  transfers between devices with their start and end apart: 19, of which 8 were waited for; matrix products, arithmetic and copies ran while one was open for 2% of the time, Pallas kernels for 3%

profile of v2, /device:TPU:6, one launch (start us, length us, event | category | flops | bytes accessed | tf_op | source)
XLA Modules:
  0.0 207.6 jit_solution(17072777265022481013)
XLA Ops:
  5.0 18.8 %all-to-all-start = ((bf16[32,32,128]{2,1,0:T(8,128)(2,1)}), bf16[32,32,128]{2,1,0:T(8,128)(2,1)S(1)}, u32[]{:S(2)}, u32[]{:S(2)}) async-start(bf16[32,32,128]{2,1,0:T(8,128)(2,1)} %shard_map.139), calls=%async_computation | async-start | bytes 524288 | tf_op jit(solution)/shard_map/all_to_all | solution.py:216
  23.8 3.6 %collective-permute-start = (bf16[32,4096]{1,0:T(8,128)(2,1)}, bf16[32,4096]{1,0:T(8,128)(2,1)S(1)}, u32[]{:S(2)}, u32[]{:S(2)}) collective-permute-start(bf16[32,4096]{1,0:T(8,128)(2,1)} %bitcast.25), channel_id=1, source_target_pairs={{0,2},{2,0},{4,6},{6,4},{1,3},{3,1},{5,7},{7,5},{8,10},{10,8},{12,... | collective-permute-start | bytes 786440 | tf_op jit(solution)/shard_map/ppermute | solution.py:218
  27.5 4.5 %collective-permute-start.1 = (bf16[32,4096]{1,0:T(8,128)(2,1)}, bf16[32,4096]{1,0:T(8,128)(2,1)S(1)}, u32[]{:S(2)}, u32[]{:S(2)}) collective-permute-start(bf16[32,4096]{1,0:T(8,128)(2,1)} %bitcast.26), channel_id=1, source_target_pairs={{0,4},{2,6},{4,0},{6,2},{1,5},{3,7},{5,1},{7,3},{8,12},{10,14},{12... | collective-permute-start | bytes 786440 | tf_op jit(solution)/shard_map/ppermute | solution.py:218
  32.0 2.1 %collective-permute-start.2 = (bf16[32,4096]{1,0:T(8,128)(2,1)}, bf16[32,4096]{1,0:T(8,128)(2,1)S(1)}, u32[]{:S(2)}, u32[]{:S(2)}) collective-permute-start(bf16[32,4096]{1,0:T(8,128)(2,1)} %bitcast.27), channel_id=1, source_target_pairs={{0,6},{2,4},{4,2},{6,0},{1,7},{3,5},{5,3},{7,1},{8,14},{10,12},{12... | collective-permute-start | bytes 786440 | tf_op jit(solution)/shard_map/ppermute | solution.py:218
  34.1 2.6 %collective-permute-done.refs_1_.refs_0_ = bf16[32,4096]{1,0:T(8,128)(2,1)S(1)} collective-permute-done((bf16[32,4096]{1,0:T(8,128)(2,1)}, bf16[32,4096]{1,0:T(8,128)(2,1)S(1)}, u32[]{:S(2)}, u32[]{:S(2)}) %collective-permute-start) | collective-permute-done | bytes 262176 | tf_op jit(solution)/shard_map/ppermute | solution.py:218
  36.8 14.1 %collective-permute-done.1.refs_2_.refs_1_ = bf16[32,4096]{1,0:T(8,128)(2,1)S(1)} collective-permute-done((bf16[32,4096]{1,0:T(8,128)(2,1)}, bf16[32,4096]{1,0:T(8,128)(2,1)S(1)}, u32[]{:S(2)}, u32[]{:S(2)}) %collective-permute-start.1) | collective-permute-done | bytes 262176 | tf_op jit(solution)/shard_map/ppermute | solution.py:218
  52.6 18.5 %all-to-all-start.1 = ((bf16[16,128,128]{2,1,0:T(8,128)(2,1)}), bf16[16,128,128]{2,1,0:T(8,128)(2,1)S(1)}, u32[]{:S(2)}, u32[]{:S(2)}) async-start(bf16[16,128,128]{2,1,0:T(8,128)(2,1)} %copy-done.7), calls=%async_computation.1 | async-start | bytes 1048576 | tf_op jit(solution)/shard_map/all_to_all | solution.py:228
  71.1 2.1 pad_maximum_fusion
  75.1 15.8 %all-to-all-done.1.refs_3_.xm_ref = bf16[16,128,128]{2,1,0:T(8,128)(2,1)S(1)} async-done(((bf16[16,128,128]{2,1,0:T(8,128)(2,1)}), bf16[16,128,128]{2,1,0:T(8,128)(2,1)S(1)}, u32[]{:S(2)}, u32[]{:S(2)}) %all-to-all-start.1) | async-done | bytes 524320 | tf_op jit(solution)/shard_map/all_to_all | solution.py:228
  96.0 3.5 %shard_map.141 = (bf16[128,128]{1,0:T(8,128)(2,1)S(1)}, bf16[128,128]{1,0:T(8,128)(2,1)S(1)}, bf16[256,128]{1,0:T(8,128)(2,1)}, bf16[128,256]{1,0:T(8,128)(2,1)S(1)}) custom-call(s32[4]{0:T(128)S(1)} %pad_add_fusion.ids_ref.refs_0_, s32[32,4]{1,0:T(8,128)S(1)} %copy.18.len_ref.refs_1_, s32[32,4]{1,0:T(8,128)S(1)} %copy.19.dest_ref.refs_2_, ...), custom_call_target="tpu_custom_call" | custom-call | tf_op jit(solution)/shard_map/pallas_call | solution.py:232
  99.5 2.6 %shard_map.142 = (bf16[8,2,128,128]{3,2,1,0:T(8,128)(2,1)S(1)}, bf16[8,2,128,128]{3,2,1,0:T(8,128)(2,1)}) custom-call(s32[4]{0:T(128)S(1)} %pad_add_fusion.ids_ref.refs_0_, bf16[4096,128]{1,0:T(8,128)(2,1)S(1)} %copy-done.1, bf16[256,4096]{1,0:T(8,128)(2,1)S(1)} %shard_map.138.refs_6_.wh_ref, bf16[128,128]{1,0:T(8,128)(2,1)S(1)} %get-tuple-element.18.gq_ref, ...), custom_call_target="tpu_custom_call" | custom-call | tf_op jit(solution)/shard_map/pallas_call | solution.py:241
  103.0 2.4 %collective-permute-start.5 = (bf16[8,2,128,128]{3,2,1,0:T(8,128)(2,1)}, bf16[8,2,128,128]{3,2,1,0:T(8,128)(2,1)}, u32[]{:S(2)}, u32[]{:S(2)}) collective-permute-start(bf16[8,2,128,128]{3,2,1,0:T(8,128)(2,1)} %get-tuple-element.21), channel_id=1, source_target_pairs={{0,1},{1,0},{2,3},{3,2},{4,5},{5,4},{6,7},{7,6},{8,9},{9,8},{10,11... | collective-permute-start | bytes 1572872 | tf_op jit(solution)/shard_map/ppermute | solution.py:244
  105.4 3.4 %all-to-all-start.3 = ((bf16[8,32,128]{2,1,0:T(8,128)(2,1)}), bf16[8,32,128]{2,1,0:T(8,128)(2,1)S(1)}, u32[]{:S(2)}, u32[]{:S(2)}) async-start(bf16[8,32,128]{2,1,0:T(8,128)(2,1)} %bitcast.11), calls=%async_computation.3 | async-start | bytes 131072 | tf_op jit(solution)/shard_map/all_to_all | solution.py:238
  115.3 6.8 %all-to-all-start.2 = ((bf16[8,2,128,128]{3,2,1,0:T(8,128)(2,1)}), bf16[8,2,128,128]{3,2,1,0:T(8,128)(2,1)}, u32[]{:S(2)}, u32[]{:S(2)}) async-start(bf16[8,2,128,128]{3,2,1,0:T(8,128)(2,1)} %copy-done.8), calls=%async_computation.2 | async-start | bytes 1048576 | tf_op jit(solution)/shard_map/all_to_all | solution.py:252
  124.0 4.8 %collective-permute-start.8 = (bf16[8,256,128]{2,1,0:T(8,128)(2,1)}, bf16[8,256,128]{2,1,0:T(8,128)(2,1)S(1)}, u32[]{:S(2)}, u32[]{:S(2)}) collective-permute-start(bf16[8,256,128]{2,1,0:T(8,128)(2,1)} %copy-done.20), channel_id=1, source_target_pairs={{0,512},{256,768},{512,0},{768,256},{1,513},{257,769},{513,1},{769... | collective-permute-start | bytes 1572872 | tf_op jit(solution)/shard_map/ppermute | solution.py:259
  131.6 5.1 %collective-permute-start.10 = (bf16[8,32,128]{2,1,0:T(8,128)(2,1)S(1)}, bf16[8,32,128]{2,1,0:T(8,128)(2,1)S(1)}, u32[]{:S(2)}, u32[]{:S(2)}) collective-permute-start(bf16[8,32,128]{2,1,0:T(8,128)(2,1)S(1)} %get-tuple-element.29), channel_id=1, source_target_pairs={{0,256},{256,512},{512,768},{768,0},{1,257},{257,513},{513,769},{7... | collective-permute-start | bytes 196616 | tf_op jit(solution)/shard_map/ppermute | solution.py:260
  138.8 12.5 %collective-permute-done.10.refs_5_ = bf16[8,32,128]{2,1,0:T(8,128)(2,1)S(1)} collective-permute-done((bf16[8,32,128]{2,1,0:T(8,128)(2,1)S(1)}, bf16[8,32,128]{2,1,0:T(8,128)(2,1)S(1)}, u32[]{:S(2)}, u32[]{:S(2)}) %collective-permute-start.10) | collective-permute-done | bytes 65568 | tf_op jit(solution)/shard_map/ppermute | solution.py:260
  151.3 2.6 %collective-permute-start.12 = (bf16[8,32,128]{2,1,0:T(8,128)(2,1)S(1)}, bf16[8,32,128]{2,1,0:T(8,128)(2,1)S(1)}, u32[]{:S(2)}, u32[]{:S(2)}) collective-permute-start(bf16[8,32,128]{2,1,0:T(8,128)(2,1)S(1)} %get-tuple-element.31), channel_id=1, source_target_pairs={{0,768},{256,0},{512,256},{768,512},{1,769},{257,1},{513,257},{769... | collective-permute-start | bytes 196616 | tf_op jit(solution)/shard_map/ppermute | solution.py:260
  154.3 4.4 %collective-permute-done.12.refs_7_ = bf16[8,32,128]{2,1,0:T(8,128)(2,1)S(1)} collective-permute-done((bf16[8,32,128]{2,1,0:T(8,128)(2,1)S(1)}, bf16[8,32,128]{2,1,0:T(8,128)(2,1)S(1)}, u32[]{:S(2)}, u32[]{:S(2)}) %collective-permute-start.12) | collective-permute-done | bytes 65568 | tf_op jit(solution)/shard_map/ppermute | solution.py:260
  159.8 16.2 %all-to-all-start.4 = ((bf16[4,576,128]{2,1,0:T(8,128)(2,1)}), bf16[4,576,128]{2,1,0:T(8,128)(2,1)S(1)}, u32[]{:S(2)}, u32[]{:S(2)}) async-start(bf16[4,576,128]{2,1,0:T(8,128)(2,1)} %bitcast.12), calls=%async_computation.4 | async-start | bytes 1179648 | tf_op jit(solution)/shard_map/all_to_all | solution.py:262
  177.2 2.5 %collective-permute-start.6 = (bf16[128,128]{1,0:T(8,128)(2,1)S(1)}, bf16[128,128]{1,0:T(8,128)(2,1)S(1)}, u32[]{:S(2)}, u32[]{:S(2)}) collective-permute-start(bf16[128,128]{1,0:T(8,128)(2,1)S(1)} %fusion.1), channel_id=1, source_target_pairs={{0,16},{16,0},{1,17},{17,1},{2,18},{18,2},{3,19},{19,3},{4,20},{20... | collective-permute-start | bytes 98312 | tf_op jit(solution)/shard_map/ppermute | solution.py:256
  179.7 11.0 %all-to-all-done.4 = bf16[4,576,128]{2,1,0:T(8,128)(2,1)S(1)} async-done(((bf16[4,576,128]{2,1,0:T(8,128)(2,1)}), bf16[4,576,128]{2,1,0:T(8,128)(2,1)S(1)}, u32[]{:S(2)}, u32[]{:S(2)}) %all-to-all-start.4) | async-done | bytes 589856 | tf_op jit(solution)/shard_map/all_to_all | solution.py:262
  190.8 12.6 %collective-permute-start.13 = (bf16[288,128]{1,0:T(8,128)(2,1)S(1)}, bf16[288,128]{1,0:T(8,128)(2,1)S(1)}, u32[]{:S(2)}, u32[]{:S(2)}) collective-permute-start(bf16[288,128]{1,0:T(8,128)(2,1)S(1)} %select_convert_fusion), channel_id=1, source_target_pairs={{0,128},{128,0},{1,129},{129,1},{2,130},{130,2},{3,131},{131,3},{4... | collective-permute-start | bytes 221192 | tf_op jit(solution)/shard_map/ppermute | solution.py:266
  204.1 2.3 %collective-permute-done.13 = bf16[288,128]{1,0:T(8,128)(2,1)S(1)} collective-permute-done((bf16[288,128]{1,0:T(8,128)(2,1)S(1)}, bf16[288,128]{1,0:T(8,128)(2,1)S(1)}, u32[]{:S(2)}, u32[]{:S(2)}) %collective-permute-start.13) | collective-permute-done | bytes 73760 | tf_op jit(solution)/shard_map/ppermute | solution.py:266
  (80 shorter events, 31.6 us)
Async XLA Ops:
  0.6 92.3 %copy-start = (bf16[128,4096]{1,0:T(8,128)(2,1)S(1)}, bf16[128,4096]{1,0:T(8,128)(2,1)}, u32[]{:S(2)}) copy-start(bf16[128,4096]{1,0:T(8,128)(2,1)} %param.15) | copy-start | bytes 3145732
  5.0 45.9 %all-to-all-start = ((bf16[32,32,128]{2,1,0:T(8,128)(2,1)}), bf16[32,32,128]{2,1,0:T(8,128)(2,1)S(1)}, u32[]{:S(2)}, u32[]{:S(2)}) async-start(bf16[32,32,128]{2,1,0:T(8,128)(2,1)} %shard_map.139), calls=%async_computation | async-start | bytes 524288 | tf_op jit(solution)/shard_map/all_to_all | solution.py:216
  23.8 69.1 %copy-start.2 = (bf16[128,4096]{1,0:T(8,128)(2,1)S(1)}, bf16[128,4096]{1,0:T(8,128)(2,1)}, u32[]{:S(2)}) copy-start(bf16[128,4096]{1,0:T(8,128)(2,1)} %go_ref.1) | copy-start | bytes 3145732
  23.8 12.9 %collective-permute-start = (bf16[32,4096]{1,0:T(8,128)(2,1)}, bf16[32,4096]{1,0:T(8,128)(2,1)S(1)}, u32[]{:S(2)}, u32[]{:S(2)}) collective-permute-start(bf16[32,4096]{1,0:T(8,128)(2,1)} %bitcast.25), channel_id=1, source_target_pairs={{0,2},{2,0},{4,6},{6,4},{1,3},{3,1},{5,7},{7,5},{8,10},{10,8},{12,... | collective-permute-start | bytes 786440 | tf_op jit(solution)/shard_map/ppermute | solution.py:218
  27.5 23.4 %collective-permute-start.1 = (bf16[32,4096]{1,0:T(8,128)(2,1)}, bf16[32,4096]{1,0:T(8,128)(2,1)S(1)}, u32[]{:S(2)}, u32[]{:S(2)}) collective-permute-start(bf16[32,4096]{1,0:T(8,128)(2,1)} %bitcast.26), channel_id=1, source_target_pairs={{0,4},{2,6},{4,0},{6,2},{1,5},{3,7},{5,1},{7,3},{8,12},{10,14},{12... | collective-permute-start | bytes 786440 | tf_op jit(solution)/shard_map/ppermute | solution.py:218
  32.0 18.9 %collective-permute-start.2 = (bf16[32,4096]{1,0:T(8,128)(2,1)}, bf16[32,4096]{1,0:T(8,128)(2,1)S(1)}, u32[]{:S(2)}, u32[]{:S(2)}) collective-permute-start(bf16[32,4096]{1,0:T(8,128)(2,1)} %bitcast.27), channel_id=1, source_target_pairs={{0,6},{2,4},{4,2},{6,0},{1,7},{3,5},{5,3},{7,1},{8,14},{10,12},{12... | collective-permute-start | bytes 786440 | tf_op jit(solution)/shard_map/ppermute | solution.py:218
  50.9 22.3 %copy-start.3 = (bf16[32,4096]{1,0:T(8,128)(2,1)}, bf16[32,4096]{1,0:T(8,128)(2,1)S(1)}, u32[]{:S(2)}) copy-start(bf16[32,4096]{1,0:T(8,128)(2,1)S(1)} %collective-permute-done.1.refs_2_.refs_1_) | copy-start | bytes 786436
  50.9 22.3 %copy-start.5 = (bf16[32,4096]{1,0:T(8,128)(2,1)}, bf16[32,4096]{1,0:T(8,128)(2,1)S(1)}, u32[]{:S(2)}) copy-start(bf16[32,4096]{1,0:T(8,128)(2,1)S(1)} %collective-permute-done.2.refs_3_.refs_2_) | copy-start | bytes 786436
  52.6 38.2 %all-to-all-start.1 = ((bf16[16,128,128]{2,1,0:T(8,128)(2,1)}), bf16[16,128,128]{2,1,0:T(8,128)(2,1)S(1)}, u32[]{:S(2)}, u32[]{:S(2)}) async-start(bf16[16,128,128]{2,1,0:T(8,128)(2,1)} %copy-done.7), calls=%async_computation.1 | async-start | bytes 1048576 | tf_op jit(solution)/shard_map/all_to_all | solution.py:228
  73.2 20.3 %collective-permute-start.3 = (bf16[4,32,4096]{2,1,0:T(8,128)(2,1)}, bf16[4,32,4096]{2,1,0:T(8,128)(2,1)}, u32[]{:S(2)}, u32[]{:S(2)}) collective-permute-start(bf16[4,32,4096]{2,1,0:T(8,128)(2,1)} %pad_maximum_fusion), channel_id=1, source_target_pairs={{0,1},{1,0},{2,3},{3,2},{4,5},{5,4},{6,7},{7,6},{8,9},{9,8},{10,11... | collective-permute-start | bytes 3145736 | tf_op jit(solution)/shard_map/ppermute | solution.py:219
  90.8 5.1 %collective-permute-start.4 = (bf16[16,128,128]{2,1,0:T(8,128)(2,1)S(1)}, bf16[16,128,128]{2,1,0:T(8,128)(2,1)S(1)}, u32[]{:S(2)}, u32[]{:S(2)}) collective-permute-start(bf16[16,128,128]{2,1,0:T(8,128)(2,1)S(1)} %all-to-all-done.1.refs_3_.xm_ref), channel_id=1, source_target_pairs={{0,1},{1,0},{2,3},{3,2},{4,5},{5,4},{6,7},{7,6},{8,9},{9,8},{10,11... | collective-permute-start | bytes 1572872 | tf_op jit(solution)/shard_map/ppermute | solution.py:229
  103.0 9.5 %collective-permute-start.5 = (bf16[8,2,128,128]{3,2,1,0:T(8,128)(2,1)}, bf16[8,2,128,128]{3,2,1,0:T(8,128)(2,1)}, u32[]{:S(2)}, u32[]{:S(2)}) collective-permute-start(bf16[8,2,128,128]{3,2,1,0:T(8,128)(2,1)} %get-tuple-element.21), channel_id=1, source_target_pairs={{0,1},{1,0},{2,3},{3,2},{4,5},{5,4},{6,7},{7,6},{8,9},{9,8},{10,11... | collective-permute-start | bytes 1572872 | tf_op jit(solution)/shard_map/ppermute | solution.py:244
  105.4 9.9 %all-to-all-start.3 = ((bf16[8,32,128]{2,1,0:T(8,128)(2,1)}), bf16[8,32,128]{2,1,0:T(8,128)(2,1)S(1)}, u32[]{:S(2)}, u32[]{:S(2)}) async-start(bf16[8,32,128]{2,1,0:T(8,128)(2,1)} %bitcast.11), calls=%async_computation.3 | async-start | bytes 131072 | tf_op jit(solution)/shard_map/all_to_all | solution.py:238
  115.3 43.4 %copy-start.10 = (bf16[8,256,128]{2,1,0:T(8,128)(2,1)S(1)}, bf16[8,256,128]{2,1,0:T(8,128)(2,1)}, u32[]{:S(2)}) copy-start(bf16[8,256,128]{2,1,0:T(8,128)(2,1)} %copy-done.9) | copy-start | bytes 1572868
  115.3 44.5 %all-to-all-start.2 = ((bf16[8,2,128,128]{3,2,1,0:T(8,128)(2,1)}), bf16[8,2,128,128]{3,2,1,0:T(8,128)(2,1)}, u32[]{:S(2)}, u32[]{:S(2)}) async-start(bf16[8,2,128,128]{3,2,1,0:T(8,128)(2,1)} %copy-done.8), calls=%async_computation.2 | async-start | bytes 1048576 | tf_op jit(solution)/shard_map/all_to_all | solution.py:252
  122.1 36.5 %collective-permute-start.7 = (bf16[8,256,128]{2,1,0:T(8,128)(2,1)}, bf16[8,256,128]{2,1,0:T(8,128)(2,1)S(1)}, u32[]{:S(2)}, u32[]{:S(2)}) collective-permute-start(bf16[8,256,128]{2,1,0:T(8,128)(2,1)} %copy-done.21), channel_id=1, source_target_pairs={{0,256},{256,512},{512,768},{768,0},{1,257},{257,513},{513,769},{7... | collective-permute-start | bytes 1572872 | tf_op jit(solution)/shard_map/ppermute | solution.py:259
  124.0 34.6 %collective-permute-start.8 = (bf16[8,256,128]{2,1,0:T(8,128)(2,1)}, bf16[8,256,128]{2,1,0:T(8,128)(2,1)S(1)}, u32[]{:S(2)}, u32[]{:S(2)}) collective-permute-start(bf16[8,256,128]{2,1,0:T(8,128)(2,1)} %copy-done.20), channel_id=1, source_target_pairs={{0,512},{256,768},{512,0},{768,256},{1,513},{257,769},{513,1},{769... | collective-permute-start | bytes 1572872 | tf_op jit(solution)/shard_map/ppermute | solution.py:259
  128.8 29.9 %collective-permute-start.9 = (bf16[8,256,128]{2,1,0:T(8,128)(2,1)}, bf16[8,256,128]{2,1,0:T(8,128)(2,1)S(1)}, u32[]{:S(2)}, u32[]{:S(2)}) collective-permute-start(bf16[8,256,128]{2,1,0:T(8,128)(2,1)} %copy-done.19), channel_id=1, source_target_pairs={{0,768},{256,0},{512,256},{768,512},{1,769},{257,1},{513,257},{769... | collective-permute-start | bytes 1572872 | tf_op jit(solution)/shard_map/ppermute | solution.py:259
  131.6 19.7 %collective-permute-start.10 = (bf16[8,32,128]{2,1,0:T(8,128)(2,1)S(1)}, bf16[8,32,128]{2,1,0:T(8,128)(2,1)S(1)}, u32[]{:S(2)}, u32[]{:S(2)}) collective-permute-start(bf16[8,32,128]{2,1,0:T(8,128)(2,1)S(1)} %get-tuple-element.29), channel_id=1, source_target_pairs={{0,256},{256,512},{512,768},{768,0},{1,257},{257,513},{513,769},{7... | collective-permute-start | bytes 196616 | tf_op jit(solution)/shard_map/ppermute | solution.py:260
  136.8 17.5 %collective-permute-start.11 = (bf16[8,32,128]{2,1,0:T(8,128)(2,1)S(1)}, bf16[8,32,128]{2,1,0:T(8,128)(2,1)S(1)}, u32[]{:S(2)}, u32[]{:S(2)}) collective-permute-start(bf16[8,32,128]{2,1,0:T(8,128)(2,1)S(1)} %get-tuple-element.30), channel_id=1, source_target_pairs={{0,512},{256,768},{512,0},{768,256},{1,513},{257,769},{513,1},{769... | collective-permute-start | bytes 196616 | tf_op jit(solution)/shard_map/ppermute | solution.py:260
  151.3 7.4 %collective-permute-start.12 = (bf16[8,32,128]{2,1,0:T(8,128)(2,1)S(1)}, bf16[8,32,128]{2,1,0:T(8,128)(2,1)S(1)}, u32[]{:S(2)}, u32[]{:S(2)}) collective-permute-start(bf16[8,32,128]{2,1,0:T(8,128)(2,1)S(1)} %get-tuple-element.31), channel_id=1, source_target_pairs={{0,768},{256,0},{512,256},{768,512},{1,769},{257,1},{513,257},{769... | collective-permute-start | bytes 196616 | tf_op jit(solution)/shard_map/ppermute | solution.py:260
  159.8 30.9 %all-to-all-start.4 = ((bf16[4,576,128]{2,1,0:T(8,128)(2,1)}), bf16[4,576,128]{2,1,0:T(8,128)(2,1)S(1)}, u32[]{:S(2)}, u32[]{:S(2)}) async-start(bf16[4,576,128]{2,1,0:T(8,128)(2,1)} %bitcast.12), calls=%async_computation.4 | async-start | bytes 1179648 | tf_op jit(solution)/shard_map/all_to_all | solution.py:262
  177.2 26.3 %collective-permute-start.6 = (bf16[128,128]{1,0:T(8,128)(2,1)S(1)}, bf16[128,128]{1,0:T(8,128)(2,1)S(1)}, u32[]{:S(2)}, u32[]{:S(2)}) collective-permute-start(bf16[128,128]{1,0:T(8,128)(2,1)S(1)} %fusion.1), channel_id=1, source_target_pairs={{0,16},{16,0},{1,17},{17,1},{2,18},{18,2},{3,19},{19,3},{4,20},{20... | collective-permute-start | bytes 98312 | tf_op jit(solution)/shard_map/ppermute | solution.py:256
  190.8 15.5 %collective-permute-start.13 = (bf16[288,128]{1,0:T(8,128)(2,1)S(1)}, bf16[288,128]{1,0:T(8,128)(2,1)S(1)}, u32[]{:S(2)}, u32[]{:S(2)}) collective-permute-start(bf16[288,128]{1,0:T(8,128)(2,1)S(1)} %select_convert_fusion), channel_id=1, source_target_pairs={{0,128},{128,0},{1,129},{129,1},{2,130},{130,2},{3,131},{131,3},{4... | collective-permute-start | bytes 221192 | tf_op jit(solution)/shard_map/ppermute | solution.py:266
  (17 other events, 24.9 us)

commit v3 on v2

--- a/solution.py
+++ b/solution.py
@@ -18,7 +18,7 @@
 F32 = jnp.float32
 BF16 = jnp.bfloat16
 SWAP = [(0, 1), (1, 0)]
-G, OX, OC, OYL = 0, 1, 2, 3
+G, OX, OC, OYL, OZH = 0, 1, 2, 3, 4
 
 
 def dot(left, right, dims):
@@ -70,26 +70,31 @@
 
 
 def incoming_kernel(ids_ref, dest_ref, x_ref, *refs):
-    out_ref = refs[-1]
+    own_ref, out_ref = refs[-2:]
     longest = x_ref.shape[1]
     senders, ranks = incoming(ids_ref, dest_ref)
     for sender, rank in zip(senders, ranks):
         rows = x_ref[sender]
+        own_ref[aligned(rank, longest), :] = rows
         for i in range(out_ref.shape[0]):
             out_ref[i, aligned(rank, longest), :] = rows
 
 
-def head_kernel(ids_ref, *refs):
+def stack_kernel(*refs):
     out_ref = refs[-1]
     for rel in range(4):
-        for flip in range(2):
+        out_ref[rel] = refs[rel][...]
+
+
+def head_kernel(ids_ref, here_ref, there_ref, out_ref):
+    for rel in range(4):
+        for flip, source in enumerate((here_ref, there_ref)):
             peer = (ids_ref[OYL] ^ rel) * 2 + (ids_ref[OC] ^ flip)
-            source = refs[rel] if flip == 0 else refs[4].at[rel]
-            out_ref[aligned(peer, 32), :] = source[...]
-
-
-def attention_kernel(longest, ids_ref, len_ref, dest_ref, xm_ref, xt_ref, wq_ref, wh_ref, ga_ref,
-                     cos_ref, sin_ref, cost_ref, sint_ref, o_ref, gq_ref, kvg_ref, gap_ref):
+            out_ref[aligned(peer, 32), :] = source[rel]
+
+
+def attention_kernel(longest, ids_ref, len_ref, dest_ref, x0_ref, x1_ref, x2_ref, x3_ref, wq_ref, wh_ref, ga_ref,
+                     cos_ref, sin_ref, cost_ref, sint_ref, o_ref, gq_ref, kvg_ref, gap_ref, x_ref):
     rows, hd = ga_ref.shape
     inv_scale = 1.0 / math.sqrt(hd)
 
@@ -101,11 +106,15 @@
 
     q = jnp.zeros((rows, hd), F32)
     kv = jnp.zeros((2 * hd, rows), F32)
-    for x_ref, c in ((xm_ref, ids_ref[OC]), (xt_ref, 1 - ids_ref[OC])):
-        for i in range(16):
-            cut = aligned(i * 2 + c, 128)
-            q = q + dot(x_ref[i], wq_ref[cut, :], ((1,), (0,)))
-            kv = kv + dot(wh_ref[:, cut], x_ref[i], ((1,), (1,)))
+    zh, c = ids_ref[OZH], ids_ref[OC]
+    for part_ref, z, core in ((x0_ref, zh, c), (x1_ref, 1 - zh, c), (x2_ref, zh, 1 - c), (x3_ref, 1 - zh, 1 - c)):
+        for y in range(8):
+            block = z * 16 + y * 2 + core
+            cut = aligned(block, 128)
+            xb = part_ref[y]
+            x_ref[block] = xb
+            q = q + dot(xb, wq_ref[cut, :], ((1,), (0,)))
+            kv = kv + dot(wh_ref[:, cut], xb, ((1,), (1,)))
     cosine, sine, cosine_t, sine_t = cos_ref[...], sin_ref[...], cost_ref[...], sint_ref[...]
     q = q.astype(BF16).astype(F32)
     q = (q * cosine + turn(q) * sine).astype(BF16)
@@ -160,36 +169,46 @@
     return ((yl & 1) * 2 + c) * 2 + (yl >> 1)
 
 
-def weight_kernel(ids_ref, xm_ref, xt_ref, go_ref, o_ref, gq_ref, *out_refs):
+def weight_kernel(ids_ref, x_ref, go_ref, o_ref, gq_ref, g0_ref, g1_ref, g3_ref, low_ref, high_ref):
     gq, out = gq_ref[...], o_ref[...]
-    for s in (1, 2, 3, 0):
+    for s, refs in ((2, (low_ref, high_ref)), (1, (g1_ref,)), (3, (g3_ref,)), (0, (g0_ref,))):
         x = (ids_ref[OX] + s) & 3
-        for x_ref, c in ((xm_ref, ids_ref[OC]), (xt_ref, 1 - ids_ref[OC])):
-            for yl in range(4):
-                row = row_of(yl, c)
-                out_refs[s][row, 0:128, :] = dot(x_ref[x * 4 + yl], gq, ((0,), (0,))).astype(BF16)
-                cut = aligned(x * 8 + yl * 2 + c, 128)
-                out_refs[s][row, 128:256, :] = dot(out, go_ref[:, cut], ((0,), (0,))).astype(BF16)
-
-
-def half_kernel(mine_ref, theirs_ref, after_ref, out_ref):
+        for yl in range(4):
+            for c in range(2):
+                row, block = row_of(yl, c), x * 8 + yl * 2 + c
+                ref = refs[row // 4 if s == 2 else 0]
+                row = row % 4 if s == 2 else row
+                ref[row, 0:128, :] = dot(x_ref[block], gq, ((0,), (0,))).astype(BF16)
+                ref[row, 128:256, :] = dot(out, go_ref[:, aligned(block, 128)], ((0,), (0,))).astype(BF16)
+
+
+def half_kernel(mine_ref, theirs_ref, low_ref, high_ref, out_ref):
     out_ref[...] = (mine_ref[...].astype(F32) + theirs_ref[...].astype(F32)).astype(BF16)
 
 
-def kv_kernel(ids_ref, xm_ref, xt_ref, kvt_ref, *out_refs):
+def kv_kernel(ids_ref, x_ref, kvt_ref, *out_refs):
     kvg = jnp.sum(kvt_ref[...].astype(F32), axis=0).astype(BF16)
-    for s in (1, 2, 3, 0):
+    for s in range(4):
         x = (ids_ref[OX] + s) & 3
-        for x_ref, c in ((xm_ref, ids_ref[OC]), (xt_ref, 1 - ids_ref[OC])):
-            for yl in range(4):
-                part = dot(kvg, x_ref[x * 4 + yl], ((1,), (0,)))
+        for yl in range(4):
+            for c in range(2):
+                part = dot(kvg, x_ref[x * 8 + yl * 2 + c], ((1,), (0,)))
                 out_refs[s][row_of(yl, c)] = part.astype(BF16)
 
 
-def sum_kernel(*refs):
-    out_ref = refs[-1]
-    out_ref[:, 0:256, :] = sum(ref[...].astype(F32) for ref in refs[:4]).astype(BF16)
-    out_ref[:, 256:288, :] = sum(ref[...].astype(F32) for ref in refs[4:8]).astype(BF16)
+def fold_kernel(g1_ref, g3_ref, low_ref, high_ref, k1_ref, k3_ref, h1_ref, h3_ref):
+    h1_ref[0:4, 0:256, :] = (g1_ref[0:4].astype(F32) + low_ref[...].astype(F32)).astype(BF16)
+    h1_ref[4:8, 0:256, :] = g1_ref[4:8]
+    h1_ref[:, 256:288, :] = k1_ref[...]
+    h3_ref[0:4, 0:256, :] = g3_ref[0:4]
+    h3_ref[4:8, 0:256, :] = (g3_ref[4:8].astype(F32) + high_ref[...].astype(F32)).astype(BF16)
+    h3_ref[:, 256:288, :] = k3_ref[...]
+
+
+def sum_kernel(g0_ref, k0_ref, k2_ref, h1_ref, h3_ref, out_ref):
+    both = h1_ref[...].astype(F32) + h3_ref[...].astype(F32)
+    out_ref[:, 0:256, :] = (g0_ref[...].astype(F32) + both[:, 0:256]).astype(BF16)
+    out_ref[:, 256:288, :] = (k0_ref[...].astype(F32) + k2_ref[...].astype(F32) + both[:, 256:288]).astype(BF16)
 
 
 def body(x_source, grad_out, w_query, w_kv, w_out, lengths, dest):
@@ -203,7 +222,7 @@
     shape = jax.ShapeDtypeStruct
     own_x, own_c, own_yl = lax.axis_index("x"), lax.axis_index("c"), lax.axis_index("yl")
     own_zh, own_zb = lax.axis_index("zh"), lax.axis_index("zb")
-    ids = jnp.stack([lax.axis_index(DP), own_x, own_c, own_yl]).astype(jnp.int32)
+    ids = jnp.stack([lax.axis_index(DP), own_x, own_c, own_yl, own_zh]).astype(jnp.int32)
 
     def call(kernel, ins, outs, out_shape, **extra):
         return pl.pallas_call(
@@ -216,25 +235,39 @@
     received = lax.all_to_all(outgoing, DP, 0, 0, tiled=True)
     w_own = w_kv.T
     w_parts = [w_own] + [lax.ppermute(w_own, "yl", [(i, i ^ s) for i in range(4)]) for s in (1, 2, 3)]
-    w_there = lax.ppermute(jnp.stack(w_parts), "c", SWAP)
-    w_head = call(head_kernel, [smem] + [vmem] * 5, vmem, shape((256, w_kv.shape[0]), BF16))(
-        ids, *w_parts, w_there
-    )
     grad_att = dot(grad_out, w_out, ((1,), (1,))).astype(BF16)
 
-    spread = call(incoming_kernel, [smem] * 2 + [vmem] + [anyw] * 3, vmem, shape((16, rows, 128), BF16))(
-        ids, dest, received, *w_parts[1:]
-    )
-    x_mine = lax.all_to_all(spread, ("zh",) + YY, 0, 0, tiled=True)
-    x_there = lax.ppermute(x_mine, "c", SWAP)
+    eighth = shape((8, rows, 128), BF16)
+    x_slice, spread = call(
+        incoming_kernel, [smem] * 2 + [vmem] + [anyw] * 2, (vmem,) * 2, (shape((rows, 128), BF16), eighth)
+    )(ids, dest, received, *w_parts[1:3])
+    x_other = lax.ppermute(x_slice, "zh", SWAP)
+    w_stack = call(stack_kernel, [vmem] * 4 + [anyw], vmem, shape((4,) + w_own.shape, BF16))(*w_parts, x_other)
+    w_there = lax.ppermute(w_stack, "c", SWAP)
+    w_head = call(head_kernel, [smem] + [vmem] * 2, vmem, shape((256, w_kv.shape[0]), BF16))(
+        ids, w_stack, w_there
+    )
+    x_own = lax.all_to_all(spread, YY, 0, 0, tiled=True)
+    x_own_there = lax.ppermute(x_own, "c", SWAP)
+    x_other = lax.all_to_all(jnp.broadcast_to(x_other[None], (8, rows, 128)), YY, 0, 0, tiled=True)
+    x_other_there = lax.ppermute(x_other, "c", SWAP)
 
     cosine, sine = tables(longest, seq_total, 128)
-    out, gq, kv_term, kv_turned = call(
+    out, gq, kv_term, kv_turned, x_all = call(
         lambda *refs: attention_kernel(longest, *refs),
-        [smem] * 3 + [vmem] * 9,
-        (vmem,) * 4,
-        (shape((rows, 128), BF16), shape((rows, 128), BF16), shape((256, rows), BF16), shape((rows, 256), BF16)),
-    )(ids, lengths, dest, x_mine, x_there, w_query, w_head, grad_att, cosine, sine, cosine.T.copy(), sine.T.copy())
+        [smem] * 3 + [vmem] * 11,
+        (vmem,) * 5,
+        (
+            shape((rows, 128), BF16),
+            shape((rows, 128), BF16),
+            shape((256, rows), BF16),
+            shape((rows, 256), BF16),
+            shape((32, rows, 128), BF16),
+        ),
+    )(
+        ids, lengths, dest, x_own, x_other, x_own_there, x_other_there, w_query, w_head, grad_att,
+        cosine, sine, cosine.T.copy(), sine.T.copy(),
+    )
     kv_terms = lax.all_to_all(kv_term.reshape(8, 32, rows), PEERS, 0, 0, tiled=True)
 
     half = shape((8, 2, rows, 128), BF16)
@@ -242,12 +275,16 @@
         ids, w_query, w_head, gq, kv_turned
     )
     theirs = lax.ppermute(other, "c", SWAP)
-    gw = call(weight_kernel, [smem] + [vmem] * 5, (vmem,) * 4, (shape((8, 256, 128), BF16),) * 4)(
-        ids, x_mine, x_there, grad_out, out, gq
-    )
-    part = call(half_kernel, [vmem] * 2 + [anyw], vmem, half)(mine, theirs, gw[0])
-    gkv = call(kv_kernel, [smem] + [vmem] * 3, (vmem,) * 4, (shape((8, 32, 128), BF16),) * 4)(
-        ids, x_mine, x_there, kv_terms
+    full, quad = shape((8, 256, 128), BF16), shape((4, 256, 128), BF16)
+    g0, g1, g3, low, high = call(
+        weight_kernel, [smem] + [vmem] * 4, (vmem,) * 5, (full, full, full, quad, quad)
+    )(ids, x_all, grad_out, out, gq)
+    around = [[(i, (i + s) % 4) for i in range(4)] for s in range(4)]
+    low = lax.ppermute(low, "x", around[1])
+    high = lax.ppermute(high, "x", around[3])
+    part = call(half_kernel, [vmem] * 2 + [anyw] * 2, vmem, half)(mine, theirs, low, high)
+    k0, k1, k2, k3 = call(kv_kernel, [smem] + [vmem] * 2, (vmem,) * 4, (shape((8, 32, 128), BF16),) * 4)(
+        ids, x_all, kv_terms
     )
     part = lax.all_to_all(part, YY, 0, 0, tiled=True)
     part = jnp.sum(part.astype(F32), axis=0)
@@ -255,10 +292,11 @@
     send = jnp.where(own_zh == 0, part[1], part[0]).astype(BF16)
     grad_input = (keep + lax.ppermute(send, "zh", SWAP).astype(F32)).astype(BF16)
 
-    around = [[(i, (i + s) % 4) for i in range(4)] for s in range(4)]
-    gw = [gw[0]] + [lax.ppermute(gw[s], "x", around[s]) for s in (1, 2, 3)]
-    gkv = [gkv[0]] + [lax.ppermute(gkv[s], "x", around[s]) for s in (1, 2, 3)]
-    total = call(sum_kernel, [vmem] * 8, vmem, shape((8, 288, 128), BF16))(*gw, *gkv)
+    most = shape((8, 288, 128), BF16)
+    h1, h3 = call(fold_kernel, [vmem] * 6, (vmem,) * 2, (most, most))(g1, g3, low, high, k1, k3)
+    h1, h3 = lax.ppermute(h1, "x", around[1]), lax.ppermute(h3, "x", around[3])
+    k2 = lax.ppermute(k2, "x", around[2])
+    total = call(sum_kernel, [vmem] * 5, vmem, most)(g0, k0, k2, h1, h3)
     total = lax.all_to_all(total.reshape(4, 576, 128), "za", 0, 0, tiled=True)
     total = jnp.sum(total.astype(F32), axis=0).reshape(2, 288, 128)
     keep = jnp.where(own_zb == 0, total[0], total[1])

time: 210 us -> 198 us (0.943)
  waiting for transfers between devices: 63 us -> 50 us
  local copies, waits for them, and re-layouts: 10.3 us -> 15.3 us
  starting transfers between devices: 114 us -> 110 us
  Pallas kernels: 14.9 us -> 17.2 us
  other arithmetic: 4.02 us -> 1.88 us
    all_to_all x1, starting transfers between devices: 16.2 us -> 4.49 us  [body(): total = lax.all_to_all(total.reshape(4, 576, 128), 'za', 0, 0, tiled=True)]
    ppermute x8 -> x9, starting transfers between devices: 22.3 us -> 32.6 us  [the longest x1 11.8 us: body(): x_other = lax.ppermute(x_slice, 'zh', SWAP)]
    all_to_all x1, waiting for transfers between devices: 11 us -> 1.04 us  [body(): total = lax.all_to_all(total.reshape(4, 576, 128), 'za', 0, 0, tiled=True)]
    ppermute x1, starting transfers between devices: 2.54 us -> 11.8 us  [body(): lax.ppermute(send, 'zh', SWAP).astype(F32)]
    all_to_all x1 -> x2, starting transfers between devices: 18.5 us -> 13 us  [the longest x1 7.21 us: body(): lax.all_to_all(jnp.broadcast_to(x_other[None], (8, rows, 128)), YY, 0, 0,...]
    all_to_all x1 -> x2, waiting for transfers between devices: 15.8 us -> 10.5 us  [the longest x1 10.5 us: body(): lax.all_to_all(jnp.broadcast_to(x_other[None], (8, rows, 128)), YY, 0, 0,...]
    unnamed x46 -> x48, local copies, waits for them, and re-layouts: 9.04 us -> 13.2 us
    ppermute x1, starting transfers between devices: 12.6 us -> 9.1 us  [body(): total = keep + lax.ppermute(send, 'zb', SWAP).astype(F32)]
  transfers between devices with their start and end apart: 19 -> 21, of which waited for: 8 -> 10; matrix products, arithmetic and copies ran while one was open for 2% -> 2% of each run, Pallas kernels for 3% -> 5%
where the time goes in v3:
time: 198 us; the launch traced here: 196 us
  starting transfers between devices  110 us (56%)
  waiting for transfers between devices  50 us (25%)
  Pallas kernels  17.2 us (9%)
  local copies, waits for them, and re-layouts  15.3 us (8%)
    all_to_all x1, starting transfers between devices, body(): received = lax.all_to_all(outgoing, DP, 0, 0, tiled=True)  18.8 us
    ppermute x3, waiting for transfers between devices, body(): lax.ppermute(w_own, 'yl', [(i, i ^ s) for i in range(4)])  16.7 us
    unnamed x48, local copies, waits for them, and re-layouts  13.2 us
    ppermute x1, starting transfers between devices, body(): x_other = lax.ppermute(x_slice, 'zh', SWAP)  11.8 us
    ppermute x1, starting transfers between devices, body(): lax.ppermute(send, 'zh', SWAP).astype(F32)  11.8 us
    ppermute x1, waiting for transfers between devices, body(): k2 = lax.ppermute(k2, 'x', around[2])  11.4 us
    all_to_all x1, waiting for transfers between devices, body(): lax.all_to_all(jnp.broadcast_to(x_other[None], (8, rows, 128)), YY, 0, 0,...  10.5 us
    ppermute x3, starting transfers between devices, body(): lax.ppermute(w_own, 'yl', [(i, i ^ s) for i in range(4)])  10.2 us
  transfers between devices with their start and end apart: 21, of which 10 were waited for; matrix products, arithmetic and copies ran while one was open for 2% of the time, Pallas kernels for 5%

profile of v3, /device:TPU:6, one launch (start us, length us, event | category | flops | bytes accessed | tf_op | source)
XLA Modules:
  0.0 196.1 jit_solution(12317893962911089328)
XLA Ops:
  5.0 18.8 %all-to-all-start = ((bf16[32,32,128]{2,1,0:T(8,128)(2,1)}), bf16[32,32,128]{2,1,0:T(8,128)(2,1)S(1)}, u32[]{:S(2)}, u32[]{:S(2)}) async-start(bf16[32,32,128]{2,1,0:T(8,128)(2,1)} %shard_map.138), calls=%async_computation | async-start | bytes 524288 | tf_op jit(solution)/shard_map/all_to_all | solution.py:235
  23.9 3.6 %collective-permute-start = (bf16[32,4096]{1,0:T(8,128)(2,1)}, bf16[32,4096]{1,0:T(8,128)(2,1)S(1)}, u32[]{:S(2)}, u32[]{:S(2)}) collective-permute-start(bf16[32,4096]{1,0:T(8,128)(2,1)} %bitcast.18), channel_id=1, source_target_pairs={{0,2},{2,0},{4,6},{6,4},{1,3},{3,1},{5,7},{7,5},{8,10},{10,8},{12,... | collective-permute-start | bytes 786440 | tf_op jit(solution)/shard_map/ppermute | solution.py:237
  27.5 4.5 %collective-permute-start.1 = (bf16[32,4096]{1,0:T(8,128)(2,1)}, bf16[32,4096]{1,0:T(8,128)(2,1)S(1)}, u32[]{:S(2)}, u32[]{:S(2)}) collective-permute-start(bf16[32,4096]{1,0:T(8,128)(2,1)} %bitcast.19), channel_id=1, source_target_pairs={{0,4},{2,6},{4,0},{6,2},{1,5},{3,7},{5,1},{7,3},{8,12},{10,14},{12... | collective-permute-start | bytes 786440 | tf_op jit(solution)/shard_map/ppermute | solution.py:237
  34.1 2.6 %collective-permute-done.refs_0_.refs_1_ = bf16[32,4096]{1,0:T(8,128)(2,1)S(1)} collective-permute-done((bf16[32,4096]{1,0:T(8,128)(2,1)}, bf16[32,4096]{1,0:T(8,128)(2,1)S(1)}, u32[]{:S(2)}, u32[]{:S(2)}) %collective-permute-start) | collective-permute-done | bytes 262176 | tf_op jit(solution)/shard_map/ppermute | solution.py:237
  36.8 14.1 %collective-permute-done.1.refs_1_.refs_2_ = bf16[32,4096]{1,0:T(8,128)(2,1)S(1)} collective-permute-done((bf16[32,4096]{1,0:T(8,128)(2,1)}, bf16[32,4096]{1,0:T(8,128)(2,1)S(1)}, u32[]{:S(2)}, u32[]{:S(2)}) %collective-permute-start.1) | collective-permute-done | bytes 262176 | tf_op jit(solution)/shard_map/ppermute | solution.py:237
  52.5 5.8 %all-to-all-start.1 = ((bf16[8,128,128]{2,1,0:T(8,128)(2,1)}), bf16[8,128,128]{2,1,0:T(8,128)(2,1)S(1)}, u32[]{:S(2)}, u32[]{:S(2)}) async-start(bf16[8,128,128]{2,1,0:T(8,128)(2,1)} %get-tuple-element.25), calls=%async_computation.1 | async-start | bytes 524288 | tf_op jit(solution)/shard_map/all_to_all | solution.py:250
  58.2 11.8 %collective-permute-start.3 = (bf16[128,128]{1,0:T(8,128)(2,1)S(1)}, bf16[128,128]{1,0:T(8,128)(2,1)S(1)}, u32[]{:S(2)}, u32[]{:S(2)}) collective-permute-start(bf16[128,128]{1,0:T(8,128)(2,1)S(1)} %get-tuple-element.24), channel_id=1, source_target_pairs={{0,16},{16,0},{1,17},{17,1},{2,18},{18,2},{3,19},{19,3},{4,20},{20... | collective-permute-start | bytes 98312 | tf_op jit(solution)/shard_map/ppermute | solution.py:244
  79.4 7.2 %all-to-all-start.2 = ((bf16[8,128,128]{2,1,0:T(8,128)(2,1)}), bf16[8,128,128]{2,1,0:T(8,128)(2,1)}, u32[]{:S(2)}, u32[]{:S(2)}) async-start(bf16[8,128,128]{2,1,0:T(8,128)(2,1)} %broadcast_in_dim.2), calls=%async_computation.2 | async-start | bytes 524288 | tf_op jit(solution)/shard_map/all_to_all | solution.py:252
  88.7 10.5 %all-to-all-done.2.refs_4_ = bf16[8,128,128]{2,1,0:T(8,128)(2,1)} async-done(((bf16[8,128,128]{2,1,0:T(8,128)(2,1)}), bf16[8,128,128]{2,1,0:T(8,128)(2,1)}, u32[]{:S(2)}, u32[]{:S(2)}) %all-to-all-start.2) | async-done | bytes 262176 | tf_op jit(solution)/shard_map/all_to_all | solution.py:252
  103.4 3.6 %shard_map.142 = (bf16[128,128]{1,0:T(8,128)(2,1)S(1)}, bf16[128,128]{1,0:T(8,128)(2,1)S(1)}, bf16[256,128]{1,0:T(8,128)(2,1)}, bf16[128,256]{1,0:T(8,128)(2,1)S(1)}, bf16[32,128,128]{2,1,0:T(8,128)(2,1)S(1)}) custom-call(s32[5]{0:T(128)S(1)} %stack.23.ids_ref.refs_0_, s32[32,4]{1,0:T(8,128)S(1)} %copy.15.len_ref.refs_1_, ...), custom_call_target="tpu_custom_call" | custom-call | tf_op jit(solution)/shard_map/pallas_call | solution.py:256
  106.9 2.7 %shard_map.143 = (bf16[8,2,128,128]{3,2,1,0:T(8,128)(2,1)S(1)}, bf16[8,2,128,128]{3,2,1,0:T(8,128)(2,1)}) custom-call(s32[5]{0:T(128)S(1)} %stack.23.ids_ref.refs_0_, bf16[4096,128]{1,0:T(8,128)(2,1)S(1)} %copy-done.1, bf16[256,4096]{1,0:T(8,128)(2,1)S(1)} %shard_map.141.refs_8_.wh_ref, bf16[128,128]{1,0:T(8,128)(2,1)S(1)} %get-tuple-element.26.gq_ref, ...), custom_call_target="tpu_custom_call" | custom-call | tf_op jit(solution)/shard_map/pallas_call | solution.py:274
  110.4 2.4 %collective-permute-start.7 = (bf16[8,2,128,128]{3,2,1,0:T(8,128)(2,1)}, bf16[8,2,128,128]{3,2,1,0:T(8,128)(2,1)}, u32[]{:S(2)}, u32[]{:S(2)}) collective-permute-start(bf16[8,2,128,128]{3,2,1,0:T(8,128)(2,1)} %get-tuple-element.29), channel_id=1, source_target_pairs={{0,1},{1,0},{2,3},{3,2},{4,5},{5,4},{6,7},{7,6},{8,9},{9,8},{10,11... | collective-permute-start | bytes 1572872 | tf_op jit(solution)/shard_map/ppermute | solution.py:277
  116.9 2.4 %collective-permute-start.8 = (bf16[4,256,128]{2,1,0:T(8,128)(2,1)}, bf16[4,256,128]{2,1,0:T(8,128)(2,1)S(1)}, u32[]{:S(2)}, u32[]{:S(2)}) collective-permute-start(bf16[4,256,128]{2,1,0:T(8,128)(2,1)} %get-tuple-element.32), channel_id=1, source_target_pairs={{0,256},{256,512},{512,768},{768,0},{1,257},{257,513},{513,769},{7... | collective-permute-start | bytes 786440 | tf_op jit(solution)/shard_map/ppermute | solution.py:283
  119.3 3.5 %collective-permute-start.9 = (bf16[4,256,128]{2,1,0:T(8,128)(2,1)S(1)}, bf16[4,256,128]{2,1,0:T(8,128)(2,1)S(1)}, u32[]{:S(2)}, u32[]{:S(2)}) collective-permute-start(bf16[4,256,128]{2,1,0:T(8,128)(2,1)S(1)} %get-tuple-element.33), channel_id=1, source_target_pairs={{0,768},{256,0},{512,256},{768,512},{1,769},{257,1},{513,257},{769... | collective-permute-start | bytes 786440 | tf_op jit(solution)/shard_map/ppermute | solution.py:284
  122.8 3.4 %all-to-all-start.4 = ((bf16[8,32,128]{2,1,0:T(8,128)(2,1)}), bf16[8,32,128]{2,1,0:T(8,128)(2,1)S(1)}, u32[]{:S(2)}, u32[]{:S(2)}) async-start(bf16[8,32,128]{2,1,0:T(8,128)(2,1)} %bitcast.8), calls=%async_computation.4 | async-start | bytes 131072 | tf_op jit(solution)/shard_map/all_to_all | solution.py:271
  127.3 3.1 %collective-permute-done.9.high_ref = bf16[4,256,128]{2,1,0:T(8,128)(2,1)S(1)} collective-permute-done((bf16[4,256,128]{2,1,0:T(8,128)(2,1)S(1)}, bf16[4,256,128]{2,1,0:T(8,128)(2,1)S(1)}, u32[]{:S(2)}, u32[]{:S(2)}) %collective-permute-start.9) | collective-permute-done | bytes 262176 | tf_op jit(solution)/shard_map/ppermute | solution.py:284
  133.4 4.3 %all-to-all-start.3 = ((bf16[8,2,128,128]{3,2,1,0:T(8,128)(2,1)}), bf16[8,2,128,128]{3,2,1,0:T(8,128)(2,1)}, u32[]{:S(2)}, u32[]{:S(2)}) async-start(bf16[8,2,128,128]{3,2,1,0:T(8,128)(2,1)} %shard_map.145), calls=%async_computation.3 | async-start | bytes 1048576 | tf_op jit(solution)/shard_map/all_to_all | solution.py:289
  143.1 3.6 %collective-permute-start.13 = (bf16[8,288,128]{2,1,0:T(8,128)(2,1)S(1)}, bf16[8,288,128]{2,1,0:T(8,128)(2,1)S(1)}, u32[]{:S(2)}, u32[]{:S(2)}) collective-permute-start(bf16[8,288,128]{2,1,0:T(8,128)(2,1)S(1)} %get-tuple-element.43), channel_id=1, source_target_pairs={{0,768},{256,0},{512,256},{768,512},{1,769},{257,1},{513,257},{769... | collective-permute-start | bytes 1769480 | tf_op jit(solution)/shard_map/ppermute | solution.py:297
  146.8 3.1 %collective-permute-start.11 = (bf16[8,32,128]{2,1,0:T(8,128)(2,1)S(1)}, bf16[8,32,128]{2,1,0:T(8,128)(2,1)S(1)}, u32[]{:S(2)}, u32[]{:S(2)}) collective-permute-start(bf16[8,32,128]{2,1,0:T(8,128)(2,1)S(1)} %get-tuple-element.37), channel_id=1, source_target_pairs={{0,512},{256,768},{512,0},{768,256},{1,513},{257,769},{513,1},{769... | collective-permute-start | bytes 196616 | tf_op jit(solution)/shard_map/ppermute | solution.py:298
  149.9 11.4 %collective-permute-done.11.k2_ref = bf16[8,32,128]{2,1,0:T(8,128)(2,1)S(1)} collective-permute-done((bf16[8,32,128]{2,1,0:T(8,128)(2,1)S(1)}, bf16[8,32,128]{2,1,0:T(8,128)(2,1)S(1)}, u32[]{:S(2)}, u32[]{:S(2)}) %collective-permute-start.11) | collective-permute-done | bytes 65568 | tf_op jit(solution)/shard_map/ppermute | solution.py:298
  163.1 4.5 %all-to-all-start.5 = ((bf16[4,576,128]{2,1,0:T(8,128)(2,1)}), bf16[4,576,128]{2,1,0:T(8,128)(2,1)S(1)}, u32[]{:S(2)}, u32[]{:S(2)}) async-start(bf16[4,576,128]{2,1,0:T(8,128)(2,1)} %bitcast.9), calls=%async_computation.5 | async-start | bytes 1179648 | tf_op jit(solution)/shard_map/all_to_all | solution.py:300
  168.8 11.8 %collective-permute-start.10 = (bf16[128,128]{1,0:T(8,128)(2,1)S(1)}, bf16[128,128]{1,0:T(8,128)(2,1)S(1)}, u32[]{:S(2)}, u32[]{:S(2)}) collective-permute-start(bf16[128,128]{1,0:T(8,128)(2,1)S(1)} %fusion.1), channel_id=1, source_target_pairs={{0,16},{16,0},{1,17},{17,1},{2,18},{18,2},{3,19},{19,3},{4,20},{20... | collective-permute-start | bytes 98312 | tf_op jit(solution)/shard_map/ppermute | solution.py:293
  181.7 9.1 %collective-permute-start.14 = (bf16[288,128]{1,0:T(8,128)(2,1)S(1)}, bf16[288,128]{1,0:T(8,128)(2,1)S(1)}, u32[]{:S(2)}, u32[]{:S(2)}) collective-permute-start(bf16[288,128]{1,0:T(8,128)(2,1)S(1)} %select_convert_fusion), channel_id=1, source_target_pairs={{0,128},{128,0},{1,129},{129,1},{2,130},{130,2},{3,131},{131,3},{4... | collective-permute-start | bytes 221192 | tf_op jit(solution)/shard_map/ppermute | solution.py:304
  191.5 3.3 %collective-permute-done.14 = bf16[288,128]{1,0:T(8,128)(2,1)S(1)} collective-permute-done((bf16[288,128]{1,0:T(8,128)(2,1)S(1)}, bf16[288,128]{1,0:T(8,128)(2,1)S(1)}, u32[]{:S(2)}, u32[]{:S(2)}) %collective-permute-start.14) | collective-permute-done | bytes 73760 | tf_op jit(solution)/shard_map/ppermute | solution.py:304
  (88 shorter events, 44.0 us)
Async XLA Ops:
  0.6 100.6 %copy-start = (bf16[128,4096]{1,0:T(8,128)(2,1)S(1)}, bf16[128,4096]{1,0:T(8,128)(2,1)}, u32[]{:S(2)}) copy-start(bf16[128,4096]{1,0:T(8,128)(2,1)} %param.15) | copy-start | bytes 3145732
  5.0 45.9 %all-to-all-start = ((bf16[32,32,128]{2,1,0:T(8,128)(2,1)}), bf16[32,32,128]{2,1,0:T(8,128)(2,1)S(1)}, u32[]{:S(2)}, u32[]{:S(2)}) async-start(bf16[32,32,128]{2,1,0:T(8,128)(2,1)} %shard_map.138), calls=%async_computation | async-start | bytes 524288 | tf_op jit(solution)/shard_map/all_to_all | solution.py:235
  23.9 77.3 %copy-start.2 = (bf16[128,4096]{1,0:T(8,128)(2,1)S(1)}, bf16[128,4096]{1,0:T(8,128)(2,1)}, u32[]{:S(2)}) copy-start(bf16[128,4096]{1,0:T(8,128)(2,1)} %go_ref.1) | copy-start | bytes 3145732
  23.9 12.9 %collective-permute-start = (bf16[32,4096]{1,0:T(8,128)(2,1)}, bf16[32,4096]{1,0:T(8,128)(2,1)S(1)}, u32[]{:S(2)}, u32[]{:S(2)}) collective-permute-start(bf16[32,4096]{1,0:T(8,128)(2,1)} %bitcast.18), channel_id=1, source_target_pairs={{0,2},{2,0},{4,6},{6,4},{1,3},{3,1},{5,7},{7,5},{8,10},{10,8},{12,... | collective-permute-start | bytes 786440 | tf_op jit(solution)/shard_map/ppermute | solution.py:237
  27.5 23.4 %collective-permute-start.1 = (bf16[32,4096]{1,0:T(8,128)(2,1)}, bf16[32,4096]{1,0:T(8,128)(2,1)S(1)}, u32[]{:S(2)}, u32[]{:S(2)}) collective-permute-start(bf16[32,4096]{1,0:T(8,128)(2,1)} %bitcast.19), channel_id=1, source_target_pairs={{0,4},{2,6},{4,0},{6,2},{1,5},{3,7},{5,1},{7,3},{8,12},{10,14},{12... | collective-permute-start | bytes 786440 | tf_op jit(solution)/shard_map/ppermute | solution.py:237
  32.0 38.1 %collective-permute-start.2 = (bf16[32,4096]{1,0:T(8,128)(2,1)}, bf16[32,4096]{1,0:T(8,128)(2,1)S(1)}, u32[]{:S(2)}, u32[]{:S(2)}) collective-permute-start(bf16[32,4096]{1,0:T(8,128)(2,1)} %bitcast.20), channel_id=1, source_target_pairs={{0,6},{2,4},{4,2},{6,0},{1,7},{3,5},{5,3},{7,1},{8,14},{10,12},{12... | collective-permute-start | bytes 786440 | tf_op jit(solution)/shard_map/ppermute | solution.py:237
  36.8 33.3 %copy-start.3 = (bf16[32,4096]{1,0:T(8,128)(2,1)}, bf16[32,4096]{1,0:T(8,128)(2,1)S(1)}, u32[]{:S(2)}) copy-start(bf16[32,4096]{1,0:T(8,128)(2,1)S(1)} %collective-permute-done.refs_0_.refs_1_) | copy-start | bytes 786436
  52.5 26.2 %all-to-all-start.1 = ((bf16[8,128,128]{2,1,0:T(8,128)(2,1)}), bf16[8,128,128]{2,1,0:T(8,128)(2,1)S(1)}, u32[]{:S(2)}, u32[]{:S(2)}) async-start(bf16[8,128,128]{2,1,0:T(8,128)(2,1)} %get-tuple-element.25), calls=%async_computation.1 | async-start | bytes 524288 | tf_op jit(solution)/shard_map/all_to_all | solution.py:250
  58.2 14.6 %collective-permute-start.3 = (bf16[128,128]{1,0:T(8,128)(2,1)S(1)}, bf16[128,128]{1,0:T(8,128)(2,1)S(1)}, u32[]{:S(2)}, u32[]{:S(2)}) collective-permute-start(bf16[128,128]{1,0:T(8,128)(2,1)S(1)} %get-tuple-element.24), channel_id=1, source_target_pairs={{0,16},{16,0},{1,17},{17,1},{2,18},{18,2},{3,19},{19,3},{4,20},{20... | collective-permute-start | bytes 98312 | tf_op jit(solution)/shard_map/ppermute | solution.py:244
  76.7 25.1 %collective-permute-start.4 = (bf16[4,32,4096]{2,1,0:T(8,128)(2,1)S(1)}, bf16[4,32,4096]{2,1,0:T(8,128)(2,1)}, u32[]{:S(2)}, u32[]{:S(2)}) collective-permute-start(bf16[4,32,4096]{2,1,0:T(8,128)(2,1)S(1)} %shard_map.140.here_ref), channel_id=1, source_target_pairs={{0,1},{1,0},{2,3},{3,2},{4,5},{5,4},{6,7},{7,6},{8,9},{9,8},{10,11... | collective-permute-start | bytes 3145736 | tf_op jit(solution)/shard_map/ppermute | solution.py:246
  79.4 19.9 %all-to-all-start.2 = ((bf16[8,128,128]{2,1,0:T(8,128)(2,1)}), bf16[8,128,128]{2,1,0:T(8,128)(2,1)}, u32[]{:S(2)}, u32[]{:S(2)}) async-start(bf16[8,128,128]{2,1,0:T(8,128)(2,1)} %broadcast_in_dim.2), calls=%async_computation.2 | async-start | bytes 524288 | tf_op jit(solution)/shard_map/all_to_all | solution.py:252
  86.6 16.7 %collective-permute-start.5 = (bf16[8,128,128]{2,1,0:T(8,128)(2,1)S(1)}, bf16[8,128,128]{2,1,0:T(8,128)(2,1)}, u32[]{:S(2)}, u32[]{:S(2)}) collective-permute-start(bf16[8,128,128]{2,1,0:T(8,128)(2,1)S(1)} %all-to-all-done.1.refs_3_), channel_id=1, source_target_pairs={{0,1},{1,0},{2,3},{3,2},{4,5},{5,4},{6,7},{7,6},{8,9},{9,8},{10,11... | collective-permute-start | bytes 786440 | tf_op jit(solution)/shard_map/ppermute | solution.py:251
  99.2 4.1 %collective-permute-start.6 = (bf16[8,128,128]{2,1,0:T(8,128)(2,1)}, bf16[8,128,128]{2,1,0:T(8,128)(2,1)S(1)}, u32[]{:S(2)}, u32[]{:S(2)}) collective-permute-start(bf16[8,128,128]{2,1,0:T(8,128)(2,1)} %all-to-all-done.2.refs_4_), channel_id=1, source_target_pairs={{0,1},{1,0},{2,3},{3,2},{4,5},{5,4},{6,7},{7,6},{8,9},{9,8},{10,11... | collective-permute-start | bytes 786440 | tf_op jit(solution)/shard_map/ppermute | solution.py:253
  110.4 20.0 %collective-permute-start.7 = (bf16[8,2,128,128]{3,2,1,0:T(8,128)(2,1)}, bf16[8,2,128,128]{3,2,1,0:T(8,128)(2,1)}, u32[]{:S(2)}, u32[]{:S(2)}) collective-permute-start(bf16[8,2,128,128]{3,2,1,0:T(8,128)(2,1)} %get-tuple-element.29), channel_id=1, source_target_pairs={{0,1},{1,0},{2,3},{3,2},{4,5},{5,4},{6,7},{7,6},{8,9},{9,8},{10,11... | collective-permute-start | bytes 1572872 | tf_op jit(solution)/shard_map/ppermute | solution.py:277
  116.9 10.3 %collective-permute-start.8 = (bf16[4,256,128]{2,1,0:T(8,128)(2,1)}, bf16[4,256,128]{2,1,0:T(8,128)(2,1)S(1)}, u32[]{:S(2)}, u32[]{:S(2)}) collective-permute-start(bf16[4,256,128]{2,1,0:T(8,128)(2,1)} %get-tuple-element.32), channel_id=1, source_target_pairs={{0,256},{256,512},{512,768},{768,0},{1,257},{257,513},{513,769},{7... | collective-permute-start | bytes 786440 | tf_op jit(solution)/shard_map/ppermute | solution.py:283
  119.3 11.1 %collective-permute-start.9 = (bf16[4,256,128]{2,1,0:T(8,128)(2,1)S(1)}, bf16[4,256,128]{2,1,0:T(8,128)(2,1)S(1)}, u32[]{:S(2)}, u32[]{:S(2)}) collective-permute-start(bf16[4,256,128]{2,1,0:T(8,128)(2,1)S(1)} %get-tuple-element.33), channel_id=1, source_target_pairs={{0,768},{256,0},{512,256},{768,512},{1,769},{257,1},{513,257},{769... | collective-permute-start | bytes 786440 | tf_op jit(solution)/shard_map/ppermute | solution.py:284
  122.8 10.6 %all-to-all-start.4 = ((bf16[8,32,128]{2,1,0:T(8,128)(2,1)}), bf16[8,32,128]{2,1,0:T(8,128)(2,1)S(1)}, u32[]{:S(2)}, u32[]{:S(2)}) async-start(bf16[8,32,128]{2,1,0:T(8,128)(2,1)} %bitcast.8), calls=%async_computation.4 | async-start | bytes 131072 | tf_op jit(solution)/shard_map/all_to_all | solution.py:271
  133.4 29.7 %all-to-all-start.3 = ((bf16[8,2,128,128]{3,2,1,0:T(8,128)(2,1)}), bf16[8,2,128,128]{3,2,1,0:T(8,128)(2,1)}, u32[]{:S(2)}, u32[]{:S(2)}) async-start(bf16[8,2,128,128]{3,2,1,0:T(8,128)(2,1)} %shard_map.145), calls=%async_computation.3 | async-start | bytes 1048576 | tf_op jit(solution)/shard_map/all_to_all | solution.py:289
  140.9 20.4 %collective-permute-start.12 = (bf16[8,288,128]{2,1,0:T(8,128)(2,1)S(1)}, bf16[8,288,128]{2,1,0:T(8,128)(2,1)S(1)}, u32[]{:S(2)}, u32[]{:S(2)}) collective-permute-start(bf16[8,288,128]{2,1,0:T(8,128)(2,1)S(1)} %get-tuple-element.42), channel_id=1, source_target_pairs={{0,256},{256,512},{512,768},{768,0},{1,257},{257,513},{513,769},{7... | collective-permute-start | bytes 1769480 | tf_op jit(solution)/shard_map/ppermute | solution.py:297
  143.1 19.0 %collective-permute-start.13 = (bf16[8,288,128]{2,1,0:T(8,128)(2,1)S(1)}, bf16[8,288,128]{2,1,0:T(8,128)(2,1)S(1)}, u32[]{:S(2)}, u32[]{:S(2)}) collective-permute-start(bf16[8,288,128]{2,1,0:T(8,128)(2,1)S(1)} %get-tuple-element.43), channel_id=1, source_target_pairs={{0,768},{256,0},{512,256},{768,512},{1,769},{257,1},{513,257},{769... | collective-permute-start | bytes 1769480 | tf_op jit(solution)/shard_map/ppermute | solution.py:297
  146.8 14.5 %collective-permute-start.11 = (bf16[8,32,128]{2,1,0:T(8,128)(2,1)S(1)}, bf16[8,32,128]{2,1,0:T(8,128)(2,1)S(1)}, u32[]{:S(2)}, u32[]{:S(2)}) collective-permute-start(bf16[8,32,128]{2,1,0:T(8,128)(2,1)S(1)} %get-tuple-element.37), channel_id=1, source_target_pairs={{0,512},{256,768},{512,0},{768,256},{1,513},{257,769},{513,1},{769... | collective-permute-start | bytes 196616 | tf_op jit(solution)/shard_map/ppermute | solution.py:298
  163.1 18.5 %all-to-all-start.5 = ((bf16[4,576,128]{2,1,0:T(8,128)(2,1)}), bf16[4,576,128]{2,1,0:T(8,128)(2,1)S(1)}, u32[]{:S(2)}, u32[]{:S(2)}) async-start(bf16[4,576,128]{2,1,0:T(8,128)(2,1)} %bitcast.9), calls=%async_computation.5 | async-start | bytes 1179648 | tf_op jit(solution)/shard_map/all_to_all | solution.py:300
  168.8 22.1 %collective-permute-start.10 = (bf16[128,128]{1,0:T(8,128)(2,1)S(1)}, bf16[128,128]{1,0:T(8,128)(2,1)S(1)}, u32[]{:S(2)}, u32[]{:S(2)}) collective-permute-start(bf16[128,128]{1,0:T(8,128)(2,1)S(1)} %fusion.1), channel_id=1, source_target_pairs={{0,16},{16,0},{1,17},{17,1},{2,18},{18,2},{3,19},{19,3},{4,20},{20... | collective-permute-start | bytes 98312 | tf_op jit(solution)/shard_map/ppermute | solution.py:293
  181.7 13.0 %collective-permute-start.14 = (bf16[288,128]{1,0:T(8,128)(2,1)S(1)}, bf16[288,128]{1,0:T(8,128)(2,1)S(1)}, u32[]{:S(2)}, u32[]{:S(2)}) collective-permute-start(bf16[288,128]{1,0:T(8,128)(2,1)S(1)} %select_convert_fusion), channel_id=1, source_target_pairs={{0,128},{128,0},{1,129},{129,1},{2,130},{130,2},{3,131},{131,3},{4... | collective-permute-start | bytes 221192 | tf_op jit(solution)/shard_map/ppermute | solution.py:304
  (20 other events, 67.3 us)

commit v4 on v3

--- a/solution.py
+++ b/solution.py
@@ -70,14 +70,19 @@
 
 
 def incoming_kernel(ids_ref, dest_ref, x_ref, *refs):
-    own_ref, out_ref = refs[-2:]
+    out_ref = refs[-1]
     longest = x_ref.shape[1]
     senders, ranks = incoming(ids_ref, dest_ref)
     for sender, rank in zip(senders, ranks):
-        rows = x_ref[sender]
-        own_ref[aligned(rank, longest), :] = rows
-        for i in range(out_ref.shape[0]):
-            out_ref[i, aligned(rank, longest), :] = rows
+        out_ref[aligned(rank, longest), :] = x_ref[sender]
+
+
+def spread_kernel(ids_ref, own_ref, other_ref, *refs):
+    out_ref = refs[-1]
+    zh = ids_ref[OZH]
+    for i in range(out_ref.shape[0]):
+        out_ref[i, zh] = own_ref[...]
+        out_ref[i, 1 - zh] = other_ref[...]
 
 
 def stack_kernel(*refs):
@@ -93,7 +98,7 @@
             out_ref[aligned(peer, 32), :] = source[rel]
 
 
-def attention_kernel(longest, ids_ref, len_ref, dest_ref, x0_ref, x1_ref, x2_ref, x3_ref, wq_ref, wh_ref, ga_ref,
+def attention_kernel(longest, ids_ref, len_ref, dest_ref, xm_ref, xt_ref, wq_ref, wh_ref, ga_ref,
                      cos_ref, sin_ref, cost_ref, sint_ref, o_ref, gq_ref, kvg_ref, gap_ref, x_ref):
     rows, hd = ga_ref.shape
     inv_scale = 1.0 / math.sqrt(hd)
@@ -106,15 +111,15 @@
 
     q = jnp.zeros((rows, hd), F32)
     kv = jnp.zeros((2 * hd, rows), F32)
-    zh, c = ids_ref[OZH], ids_ref[OC]
-    for part_ref, z, core in ((x0_ref, zh, c), (x1_ref, 1 - zh, c), (x2_ref, zh, 1 - c), (x3_ref, 1 - zh, 1 - c)):
+    for part_ref, core in ((xm_ref, ids_ref[OC]), (xt_ref, 1 - ids_ref[OC])):
         for y in range(8):
-            block = z * 16 + y * 2 + core
-            cut = aligned(block, 128)
-            xb = part_ref[y]
-            x_ref[block] = xb
-            q = q + dot(xb, wq_ref[cut, :], ((1,), (0,)))
-            kv = kv + dot(wh_ref[:, cut], xb, ((1,), (1,)))
+            for zh in range(2):
+                block = zh * 16 + y * 2 + core
+                cut = aligned(block, 128)
+                xb = part_ref[y, zh]
+                x_ref[block] = xb
+                q = q + dot(xb, wq_ref[cut, :], ((1,), (0,)))
+                kv = kv + dot(wh_ref[:, cut], xb, ((1,), (1,)))
     cosine, sine, cosine_t, sine_t = cos_ref[...], sin_ref[...], cost_ref[...], sint_ref[...]
     q = q.astype(BF16).astype(F32)
     q = (q * cosine + turn(q) * sine).astype(BF16)
@@ -169,8 +174,9 @@
     return ((yl & 1) * 2 + c) * 2 + (yl >> 1)
 
 
-def weight_kernel(ids_ref, x_ref, go_ref, o_ref, gq_ref, g0_ref, g1_ref, g3_ref, low_ref, high_ref):
+def weight_kernel(ids_ref, x_ref, go_ref, o_ref, gq_ref, kvt_ref, g0_ref, g1_ref, g3_ref, low_ref, high_ref):
     gq, out = gq_ref[...], o_ref[...]
+    kvg = jnp.sum(kvt_ref[...].astype(F32), axis=0).astype(BF16)
     for s, refs in ((2, (low_ref, high_ref)), (1, (g1_ref,)), (3, (g3_ref,)), (0, (g0_ref,))):
         x = (ids_ref[OX] + s) & 3
         for yl in range(4):
@@ -180,35 +186,22 @@
                 row = row % 4 if s == 2 else row
                 ref[row, 0:128, :] = dot(x_ref[block], gq, ((0,), (0,))).astype(BF16)
                 ref[row, 128:256, :] = dot(out, go_ref[:, aligned(block, 128)], ((0,), (0,))).astype(BF16)
-
-
-def half_kernel(mine_ref, theirs_ref, low_ref, high_ref, out_ref):
+                ref[row, 256:288, :] = dot(kvg, x_ref[block], ((1,), (0,))).astype(BF16)
+
+
+def half_kernel(mine_ref, theirs_ref, after_ref, out_ref):
     out_ref[...] = (mine_ref[...].astype(F32) + theirs_ref[...].astype(F32)).astype(BF16)
 
 
-def kv_kernel(ids_ref, x_ref, kvt_ref, *out_refs):
-    kvg = jnp.sum(kvt_ref[...].astype(F32), axis=0).astype(BF16)
-    for s in range(4):
-        x = (ids_ref[OX] + s) & 3
-        for yl in range(4):
-            for c in range(2):
-                part = dot(kvg, x_ref[x * 8 + yl * 2 + c], ((1,), (0,)))
-                out_refs[s][row_of(yl, c)] = part.astype(BF16)
-
-
-def fold_kernel(g1_ref, g3_ref, low_ref, high_ref, k1_ref, k3_ref, h1_ref, h3_ref):
-    h1_ref[0:4, 0:256, :] = (g1_ref[0:4].astype(F32) + low_ref[...].astype(F32)).astype(BF16)
-    h1_ref[4:8, 0:256, :] = g1_ref[4:8]
-    h1_ref[:, 256:288, :] = k1_ref[...]
-    h3_ref[0:4, 0:256, :] = g3_ref[0:4]
-    h3_ref[4:8, 0:256, :] = (g3_ref[4:8].astype(F32) + high_ref[...].astype(F32)).astype(BF16)
-    h3_ref[:, 256:288, :] = k3_ref[...]
-
-
-def sum_kernel(g0_ref, k0_ref, k2_ref, h1_ref, h3_ref, out_ref):
-    both = h1_ref[...].astype(F32) + h3_ref[...].astype(F32)
-    out_ref[:, 0:256, :] = (g0_ref[...].astype(F32) + both[:, 0:256]).astype(BF16)
-    out_ref[:, 256:288, :] = (k0_ref[...].astype(F32) + k2_ref[...].astype(F32) + both[:, 256:288]).astype(BF16)
+def fold_kernel(g1_ref, g3_ref, low_ref, high_ref, h1_ref, h3_ref):
+    h1_ref[0:4] = (g1_ref[0:4].astype(F32) + low_ref[...].astype(F32)).astype(BF16)
+    h1_ref[4:8] = g1_ref[4:8]
+    h3_ref[0:4] = g3_ref[0:4]
+    h3_ref[4:8] = (g3_ref[4:8].astype(F32) + high_ref[...].astype(F32)).astype(BF16)
+
+
+def sum_kernel(g0_ref, h1_ref, h3_ref, out_ref):
+    out_ref[...] = sum(ref[...].astype(F32) for ref in (g0_ref, h1_ref, h3_ref)).astype(BF16)
 
 
 def body(x_source, grad_out, w_query, w_kv, w_out, lengths, dest):
@@ -224,9 +217,10 @@
     own_zh, own_zb = lax.axis_index("zh"), lax.axis_index("zb")
     ids = jnp.stack([lax.axis_index(DP), own_x, own_c, own_yl, own_zh]).astype(jnp.int32)
 
-    def call(kernel, ins, outs, out_shape, **extra):
+    def call(kernel, ins, outs, out_shape, micros=1):
+        cost = pl.CostEstimate(flops=micros * 10**9, bytes_accessed=micros * 3_600_000, transcendentals=0)
         return pl.pallas_call(
-            kernel, out_shape=out_shape, in_specs=ins, out_specs=outs, compiler_params=params, **extra
+            kernel, out_shape=out_shape, in_specs=ins, out_specs=outs, compiler_params=params, cost_estimate=cost
         )
 
     outgoing = call(outgoing_kernel, [smem] * 3 + [vmem], vmem, shape((groups, longest, 128), BF16))(
@@ -234,28 +228,28 @@
     )
     received = lax.all_to_all(outgoing, DP, 0, 0, tiled=True)
     w_own = w_kv.T
-    w_parts = [w_own] + [lax.ppermute(w_own, "yl", [(i, i ^ s) for i in range(4)]) for s in (1, 2, 3)]
+    across = [[(i, i ^ s) for i in range(4)] for s in range(4)]
+    w_parts = [w_own] + [lax.ppermute(w_own, "yl", across[s]) for s in (1, 2, 3)]
     grad_att = dot(grad_out, w_out, ((1,), (1,))).astype(BF16)
 
-    eighth = shape((8, rows, 128), BF16)
-    x_slice, spread = call(
-        incoming_kernel, [smem] * 2 + [vmem] + [anyw] * 2, (vmem,) * 2, (shape((rows, 128), BF16), eighth)
-    )(ids, dest, received, *w_parts[1:3])
+    half = shape((8, 2, rows, 128), BF16)
+    x_slice = call(incoming_kernel, [smem] * 2 + [vmem, anyw], vmem, shape((rows, 128), BF16))(
+        ids, dest, received, w_parts[1]
+    )
     x_other = lax.ppermute(x_slice, "zh", SWAP)
-    w_stack = call(stack_kernel, [vmem] * 4 + [anyw], vmem, shape((4,) + w_own.shape, BF16))(*w_parts, x_other)
+    spread = call(spread_kernel, [smem] + [vmem] * 2 + [anyw] * 2, vmem, half)(ids, x_slice, x_other, *w_parts[2:])
+    x_mine = lax.all_to_all(spread, YY, 0, 0, tiled=True)
+    x_there = lax.ppermute(x_mine, "c", SWAP)
+    w_stack = call(stack_kernel, [vmem] * 4 + [anyw], vmem, shape((4,) + w_own.shape, BF16))(*w_parts, spread)
     w_there = lax.ppermute(w_stack, "c", SWAP)
     w_head = call(head_kernel, [smem] + [vmem] * 2, vmem, shape((256, w_kv.shape[0]), BF16))(
         ids, w_stack, w_there
     )
-    x_own = lax.all_to_all(spread, YY, 0, 0, tiled=True)
-    x_own_there = lax.ppermute(x_own, "c", SWAP)
-    x_other = lax.all_to_all(jnp.broadcast_to(x_other[None], (8, rows, 128)), YY, 0, 0, tiled=True)
-    x_other_there = lax.ppermute(x_other, "c", SWAP)
 
     cosine, sine = tables(longest, seq_total, 128)
     out, gq, kv_term, kv_turned, x_all = call(
         lambda *refs: attention_kernel(longest, *refs),
-        [smem] * 3 + [vmem] * 11,
+        [smem] * 3 + [vmem] * 9,
         (vmem,) * 5,
         (
             shape((rows, 128), BF16),
@@ -265,38 +259,33 @@
             shape((32, rows, 128), BF16),
         ),
     )(
-        ids, lengths, dest, x_own, x_other, x_own_there, x_other_there, w_query, w_head, grad_att,
+        ids, lengths, dest, x_mine, x_there, w_query, w_head, grad_att,
         cosine, sine, cosine.T.copy(), sine.T.copy(),
     )
     kv_terms = lax.all_to_all(kv_term.reshape(8, 32, rows), PEERS, 0, 0, tiled=True)
 
-    half = shape((8, 2, rows, 128), BF16)
-    mine, other = call(input_kernel, [smem] + [vmem] * 4, (vmem,) * 2, (half, half))(
+    mine, other = call(input_kernel, [smem] + [vmem] * 4, (vmem,) * 2, (half, half), 3)(
         ids, w_query, w_head, gq, kv_turned
     )
     theirs = lax.ppermute(other, "c", SWAP)
-    full, quad = shape((8, 256, 128), BF16), shape((4, 256, 128), BF16)
+    full, quad = shape((8, 288, 128), BF16), shape((4, 288, 128), BF16)
     g0, g1, g3, low, high = call(
-        weight_kernel, [smem] + [vmem] * 4, (vmem,) * 5, (full, full, full, quad, quad)
-    )(ids, x_all, grad_out, out, gq)
+        weight_kernel, [smem] + [vmem] * 5, (vmem,) * 5, (full, full, full, quad, quad)
+    )(ids, x_all, grad_out, out, gq, kv_terms)
     around = [[(i, (i + s) % 4) for i in range(4)] for s in range(4)]
     low = lax.ppermute(low, "x", around[1])
     high = lax.ppermute(high, "x", around[3])
-    part = call(half_kernel, [vmem] * 2 + [anyw] * 2, vmem, half)(mine, theirs, low, high)
-    k0, k1, k2, k3 = call(kv_kernel, [smem] + [vmem] * 2, (vmem,) * 4, (shape((8, 32, 128), BF16),) * 4)(
-        ids, x_all, kv_terms
-    )
+    h1, h3 = call(fold_kernel, [vmem] * 4, (vmem,) * 2, (full, full))(g1, g3, low, high)
+    h1, h3 = lax.ppermute(h1, "x", around[1]), lax.ppermute(h3, "x", around[3])
+    total = call(sum_kernel, [vmem] * 3, vmem, full)(g0, h1, h3)
+
+    part = call(half_kernel, [vmem] * 2 + [anyw], vmem, half)(mine, theirs, g0)
     part = lax.all_to_all(part, YY, 0, 0, tiled=True)
     part = jnp.sum(part.astype(F32), axis=0)
     keep = jnp.where(own_zh == 0, part[0], part[1])
     send = jnp.where(own_zh == 0, part[1], part[0]).astype(BF16)
     grad_input = (keep + lax.ppermute(send, "zh", SWAP).astype(F32)).astype(BF16)
 
-    most = shape((8, 288, 128), BF16)
-    h1, h3 = call(fold_kernel, [vmem] * 6, (vmem,) * 2, (most, most))(g1, g3, low, high, k1, k3)
-    h1, h3 = lax.ppermute(h1, "x", around[1]), lax.ppermute(h3, "x", around[3])
-    k2 = lax.ppermute(k2, "x", around[2])
-    total = call(sum_kernel, [vmem] * 5, vmem, most)(g0, k0, k2, h1, h3)
     total = lax.all_to_all(total.reshape(4, 576, 128), "za", 0, 0, tiled=True)
     total = jnp.sum(total.astype(F32), axis=0).reshape(2, 288, 128)
     keep = jnp.where(own_zb == 0, total[0], total[1])

time: 198 us -> 174 us (0.88)
  starting transfers between devices: 110 us -> 89.4 us
  blocking collectives: 0 us -> 8.3 us
  local copies, waits for them, and re-layouts: 15.3 us -> 7.4 us
  Pallas kernels: 17.2 us -> 14.3 us
    ppermute x6 -> x4, waiting for transfers between devices: 28.1 us -> 2.43 us  [the longest x3 2.43 us: body(): lax.ppermute(w_own, 'yl', across[s])]
    ppermute x1, waiting for transfers between devices: 0.01 us -> 9.73 us  [body(): lax.ppermute(h1, 'x', around[1])]
    all_to_all x3 -> x1, starting transfers between devices: 16.3 us -> 7.1 us  [body(): x_mine = lax.all_to_all(spread, YY, 0, 0, tiled=True)]
    all_to_all x0 -> x1, blocking collectives: none -> 8.3 us  [body(): lax.all_to_all(kv_term.reshape(8, 32, rows), PEERS, 0, 0, tiled=True)]
    unnamed x48 -> x32, local copies, waits for them, and re-layouts: 13.2 us -> 6.05 us
    ppermute x6 -> x4, starting transfers between devices: 17.4 us -> 12 us  [the longest x3 10.1 us: body(): lax.ppermute(w_own, 'yl', across[s])]
    ppermute x1, starting transfers between devices: 9.1 us -> 3.74 us  [body(): total = keep + lax.ppermute(send, 'zb', SWAP).astype(F32)]
    all_to_all x1, waiting for transfers between devices: 0.01 us -> 4.72 us  [body(): received = lax.all_to_all(outgoing, DP, 0, 0, tiled=True)]
  transfers between devices with their start and end apart: 21 -> 17, of which waited for: 10 -> 10; matrix products, arithmetic and copies ran while one was open for 2% -> 2% of each run, Pallas kernels for 5% -> 4%
where the time goes in v4:
time: 174 us; the launch traced here: 173 us
  starting transfers between devices  89.4 us (51%)
  waiting for transfers between devices  48.7 us (28%)
  Pallas kernels  14.3 us (8%)
  blocking collectives  8.3 us (5%)
  local copies, waits for them, and re-layouts  7.4 us (4%)
  other arithmetic  1.88 us (1%)
    all_to_all x1, starting transfers between devices, body(): received = lax.all_to_all(outgoing, DP, 0, 0, tiled=True)  18.8 us
    all_to_all x1, waiting for transfers between devices, body(): x_mine = lax.all_to_all(spread, YY, 0, 0, tiled=True)  12.4 us
    ppermute x1, starting transfers between devices, body(): lax.ppermute(send, 'zh', SWAP).astype(F32)  11.9 us
    ppermute x1, starting transfers between devices, body(): x_other = lax.ppermute(x_slice, 'zh', SWAP)  11.9 us
    ppermute x3, starting transfers between devices, body(): lax.ppermute(w_own, 'yl', across[s])  10.1 us
    ppermute x1, waiting for transfers between devices, body(): lax.ppermute(h1, 'x', around[1])  9.73 us
    all_to_all x1, blocking collectives, body(): lax.all_to_all(kv_term.reshape(8, 32, rows), PEERS, 0, 0, tiled=True)  8.3 us
    all_to_all x1, starting transfers between devices, body(): x_mine = lax.all_to_all(spread, YY, 0, 0, tiled=True)  7.1 us
  transfers between devices with their start and end apart: 17, of which 10 were waited for; matrix products, arithmetic and copies ran while one was open for 2% of the time, Pallas kernels for 4%

profile of v4, /device:TPU:6, one launch (start us, length us, event | category | flops | bytes accessed | tf_op | source)
XLA Modules:
  0.0 172.7 jit_solution(2565636482030405791)
XLA Ops:
  5.0 18.8 %all-to-all-start = ((bf16[32,32,128]{2,1,0:T(8,128)(2,1)}), bf16[32,32,128]{2,1,0:T(8,128)(2,1)S(1)}, u32[]{:S(2)}, u32[]{:S(2)}) async-start(bf16[32,32,128]{2,1,0:T(8,128)(2,1)} %shard_map.138), calls=%async_computation | async-start | bytes 524288 | tf_op jit(solution)/shard_map/all_to_all | solution.py:229
  23.8 3.5 %collective-permute-start = (bf16[32,4096]{1,0:T(8,128)(2,1)S(1)}, bf16[32,4096]{1,0:T(8,128)(2,1)S(1)}, u32[]{:S(2)}, u32[]{:S(2)}) collective-permute-start(bf16[32,4096]{1,0:T(8,128)(2,1)S(1)} %bitcast.19), channel_id=1, source_target_pairs={{0,2},{2,0},{4,6},{6,4},{1,3},{3,1},{5,7},{7,5},{8,10},{10,8},{12,... | collective-permute-start | bytes 786440 | tf_op jit(solution)/shard_map/ppermute | solution.py:232
  27.3 4.5 %collective-permute-start.1 = (bf16[32,4096]{1,0:T(8,128)(2,1)S(1)}, bf16[32,4096]{1,0:T(8,128)(2,1)S(1)}, u32[]{:S(2)}, u32[]{:S(2)}) collective-permute-start(bf16[32,4096]{1,0:T(8,128)(2,1)S(1)} %bitcast.20), channel_id=1, source_target_pairs={{0,4},{2,6},{4,0},{6,2},{1,5},{3,7},{5,1},{7,3},{8,12},{10,14},{12... | collective-permute-start | bytes 786440 | tf_op jit(solution)/shard_map/ppermute | solution.py:232
  31.8 2.1 %collective-permute-start.2 = (bf16[32,4096]{1,0:T(8,128)(2,1)S(1)}, bf16[32,4096]{1,0:T(8,128)(2,1)S(1)}, u32[]{:S(2)}, u32[]{:S(2)}) collective-permute-start(bf16[32,4096]{1,0:T(8,128)(2,1)S(1)} %bitcast.21), channel_id=1, source_target_pairs={{0,6},{2,4},{4,2},{6,0},{1,7},{3,5},{5,3},{7,1},{8,14},{10,12},{12... | collective-permute-start | bytes 786440 | tf_op jit(solution)/shard_map/ppermute | solution.py:232
  34.0 2.4 %collective-permute-done.refs_0_.refs_1_ = bf16[32,4096]{1,0:T(8,128)(2,1)S(1)} collective-permute-done((bf16[32,4096]{1,0:T(8,128)(2,1)S(1)}, bf16[32,4096]{1,0:T(8,128)(2,1)S(1)}, u32[]{:S(2)}, u32[]{:S(2)}) %collective-permute-start) | collective-permute-done | bytes 262176 | tf_op jit(solution)/shard_map/ppermute | solution.py:232
  36.4 4.7 %all-to-all-done.x_ref = bf16[32,32,128]{2,1,0:T(8,128)(2,1)S(1)} async-done(((bf16[32,32,128]{2,1,0:T(8,128)(2,1)}), bf16[32,32,128]{2,1,0:T(8,128)(2,1)S(1)}, u32[]{:S(2)}, u32[]{:S(2)}) %all-to-all-start) | async-done | bytes 262176 | tf_op jit(solution)/shard_map/all_to_all | solution.py:229
  42.0 11.9 %collective-permute-start.3 = (bf16[128,128]{1,0:T(8,128)(2,1)S(1)}, bf16[128,128]{1,0:T(8,128)(2,1)S(1)}, u32[]{:S(2)}, u32[]{:S(2)}) collective-permute-start(bf16[128,128]{1,0:T(8,128)(2,1)S(1)} %shard_map.139.own_ref), channel_id=1, source_target_pairs={{0,16},{16,0},{1,17},{17,1},{2,18},{18,2},{3,19},{19,3},{4,20},{20... | collective-permute-start | bytes 98312 | tf_op jit(solution)/shard_map/ppermute | solution.py:239
  53.9 2.6 %collective-permute-done.3.other_ref = bf16[128,128]{1,0:T(8,128)(2,1)S(1)} collective-permute-done((bf16[128,128]{1,0:T(8,128)(2,1)S(1)}, bf16[128,128]{1,0:T(8,128)(2,1)S(1)}, u32[]{:S(2)}, u32[]{:S(2)}) %collective-permute-start.3) | collective-permute-done | bytes 32800 | tf_op jit(solution)/shard_map/ppermute | solution.py:239
  57.9 7.1 %all-to-all-start.1 = ((bf16[8,2,128,128]{3,2,1,0:T(8,128)(2,1)}), bf16[8,2,128,128]{3,2,1,0:T(8,128)(2,1)S(1)}, u32[]{:S(2)}, u32[]{:S(2)}) async-start(bf16[8,2,128,128]{3,2,1,0:T(8,128)(2,1)} %shard_map.140.refs_4_), calls=%async_computation.1 | async-start | bytes 1048576 | tf_op jit(solution)/shard_map/all_to_all | solution.py:241
  67.9 12.4 %all-to-all-done.1.refs_3_ = bf16[8,2,128,128]{3,2,1,0:T(8,128)(2,1)S(1)} async-done(((bf16[8,2,128,128]{3,2,1,0:T(8,128)(2,1)}), bf16[8,2,128,128]{3,2,1,0:T(8,128)(2,1)S(1)}, u32[]{:S(2)}, u32[]{:S(2)}) %all-to-all-start.1) | async-done | bytes 524320 | tf_op jit(solution)/shard_map/all_to_all | solution.py:241
  85.5 3.0 %shard_map.143 = (bf16[128,128]{1,0:T(8,128)(2,1)S(1)}, bf16[128,128]{1,0:T(8,128)(2,1)S(1)}, bf16[256,128]{1,0:T(8,128)(2,1)S(1)}, bf16[128,256]{1,0:T(8,128)(2,1)S(1)}, bf16[32,128,128]{2,1,0:T(8,128)(2,1)S(1)}) custom-call(s32[5]{0:T(128)S(1)} %stack.23.ids_ref.refs_0_, s32[32,4]{1,0:T(8,128)S(1)} %copy.15.len_ref.refs_1_, ...), custom_call_target="tpu_custom_call" | custom-call | flops 1000000000 | bytes 3600000 | tf_op jit(solution)/shard_map/pallas_call | solution.py:250
  88.5 2.0 %shard_map.144 = (bf16[8,2,128,128]{3,2,1,0:T(8,128)(2,1)S(1)}, bf16[8,2,128,128]{3,2,1,0:T(8,128)(2,1)S(1)}) custom-call(s32[5]{0:T(128)S(1)} %stack.23.ids_ref.refs_0_, bf16[4096,128]{1,0:T(8,128)(2,1)S(1)} %copy-done.1, bf16[256,4096]{1,0:T(8,128)(2,1)S(1)} %shard_map.142.refs_6_.wh_ref, bf16[128,128]{1,0:T(8,128)(2,1)S(1)} %get-tuple-element.18.gq_ref, ...), custom_call_target="tpu_custom_call" | custom-call | flops 3000000000 | bytes 10800000 | tf_op jit(solution)/shard_map/pallas_call | solution.py:267
  90.5 2.4 %collective-permute-start.6 = (bf16[8,2,128,128]{3,2,1,0:T(8,128)(2,1)S(1)}, bf16[8,2,128,128]{3,2,1,0:T(8,128)(2,1)S(1)}, u32[]{:S(2)}, u32[]{:S(2)}) collective-permute-start(bf16[8,2,128,128]{3,2,1,0:T(8,128)(2,1)S(1)} %get-tuple-element.21), channel_id=1, source_target_pairs={{0,1},{1,0},{2,3},{3,2},{4,5},{5,4},{6,7},{7,6},{8,9},{9,8},{10,11... | collective-permute-start | bytes 1572872 | tf_op jit(solution)/shard_map/ppermute | solution.py:270
  92.9 8.3 %all_to_all.25.kvt_ref = bf16[8,32,128]{2,1,0:T(8,128)(2,1)S(1)} all-to-all(bf16[8,32,128]{2,1,0:T(8,128)(2,1)S(1)} %bitcast.18), channel_id=1, replica_groups=mesh['x'=4,'zb'=2,'za'=4,'zh'=2,'yh'=2,'yl'=4,'c'=2] {'yl','c'}, dimensions={0} | all-to-all | bytes 131072 | tf_op jit(solution)/shard_map/all_to_all | solution.py:265
  104.4 4.3 %collective-permute-start.8 = (bf16[4,288,128]{2,1,0:T(8,128)(2,1)S(1)}, bf16[4,288,128]{2,1,0:T(8,128)(2,1)S(1)}, u32[]{:S(2)}, u32[]{:S(2)}) collective-permute-start(bf16[4,288,128]{2,1,0:T(8,128)(2,1)S(1)} %get-tuple-element.28), channel_id=1, source_target_pairs={{0,256},{256,512},{512,768},{768,0},{1,257},{257,513},{513,769},{7... | collective-permute-start | bytes 884744 | tf_op jit(solution)/shard_map/ppermute | solution.py:276
  111.6 4.1 %all-to-all-start.3 = ((bf16[8,2,128,128]{3,2,1,0:T(8,128)(2,1)}), bf16[8,2,128,128]{3,2,1,0:T(8,128)(2,1)}, u32[]{:S(2)}, u32[]{:S(2)}) async-start(bf16[8,2,128,128]{3,2,1,0:T(8,128)(2,1)} %shard_map.146), calls=%async_computation.3 | async-start | bytes 1048576 | tf_op jit(solution)/shard_map/all_to_all | solution.py:283
  115.8 4.4 %collective-permute-done.9.high_ref = bf16[4,288,128]{2,1,0:T(8,128)(2,1)S(1)} collective-permute-done((bf16[4,288,128]{2,1,0:T(8,128)(2,1)S(1)}, bf16[4,288,128]{2,1,0:T(8,128)(2,1)S(1)}, u32[]{:S(2)}, u32[]{:S(2)}) %collective-permute-start.9) | collective-permute-done | bytes 294944 | tf_op jit(solution)/shard_map/ppermute | solution.py:277
  123.3 3.9 %collective-permute-start.11 = (bf16[8,288,128]{2,1,0:T(8,128)(2,1)S(1)}, bf16[8,288,128]{2,1,0:T(8,128)(2,1)S(1)}, u32[]{:S(2)}, u32[]{:S(2)}) collective-permute-start(bf16[8,288,128]{2,1,0:T(8,128)(2,1)S(1)} %get-tuple-element.31), channel_id=1, source_target_pairs={{0,768},{256,0},{512,256},{768,512},{1,769},{257,1},{513,257},{769... | collective-permute-start | bytes 1769480 | tf_op jit(solution)/shard_map/ppermute | solution.py:279
  127.2 9.7 %collective-permute-done.10.h1_ref = bf16[8,288,128]{2,1,0:T(8,128)(2,1)S(1)} collective-permute-done((bf16[8,288,128]{2,1,0:T(8,128)(2,1)S(1)}, bf16[8,288,128]{2,1,0:T(8,128)(2,1)S(1)}, u32[]{:S(2)}, u32[]{:S(2)}) %collective-permute-start.10) | collective-permute-done | bytes 589856 | tf_op jit(solution)/shard_map/ppermute | solution.py:279
  136.9 3.1 %collective-permute-done.11.h3_ref = bf16[8,288,128]{2,1,0:T(8,128)(2,1)S(1)} collective-permute-done((bf16[8,288,128]{2,1,0:T(8,128)(2,1)S(1)}, bf16[8,288,128]{2,1,0:T(8,128)(2,1)S(1)}, u32[]{:S(2)}, u32[]{:S(2)}) %collective-permute-start.11) | collective-permute-done | bytes 589856 | tf_op jit(solution)/shard_map/ppermute | solution.py:279
  141.1 3.5 %all-to-all-start.4 = ((bf16[4,576,128]{2,1,0:T(8,128)(2,1)}), bf16[4,576,128]{2,1,0:T(8,128)(2,1)S(1)}, u32[]{:S(2)}, u32[]{:S(2)}) async-start(bf16[4,576,128]{2,1,0:T(8,128)(2,1)} %bitcast.9), calls=%async_computation.4 | async-start | bytes 1179648 | tf_op jit(solution)/shard_map/all_to_all | solution.py:289
  145.8 11.9 %collective-permute-start.7 = (bf16[128,128]{1,0:T(8,128)(2,1)S(1)}, bf16[128,128]{1,0:T(8,128)(2,1)S(1)}, u32[]{:S(2)}, u32[]{:S(2)}) collective-permute-start(bf16[128,128]{1,0:T(8,128)(2,1)S(1)} %fusion.1), channel_id=1, source_target_pairs={{0,16},{16,0},{1,17},{17,1},{2,18},{18,2},{3,19},{19,3},{4,20},{20... | collective-permute-start | bytes 98312 | tf_op jit(solution)/shard_map/ppermute | solution.py:287
  158.9 3.7 %collective-permute-start.12 = (bf16[288,128]{1,0:T(8,128)(2,1)S(1)}, bf16[288,128]{1,0:T(8,128)(2,1)S(1)}, u32[]{:S(2)}, u32[]{:S(2)}) collective-permute-start(bf16[288,128]{1,0:T(8,128)(2,1)S(1)} %select_convert_fusion), channel_id=1, source_target_pairs={{0,128},{128,0},{1,129},{129,1},{2,130},{130,2},{3,131},{131,3},{4... | collective-permute-start | bytes 221192 | tf_op jit(solution)/shard_map/ppermute | solution.py:293
  164.8 6.7 %collective-permute-done.12 = bf16[288,128]{1,0:T(8,128)(2,1)S(1)} collective-permute-done((bf16[288,128]{1,0:T(8,128)(2,1)S(1)}, bf16[288,128]{1,0:T(8,128)(2,1)S(1)}, u32[]{:S(2)}, u32[]{:S(2)}) %collective-permute-start.12) | collective-permute-done | bytes 73760 | tf_op jit(solution)/shard_map/ppermute | solution.py:293
  (64 shorter events, 30.7 us)
Async XLA Ops:
  0.6 81.6 %copy-start = (bf16[128,4096]{1,0:T(8,128)(2,1)S(1)}, bf16[128,4096]{1,0:T(8,128)(2,1)}, u32[]{:S(2)}) copy-start(bf16[128,4096]{1,0:T(8,128)(2,1)} %param.15) | copy-start | bytes 3145732
  3.1 20.8 %copy-start.7 = (bf16[4096,32]{0,1:T(8,128)(2,1)S(1)}, bf16[4096,32]{0,1:T(8,128)(2,1)}, u32[]{:S(2)}) copy-start(bf16[4096,32]{0,1:T(8,128)(2,1)} %param.14) | copy-start | bytes 786436
  5.0 36.1 %all-to-all-start = ((bf16[32,32,128]{2,1,0:T(8,128)(2,1)}), bf16[32,32,128]{2,1,0:T(8,128)(2,1)S(1)}, u32[]{:S(2)}, u32[]{:S(2)}) async-start(bf16[32,32,128]{2,1,0:T(8,128)(2,1)} %shard_map.138), calls=%async_computation | async-start | bytes 524288 | tf_op jit(solution)/shard_map/all_to_all | solution.py:229
  23.8 12.6 %collective-permute-start = (bf16[32,4096]{1,0:T(8,128)(2,1)S(1)}, bf16[32,4096]{1,0:T(8,128)(2,1)S(1)}, u32[]{:S(2)}, u32[]{:S(2)}) collective-permute-start(bf16[32,4096]{1,0:T(8,128)(2,1)S(1)} %bitcast.19), channel_id=1, source_target_pairs={{0,2},{2,0},{4,6},{6,4},{1,3},{3,1},{5,7},{7,5},{8,10},{10,8},{12,... | collective-permute-start | bytes 786440 | tf_op jit(solution)/shard_map/ppermute | solution.py:232
  27.3 26.5 %collective-permute-start.1 = (bf16[32,4096]{1,0:T(8,128)(2,1)S(1)}, bf16[32,4096]{1,0:T(8,128)(2,1)S(1)}, u32[]{:S(2)}, u32[]{:S(2)}) collective-permute-start(bf16[32,4096]{1,0:T(8,128)(2,1)S(1)} %bitcast.20), channel_id=1, source_target_pairs={{0,4},{2,6},{4,0},{6,2},{1,5},{3,7},{5,1},{7,3},{8,12},{10,14},{12... | collective-permute-start | bytes 786440 | tf_op jit(solution)/shard_map/ppermute | solution.py:232
  31.8 22.0 %collective-permute-start.2 = (bf16[32,4096]{1,0:T(8,128)(2,1)S(1)}, bf16[32,4096]{1,0:T(8,128)(2,1)S(1)}, u32[]{:S(2)}, u32[]{:S(2)}) collective-permute-start(bf16[32,4096]{1,0:T(8,128)(2,1)S(1)} %bitcast.21), channel_id=1, source_target_pairs={{0,6},{2,4},{4,2},{6,0},{1,7},{3,5},{5,3},{7,1},{8,14},{10,12},{12... | collective-permute-start | bytes 786440 | tf_op jit(solution)/shard_map/ppermute | solution.py:232
  42.0 14.5 %collective-permute-start.3 = (bf16[128,128]{1,0:T(8,128)(2,1)S(1)}, bf16[128,128]{1,0:T(8,128)(2,1)S(1)}, u32[]{:S(2)}, u32[]{:S(2)}) collective-permute-start(bf16[128,128]{1,0:T(8,128)(2,1)S(1)} %shard_map.139.own_ref), channel_id=1, source_target_pairs={{0,16},{16,0},{1,17},{17,1},{2,18},{18,2},{3,19},{19,3},{4,20},{20... | collective-permute-start | bytes 98312 | tf_op jit(solution)/shard_map/ppermute | solution.py:239
  53.8 4.0 %copy-start.8 = (bf16[32,4096]{1,0:T(8,128)(2,1)}, bf16[32,4096]{1,0:T(8,128)(2,1)S(1)}, u32[]{:S(2)}) copy-start(bf16[32,4096]{1,0:T(8,128)(2,1)S(1)} %collective-permute-done.2.refs_1_.refs_3_) | copy-start | bytes 786436
  57.9 22.4 %all-to-all-start.1 = ((bf16[8,2,128,128]{3,2,1,0:T(8,128)(2,1)}), bf16[8,2,128,128]{3,2,1,0:T(8,128)(2,1)S(1)}, u32[]{:S(2)}, u32[]{:S(2)}) async-start(bf16[8,2,128,128]{3,2,1,0:T(8,128)(2,1)} %shard_map.140.refs_4_), calls=%async_computation.1 | async-start | bytes 1048576 | tf_op jit(solution)/shard_map/all_to_all | solution.py:241
  66.0 17.9 %collective-permute-start.4 = (bf16[4,32,4096]{2,1,0:T(8,128)(2,1)S(1)}, bf16[4,32,4096]{2,1,0:T(8,128)(2,1)}, u32[]{:S(2)}, u32[]{:S(2)}) collective-permute-start(bf16[4,32,4096]{2,1,0:T(8,128)(2,1)S(1)} %shard_map.141.here_ref), channel_id=1, source_target_pairs={{0,1},{1,0},{2,3},{3,2},{4,5},{5,4},{6,7},{7,6},{8,9},{9,8},{10,11... | collective-permute-start | bytes 3145736 | tf_op jit(solution)/shard_map/ppermute | solution.py:244
  80.3 5.1 %collective-permute-start.5 = (bf16[8,2,128,128]{3,2,1,0:T(8,128)(2,1)S(1)}, bf16[8,2,128,128]{3,2,1,0:T(8,128)(2,1)S(1)}, u32[]{:S(2)}, u32[]{:S(2)}) collective-permute-start(bf16[8,2,128,128]{3,2,1,0:T(8,128)(2,1)S(1)} %all-to-all-done.1.refs_3_), channel_id=1, source_target_pairs={{0,1},{1,0},{2,3},{3,2},{4,5},{5,4},{6,7},{7,6},{8,9},{9,8},{10,11... | collective-permute-start | bytes 1572872 | tf_op jit(solution)/shard_map/ppermute | solution.py:242
  83.9 1.6 copy-start.1
  83.9 1.6 copy-start.3
  88.5 12.7 %copy-start.2 = (bf16[128,4096]{1,0:T(8,128)(2,1)S(1)}, bf16[128,4096]{1,0:T(8,128)(2,1)}, u32[]{:S(2)}) copy-start(bf16[128,4096]{1,0:T(8,128)(2,1)} %go_ref.1) | copy-start | bytes 3145732
  90.5 20.2 %collective-permute-start.6 = (bf16[8,2,128,128]{3,2,1,0:T(8,128)(2,1)S(1)}, bf16[8,2,128,128]{3,2,1,0:T(8,128)(2,1)S(1)}, u32[]{:S(2)}, u32[]{:S(2)}) collective-permute-start(bf16[8,2,128,128]{3,2,1,0:T(8,128)(2,1)S(1)} %get-tuple-element.21), channel_id=1, source_target_pairs={{0,1},{1,0},{2,3},{3,2},{4,5},{5,4},{6,7},{7,6},{8,9},{9,8},{10,11... | collective-permute-start | bytes 1572872 | tf_op jit(solution)/shard_map/ppermute | solution.py:270
  104.4 11.3 %collective-permute-start.8 = (bf16[4,288,128]{2,1,0:T(8,128)(2,1)S(1)}, bf16[4,288,128]{2,1,0:T(8,128)(2,1)S(1)}, u32[]{:S(2)}, u32[]{:S(2)}) collective-permute-start(bf16[4,288,128]{2,1,0:T(8,128)(2,1)S(1)} %get-tuple-element.28), channel_id=1, source_target_pairs={{0,256},{256,512},{512,768},{768,0},{1,257},{257,513},{513,769},{7... | collective-permute-start | bytes 884744 | tf_op jit(solution)/shard_map/ppermute | solution.py:276
  108.7 11.4 %collective-permute-start.9 = (bf16[4,288,128]{2,1,0:T(8,128)(2,1)S(1)}, bf16[4,288,128]{2,1,0:T(8,128)(2,1)S(1)}, u32[]{:S(2)}, u32[]{:S(2)}) collective-permute-start(bf16[4,288,128]{2,1,0:T(8,128)(2,1)S(1)} %get-tuple-element.29), channel_id=1, source_target_pairs={{0,768},{256,0},{512,256},{768,512},{1,769},{257,1},{513,257},{769... | collective-permute-start | bytes 884744 | tf_op jit(solution)/shard_map/ppermute | solution.py:277
  110.7 9.5 %copy-start.12 = (bf16[8,288,128]{2,1,0:T(8,128)(2,1)S(1)}, bf16[8,288,128]{2,1,0:T(8,128)(2,1)}, u32[]{:S(2)}) copy-start(bf16[8,288,128]{2,1,0:T(8,128)(2,1)} %copy-done.11) | copy-start | bytes 1769476
  111.6 29.5 %all-to-all-start.3 = ((bf16[8,2,128,128]{3,2,1,0:T(8,128)(2,1)}), bf16[8,2,128,128]{3,2,1,0:T(8,128)(2,1)}, u32[]{:S(2)}, u32[]{:S(2)}) async-start(bf16[8,2,128,128]{3,2,1,0:T(8,128)(2,1)} %shard_map.146), calls=%async_computation.3 | async-start | bytes 1048576 | tf_op jit(solution)/shard_map/all_to_all | solution.py:283
  121.4 15.6 %collective-permute-start.10 = (bf16[8,288,128]{2,1,0:T(8,128)(2,1)S(1)}, bf16[8,288,128]{2,1,0:T(8,128)(2,1)S(1)}, u32[]{:S(2)}, u32[]{:S(2)}) collective-permute-start(bf16[8,288,128]{2,1,0:T(8,128)(2,1)S(1)} %get-tuple-element.30), channel_id=1, source_target_pairs={{0,256},{256,512},{512,768},{768,0},{1,257},{257,513},{513,769},{7... | collective-permute-start | bytes 1769480 | tf_op jit(solution)/shard_map/ppermute | solution.py:279
  123.3 16.8 %collective-permute-start.11 = (bf16[8,288,128]{2,1,0:T(8,128)(2,1)S(1)}, bf16[8,288,128]{2,1,0:T(8,128)(2,1)S(1)}, u32[]{:S(2)}, u32[]{:S(2)}) collective-permute-start(bf16[8,288,128]{2,1,0:T(8,128)(2,1)S(1)} %get-tuple-element.31), channel_id=1, source_target_pairs={{0,768},{256,0},{512,256},{768,512},{1,769},{257,1},{513,257},{769... | collective-permute-start | bytes 1769480 | tf_op jit(solution)/shard_map/ppermute | solution.py:279
  141.1 17.7 %all-to-all-start.4 = ((bf16[4,576,128]{2,1,0:T(8,128)(2,1)}), bf16[4,576,128]{2,1,0:T(8,128)(2,1)S(1)}, u32[]{:S(2)}, u32[]{:S(2)}) async-start(bf16[4,576,128]{2,1,0:T(8,128)(2,1)} %bitcast.9), calls=%async_computation.4 | async-start | bytes 1179648 | tf_op jit(solution)/shard_map/all_to_all | solution.py:289
  145.8 18.4 %collective-permute-start.7 = (bf16[128,128]{1,0:T(8,128)(2,1)S(1)}, bf16[128,128]{1,0:T(8,128)(2,1)S(1)}, u32[]{:S(2)}, u32[]{:S(2)}) collective-permute-start(bf16[128,128]{1,0:T(8,128)(2,1)S(1)} %fusion.1), channel_id=1, source_target_pairs={{0,16},{16,0},{1,17},{17,1},{2,18},{18,2},{3,19},{19,3},{4,20},{20... | collective-permute-start | bytes 98312 | tf_op jit(solution)/shard_map/ppermute | solution.py:287
  158.9 12.5 %collective-permute-start.12 = (bf16[288,128]{1,0:T(8,128)(2,1)S(1)}, bf16[288,128]{1,0:T(8,128)(2,1)S(1)}, u32[]{:S(2)}, u32[]{:S(2)}) collective-permute-start(bf16[288,128]{1,0:T(8,128)(2,1)S(1)} %select_convert_fusion), channel_id=1, source_target_pairs={{0,128},{128,0},{1,129},{129,1},{2,130},{130,2},{3,131},{131,3},{4... | collective-permute-start | bytes 221192 | tf_op jit(solution)/shard_map/ppermute | solution.py:293
  (8 other events, 9.1 us)

commit v5 on v4

--- a/solution.py
+++ b/solution.py
@@ -18,7 +18,7 @@
 F32 = jnp.float32
 BF16 = jnp.bfloat16
 SWAP = [(0, 1), (1, 0)]
-G, OX, OC, OYL, OZH = 0, 1, 2, 3, 4
+G, OX, OC, OYL, OZH, OYH, OZB = 0, 1, 2, 3, 4, 5, 6
 
 
 def dot(left, right, dims):
@@ -160,23 +160,24 @@
     gap_ref[:, hd:] = gv.astype(F32).T.astype(BF16)
 
 
-def input_kernel(ids_ref, wq_ref, wh_ref, gq_ref, kvt_ref, mine_ref, other_ref):
+def input_kernel(ids_ref, wq_ref, wh_ref, gq_ref, kvt_ref, term_ref, mine_ref, other_ref):
     gq, kvt = gq_ref[...], kvt_ref[...]
     for out_ref, c in ((other_ref, 1 - ids_ref[OC]), (mine_ref, ids_ref[OC])):
         for y in range(8):
             for zh in range(2):
                 cut = aligned(zh * 16 + y * 2 + c, 128)
                 part = dot(gq, wq_ref[cut, :], ((1,), (1,))) + dot(kvt, wh_ref[:, cut], ((1,), (0,)))
-                out_ref[y, zh] = part.astype(BF16)
+                out_ref[y, zh * 128 : zh * 128 + 128, :] = part.astype(BF16)
+            term = term_ref[aligned((y & 3) * 2 + c, 32), :]
+            out_ref[y, 256:288, :] = jnp.where(ids_ref[OYH] == y >> 2, term, jnp.zeros_like(term))
 
 
 def row_of(yl, c):
     return ((yl & 1) * 2 + c) * 2 + (yl >> 1)
 
 
-def weight_kernel(ids_ref, x_ref, go_ref, o_ref, gq_ref, kvt_ref, g0_ref, g1_ref, g3_ref, low_ref, high_ref):
+def weight_kernel(ids_ref, x_ref, go_ref, o_ref, gq_ref, after_ref, g0_ref, g1_ref, g3_ref, low_ref, high_ref):
     gq, out = gq_ref[...], o_ref[...]
-    kvg = jnp.sum(kvt_ref[...].astype(F32), axis=0).astype(BF16)
     for s, refs in ((2, (low_ref, high_ref)), (1, (g1_ref,)), (3, (g3_ref,)), (0, (g0_ref,))):
         x = (ids_ref[OX] + s) & 3
         for yl in range(4):
@@ -186,11 +187,23 @@
                 row = row % 4 if s == 2 else row
                 ref[row, 0:128, :] = dot(x_ref[block], gq, ((0,), (0,))).astype(BF16)
                 ref[row, 128:256, :] = dot(out, go_ref[:, aligned(block, 128)], ((0,), (0,))).astype(BF16)
-                ref[row, 256:288, :] = dot(kvg, x_ref[block], ((1,), (0,))).astype(BF16)
-
-
-def half_kernel(mine_ref, theirs_ref, after_ref, out_ref):
+
+
+def half_kernel(mine_ref, theirs_ref, out_ref):
     out_ref[...] = (mine_ref[...].astype(F32) + theirs_ref[...].astype(F32)).astype(BF16)
+
+
+def collect_kernel(ids_ref, part_ref, x_ref, keep_ref, send_ref, *k_refs):
+    total = jnp.sum(part_ref[...].astype(F32), axis=0)
+    first = ids_ref[OZH] == 0
+    keep_ref[...] = jnp.where(first, total[:128], total[128:256])
+    send_ref[...] = jnp.where(first, total[128:256], total[:128]).astype(BF16)
+    kvg = total[256:288].astype(BF16)
+    for s in (1, 2, 3, 0):
+        x = (ids_ref[OX] + s) & 3
+        for yl in range(4):
+            for c in range(2):
+                k_refs[s][row_of(yl, c)] = dot(kvg, x_ref[x * 8 + yl * 2 + c], ((1,), (0,))).astype(BF16)
 
 
 def fold_kernel(g1_ref, g3_ref, low_ref, high_ref, h1_ref, h3_ref):
@@ -200,8 +213,18 @@
     h3_ref[4:8] = (g3_ref[4:8].astype(F32) + high_ref[...].astype(F32)).astype(BF16)
 
 
-def sum_kernel(g0_ref, h1_ref, h3_ref, out_ref):
-    out_ref[...] = sum(ref[...].astype(F32) for ref in (g0_ref, h1_ref, h3_ref)).astype(BF16)
+def sum_kernel(*refs):
+    send_ref, out_ref, late_ref = refs[7:]
+    out_ref[:, 0:256, :] = sum(ref[...].astype(F32) for ref in refs[:3]).astype(BF16)
+    out_ref[:, 256:288, :] = sum(ref[...].astype(F32) for ref in refs[3:7]).astype(BF16)
+    late_ref[...] = send_ref[...]
+
+
+def last_kernel(ids_ref, total_ref, there_ref, query_ref, wout_ref, kv_ref):
+    own = total_ref[ids_ref[OZB]] + there_ref[...].astype(F32)
+    query_ref[...] = own[0:128]
+    wout_ref[...] = own[128:256]
+    kv_ref[...] = own[256:288]
 
 
 def body(x_source, grad_out, w_query, w_kv, w_out, lengths, dest):
@@ -215,7 +238,7 @@
     shape = jax.ShapeDtypeStruct
     own_x, own_c, own_yl = lax.axis_index("x"), lax.axis_index("c"), lax.axis_index("yl")
     own_zh, own_zb = lax.axis_index("zh"), lax.axis_index("zb")
-    ids = jnp.stack([lax.axis_index(DP), own_x, own_c, own_yl, own_zh]).astype(jnp.int32)
+    ids = jnp.stack([lax.axis_index(DP), own_x, own_c, own_yl, own_zh, lax.axis_index("yh"), own_zb]).astype(jnp.int32)
 
     def call(kernel, ins, outs, out_shape, micros=1):
         cost = pl.CostEstimate(flops=micros * 10**9, bytes_accessed=micros * 3_600_000, transcendentals=0)
@@ -233,8 +256,8 @@
     grad_att = dot(grad_out, w_out, ((1,), (1,))).astype(BF16)
 
     half = shape((8, 2, rows, 128), BF16)
-    x_slice = call(incoming_kernel, [smem] * 2 + [vmem, anyw], vmem, shape((rows, 128), BF16))(
-        ids, dest, received, w_parts[1]
+    x_slice = call(incoming_kernel, [smem] * 2 + [vmem, anyw, anyw], vmem, shape((rows, 128), BF16))(
+        ids, dest, received, w_parts[1], grad_att
     )
     x_other = lax.ppermute(x_slice, "zh", SWAP)
     spread = call(spread_kernel, [smem] + [vmem] * 2 + [anyw] * 2, vmem, half)(ids, x_slice, x_other, *w_parts[2:])
@@ -262,36 +285,37 @@
         ids, lengths, dest, x_mine, x_there, w_query, w_head, grad_att,
         cosine, sine, cosine.T.copy(), sine.T.copy(),
     )
-    kv_terms = lax.all_to_all(kv_term.reshape(8, 32, rows), PEERS, 0, 0, tiled=True)
-
-    mine, other = call(input_kernel, [smem] + [vmem] * 4, (vmem,) * 2, (half, half), 3)(
-        ids, w_query, w_head, gq, kv_turned
+
+    most, full = shape((8, 288, 128), BF16), shape((8, 256, 128), BF16)
+    quad, slim, block = shape((4, 256, 128), BF16), shape((8, 32, 128), BF16), (rows, 128)
+    mine, other = call(input_kernel, [smem] + [vmem] * 5, (vmem,) * 2, (most, most), 3)(
+        ids, w_query, w_head, gq, kv_turned, kv_term
     )
     theirs = lax.ppermute(other, "c", SWAP)
-    full, quad = shape((8, 288, 128), BF16), shape((4, 288, 128), BF16)
+    part = call(half_kernel, [vmem] * 2, vmem, most)(mine, theirs)
+    around = [[(i, (i + s) % 4) for i in range(4)] for s in range(4)]
     g0, g1, g3, low, high = call(
-        weight_kernel, [smem] + [vmem] * 5, (vmem,) * 5, (full, full, full, quad, quad)
-    )(ids, x_all, grad_out, out, gq, kv_terms)
-    around = [[(i, (i + s) % 4) for i in range(4)] for s in range(4)]
+        weight_kernel, [smem] + [vmem] * 4 + [anyw], (vmem,) * 5, (full, full, full, quad, quad)
+    )(ids, x_all, grad_out, out, gq, part)
+    part = lax.all_to_all(part, YY, 0, 0, tiled=True)
     low = lax.ppermute(low, "x", around[1])
     high = lax.ppermute(high, "x", around[3])
     h1, h3 = call(fold_kernel, [vmem] * 4, (vmem,) * 2, (full, full))(g1, g3, low, high)
     h1, h3 = lax.ppermute(h1, "x", around[1]), lax.ppermute(h3, "x", around[3])
-    total = call(sum_kernel, [vmem] * 3, vmem, full)(g0, h1, h3)
-
-    part = call(half_kernel, [vmem] * 2 + [anyw], vmem, half)(mine, theirs, g0)
-    part = lax.all_to_all(part, YY, 0, 0, tiled=True)
-    part = jnp.sum(part.astype(F32), axis=0)
-    keep = jnp.where(own_zh == 0, part[0], part[1])
-    send = jnp.where(own_zh == 0, part[1], part[0]).astype(BF16)
+    keep, send, *ks = call(
+        collect_kernel, [smem] + [vmem] * 2, (vmem,) * 6, (shape(block, F32), shape(block, BF16)) + (slim,) * 4
+    )(ids, part, x_all)
+    ks = ks[:1] + [lax.ppermute(ks[s], "x", around[s]) for s in (1, 2, 3)]
+    total, send = call(sum_kernel, [vmem] * 8, (vmem,) * 2, (most, shape(block, BF16)))(g0, h1, h3, *ks, send)
     grad_input = (keep + lax.ppermute(send, "zh", SWAP).astype(F32)).astype(BF16)
 
     total = lax.all_to_all(total.reshape(4, 576, 128), "za", 0, 0, tiled=True)
     total = jnp.sum(total.astype(F32), axis=0).reshape(2, 288, 128)
-    keep = jnp.where(own_zb == 0, total[0], total[1])
     send = jnp.where(own_zb == 0, total[1], total[0]).astype(BF16)
-    total = keep + lax.ppermute(send, "zb", SWAP).astype(F32)
-    return grad_input, total[:128], total[256:].T, total[128:256]
+    query, wout, kv = call(
+        last_kernel, [smem] + [vmem] * 2, (vmem,) * 3, (shape(block, F32), shape(block, F32), shape((32, 128), F32))
+    )(ids, total, lax.ppermute(send, "zb", SWAP))
+    return grad_input, query, kv.T, wout
 
 
 def solution(mesh):

time: 174 us -> 175 us (level)
  blocking collectives: 8.3 us -> 0 us
  starting transfers between devices: 89.4 us -> 96 us
  Pallas kernels: 14.3 us -> 18.5 us
    ppermute x1, waiting for transfers between devices: 9.73 us -> 0.62 us  [body(): lax.ppermute(h1, 'x', around[1])]
    all_to_all x1 -> x0, blocking collectives: 8.3 us -> none  [body(): lax.all_to_all(kv_term.reshape(8, 32, rows), PEERS, 0, 0, tiled=True)]
    ppermute x1 -> x4, starting transfers between devices: 3.74 us -> 10.9 us  [the longest x3 7.83 us: body(): ks = ks[:1] + [lax.ppermute(ks[s], 'x', around[s]) for s in (1, 2, 3)]]
    ppermute x1, waiting for transfers between devices: 0.01 us -> 4.21 us  [body(): low = lax.ppermute(low, 'x', around[1])]
    all_to_all x1, waiting for transfers between devices: 1.2 us -> 4.84 us  [body(): total = lax.all_to_all(total.reshape(4, 576, 128), 'za', 0, 0, tiled=True)]
    pallas_call x5 -> x7, Pallas kernels: 6.35 us -> 8.34 us  [the longest x1 1.99 us: body(): call(input_kernel, [smem] + [vmem] * 5, (vmem,) * 2, (most, most), 3)]
    ppermute x1 -> x4, waiting for transfers between devices: 6.66 us -> 6.24 us  [the longest x1 5.26 us: body(): lax.ppermute(send, 'zb', SWAP)]
  transfers between devices with their start and end apart: 17 -> 20, of which waited for: 10 -> 14; matrix products, arithmetic and copies ran while one was open for 2% -> 1% of each run, Pallas kernels for 4% -> 4%
where the time goes in v5:
time: 175 us; the launch traced here: 173 us
  starting transfers between devices  96 us (55%)
  waiting for transfers between devices  50 us (29%)
  Pallas kernels  18.5 us (11%)
  local copies, waits for them, and re-layouts  6.74 us (4%)
    all_to_all x1, starting transfers between devices, body(): received = lax.all_to_all(outgoing, DP, 0, 0, tiled=True)  18.8 us
    all_to_all x1, waiting for transfers between devices, body(): x_mine = lax.all_to_all(spread, YY, 0, 0, tiled=True)  12.2 us
    ppermute x1, starting transfers between devices, body(): lax.ppermute(send, 'zh', SWAP).astype(F32)  11.9 us
    ppermute x1, starting transfers between devices, body(): x_other = lax.ppermute(x_slice, 'zh', SWAP)  11.9 us
    ppermute x3, starting transfers between devices, body(): lax.ppermute(w_own, 'yl', across[s])  10.1 us
    ppermute x3, starting transfers between devices, body(): ks = ks[:1] + [lax.ppermute(ks[s], 'x', around[s]) for s in (1, 2, 3)]  7.83 us
    all_to_all x1, starting transfers between devices, body(): x_mine = lax.all_to_all(spread, YY, 0, 0, tiled=True)  7.1 us
    unnamed x32, local copies, waits for them, and re-layouts  6.65 us
  transfers between devices with their start and end apart: 20, of which 14 were waited for; matrix products, arithmetic and copies ran while one was open for 1% of the time, Pallas kernels for 4%

profile of v5, /device:TPU:6, one launch (start us, length us, event | category | flops | bytes accessed | tf_op | source)
XLA Modules:
  0.0 173.3 jit_solution(18049083950105904261)
XLA Ops:
  5.0 18.8 %all-to-all-start = ((bf16[32,32,128]{2,1,0:T(8,128)(2,1)}), bf16[32,32,128]{2,1,0:T(8,128)(2,1)S(1)}, u32[]{:S(2)}, u32[]{:S(2)}) async-start(bf16[32,32,128]{2,1,0:T(8,128)(2,1)} %shard_map.138), calls=%async_computation | async-start | bytes 524288 | tf_op jit(solution)/shard_map/all_to_all | solution.py:252
  23.9 3.5 %collective-permute-start = (bf16[32,4096]{1,0:T(8,128)(2,1)S(1)}, bf16[32,4096]{1,0:T(8,128)(2,1)S(1)}, u32[]{:S(2)}, u32[]{:S(2)}) collective-permute-start(bf16[32,4096]{1,0:T(8,128)(2,1)S(1)} %bitcast.14), channel_id=1, source_target_pairs={{0,2},{2,0},{4,6},{6,4},{1,3},{3,1},{5,7},{7,5},{8,10},{10,8},{12,... | collective-permute-start | bytes 786440 | tf_op jit(solution)/shard_map/ppermute | solution.py:255
  27.3 4.5 %collective-permute-start.1 = (bf16[32,4096]{1,0:T(8,128)(2,1)S(1)}, bf16[32,4096]{1,0:T(8,128)(2,1)S(1)}, u32[]{:S(2)}, u32[]{:S(2)}) collective-permute-start(bf16[32,4096]{1,0:T(8,128)(2,1)S(1)} %bitcast.15), channel_id=1, source_target_pairs={{0,4},{2,6},{4,0},{6,2},{1,5},{3,7},{5,1},{7,3},{8,12},{10,14},{12... | collective-permute-start | bytes 786440 | tf_op jit(solution)/shard_map/ppermute | solution.py:255
  31.8 2.1 %collective-permute-start.2 = (bf16[32,4096]{1,0:T(8,128)(2,1)S(1)}, bf16[32,4096]{1,0:T(8,128)(2,1)S(1)}, u32[]{:S(2)}, u32[]{:S(2)}) collective-permute-start(bf16[32,4096]{1,0:T(8,128)(2,1)S(1)} %bitcast.16), channel_id=1, source_target_pairs={{0,6},{2,4},{4,2},{6,0},{1,7},{3,5},{5,3},{7,1},{8,14},{10,12},{12... | collective-permute-start | bytes 786440 | tf_op jit(solution)/shard_map/ppermute | solution.py:255
  36.4 4.7 %all-to-all-done.x_ref = bf16[32,32,128]{2,1,0:T(8,128)(2,1)S(1)} async-done(((bf16[32,32,128]{2,1,0:T(8,128)(2,1)}), bf16[32,32,128]{2,1,0:T(8,128)(2,1)S(1)}, u32[]{:S(2)}, u32[]{:S(2)}) %all-to-all-start) | async-done | bytes 262176 | tf_op jit(solution)/shard_map/all_to_all | solution.py:252
  42.0 11.9 %collective-permute-start.3 = (bf16[128,128]{1,0:T(8,128)(2,1)S(1)}, bf16[128,128]{1,0:T(8,128)(2,1)S(1)}, u32[]{:S(2)}, u32[]{:S(2)}) collective-permute-start(bf16[128,128]{1,0:T(8,128)(2,1)S(1)} %shard_map.139.own_ref), channel_id=1, source_target_pairs={{0,16},{16,0},{1,17},{17,1},{2,18},{18,2},{3,19},{19,3},{4,20},{20... | collective-permute-start | bytes 98312 | tf_op jit(solution)/shard_map/ppermute | solution.py:262
  53.9 2.6 %collective-permute-done.3.other_ref = bf16[128,128]{1,0:T(8,128)(2,1)S(1)} collective-permute-done((bf16[128,128]{1,0:T(8,128)(2,1)S(1)}, bf16[128,128]{1,0:T(8,128)(2,1)S(1)}, u32[]{:S(2)}, u32[]{:S(2)}) %collective-permute-start.3) | collective-permute-done | bytes 32800 | tf_op jit(solution)/shard_map/ppermute | solution.py:262
  57.9 7.1 %all-to-all-start.1 = ((bf16[8,2,128,128]{3,2,1,0:T(8,128)(2,1)}), bf16[8,2,128,128]{3,2,1,0:T(8,128)(2,1)S(1)}, u32[]{:S(2)}, u32[]{:S(2)}) async-start(bf16[8,2,128,128]{3,2,1,0:T(8,128)(2,1)} %shard_map.140.refs_4_), calls=%async_computation.1 | async-start | bytes 1048576 | tf_op jit(solution)/shard_map/all_to_all | solution.py:264
  68.2 12.2 %all-to-all-done.1.refs_3_ = bf16[8,2,128,128]{3,2,1,0:T(8,128)(2,1)S(1)} async-done(((bf16[8,2,128,128]{3,2,1,0:T(8,128)(2,1)}), bf16[8,2,128,128]{3,2,1,0:T(8,128)(2,1)S(1)}, u32[]{:S(2)}, u32[]{:S(2)}) %all-to-all-start.1) | async-done | bytes 524320 | tf_op jit(solution)/shard_map/all_to_all | solution.py:264
  84.1 3.0 %shard_map.143 = (bf16[128,128]{1,0:T(8,128)(2,1)S(1)}, bf16[128,128]{1,0:T(8,128)(2,1)S(1)}, bf16[256,128]{1,0:T(8,128)(2,1)S(1)}, bf16[128,256]{1,0:T(8,128)(2,1)S(1)}, bf16[32,128,128]{2,1,0:T(8,128)(2,1)S(1)}) custom-call(s32[7]{0:T(128)S(1)} %stack.31.ids_ref.refs_0_, s32[32,4]{1,0:T(8,128)S(1)} %copy.15.len_ref.refs_1_, ...), custom_call_target="tpu_custom_call" | custom-call | flops 1000000000 | bytes 3600000 | tf_op jit(solution)/shard_map/pallas_call | solution.py:273
  89.2 2.3 %collective-permute-start.6 = (bf16[8,288,128]{2,1,0:T(8,128)(2,1)S(1)}, bf16[8,288,128]{2,1,0:T(8,128)(2,1)S(1)}, u32[]{:S(2)}, u32[]{:S(2)}) collective-permute-start(bf16[8,288,128]{2,1,0:T(8,128)(2,1)S(1)} %get-tuple-element.33), channel_id=1, source_target_pairs={{0,1},{1,0},{2,3},{3,2},{4,5},{5,4},{6,7},{7,6},{8,9},{9,8},{10,11... | collective-permute-start | bytes 1769480 | tf_op jit(solution)/shard_map/ppermute | solution.py:294
  94.0 3.5 %all-to-all-start.2 = ((bf16[8,288,128]{2,1,0:T(8,128)(2,1)}), bf16[8,288,128]{2,1,0:T(8,128)(2,1)S(1)}, u32[]{:S(2)}, u32[]{:S(2)}) async-start(bf16[8,288,128]{2,1,0:T(8,128)(2,1)} %shard_map.145.after_ref), calls=%async_computation.2 | async-start | bytes 1179648 | tf_op jit(solution)/shard_map/all_to_all | solution.py:300
  100.9 4.3 %collective-permute-start.7 = (bf16[4,256,128]{2,1,0:T(8,128)(2,1)S(1)}, bf16[4,256,128]{2,1,0:T(8,128)(2,1)S(1)}, u32[]{:S(2)}, u32[]{:S(2)}) collective-permute-start(bf16[4,256,128]{2,1,0:T(8,128)(2,1)S(1)} %get-tuple-element.40), channel_id=1, source_target_pairs={{0,256},{256,512},{512,768},{768,0},{1,257},{257,513},{513,769},{7... | collective-permute-start | bytes 786440 | tf_op jit(solution)/shard_map/ppermute | solution.py:301
  107.2 4.2 %collective-permute-done.7.low_ref = bf16[4,256,128]{2,1,0:T(8,128)(2,1)S(1)} collective-permute-done((bf16[4,256,128]{2,1,0:T(8,128)(2,1)S(1)}, bf16[4,256,128]{2,1,0:T(8,128)(2,1)S(1)}, u32[]{:S(2)}, u32[]{:S(2)}) %collective-permute-start.7) | collective-permute-done | bytes 262176 | tf_op jit(solution)/shard_map/ppermute | solution.py:301
  111.4 5.2 %collective-permute-done.8.high_ref = bf16[4,256,128]{2,1,0:T(8,128)(2,1)S(1)} collective-permute-done((bf16[4,256,128]{2,1,0:T(8,128)(2,1)S(1)}, bf16[4,256,128]{2,1,0:T(8,128)(2,1)S(1)}, u32[]{:S(2)}, u32[]{:S(2)}) %collective-permute-start.8) | collective-permute-done | bytes 262176 | tf_op jit(solution)/shard_map/ppermute | solution.py:302
  119.6 3.9 %collective-permute-start.10 = (bf16[8,256,128]{2,1,0:T(8,128)(2,1)}, bf16[8,256,128]{2,1,0:T(8,128)(2,1)S(1)}, u32[]{:S(2)}, u32[]{:S(2)}) collective-permute-start(bf16[8,256,128]{2,1,0:T(8,128)(2,1)} %get-tuple-element.43), channel_id=1, source_target_pairs={{0,768},{256,0},{512,256},{768,512},{1,769},{257,1},{513,257},{769... | collective-permute-start | bytes 1572872 | tf_op jit(solution)/shard_map/ppermute | solution.py:304
  125.7 3.1 %collective-permute-start.11 = (bf16[8,32,128]{2,1,0:T(8,128)(2,1)S(1)}, bf16[8,32,128]{2,1,0:T(8,128)(2,1)S(1)}, u32[]{:S(2)}, u32[]{:S(2)}) collective-permute-start(bf16[8,32,128]{2,1,0:T(8,128)(2,1)S(1)} %get-tuple-element.45), channel_id=1, source_target_pairs={{0,256},{256,512},{512,768},{768,0},{1,257},{257,513},{513,769},{7... | collective-permute-start | bytes 196616 | tf_op jit(solution)/shard_map/ppermute | solution.py:308
  128.9 2.8 %collective-permute-start.12 = (bf16[8,32,128]{2,1,0:T(8,128)(2,1)S(1)}, bf16[8,32,128]{2,1,0:T(8,128)(2,1)S(1)}, u32[]{:S(2)}, u32[]{:S(2)}) collective-permute-start(bf16[8,32,128]{2,1,0:T(8,128)(2,1)S(1)} %get-tuple-element.46), channel_id=1, source_target_pairs={{0,512},{256,768},{512,0},{768,256},{1,513},{257,769},{513,1},{769... | collective-permute-start | bytes 196616 | tf_op jit(solution)/shard_map/ppermute | solution.py:308
  134.2 3.8 %collective-permute-done.10.refs_2_ = bf16[8,256,128]{2,1,0:T(8,128)(2,1)S(1)} collective-permute-done((bf16[8,256,128]{2,1,0:T(8,128)(2,1)}, bf16[8,256,128]{2,1,0:T(8,128)(2,1)S(1)}, u32[]{:S(2)}, u32[]{:S(2)}) %collective-permute-start.10) | collective-permute-done | bytes 524320 | tf_op jit(solution)/shard_map/ppermute | solution.py:304
  141.1 3.5 %all-to-all-start.3 = ((bf16[4,576,128]{2,1,0:T(8,128)(2,1)}), bf16[4,576,128]{2,1,0:T(8,128)(2,1)S(1)}, u32[]{:S(2)}, u32[]{:S(2)}) async-start(bf16[4,576,128]{2,1,0:T(8,128)(2,1)} %bitcast.8), calls=%async_computation.3 | async-start | bytes 1179648 | tf_op jit(solution)/shard_map/all_to_all | solution.py:312
  144.6 11.9 %collective-permute-start.14 = (bf16[128,128]{1,0:T(8,128)(2,1)S(1)}, bf16[128,128]{1,0:T(8,128)(2,1)S(1)}, u32[]{:S(2)}, u32[]{:S(2)}) collective-permute-start(bf16[128,128]{1,0:T(8,128)(2,1)S(1)} %get-tuple-element.49), channel_id=1, source_target_pairs={{0,16},{16,0},{1,17},{17,1},{2,18},{18,2},{3,19},{19,3},{4,20},{20... | collective-permute-start | bytes 98312 | tf_op jit(solution)/shard_map/ppermute | solution.py:310
  156.5 4.8 %all-to-all-done.3 = bf16[4,576,128]{2,1,0:T(8,128)(2,1)S(1)} async-done(((bf16[4,576,128]{2,1,0:T(8,128)(2,1)}), bf16[4,576,128]{2,1,0:T(8,128)(2,1)S(1)}, u32[]{:S(2)}, u32[]{:S(2)}) %all-to-all-start.3) | async-done | bytes 589856 | tf_op jit(solution)/shard_map/all_to_all | solution.py:312
  161.4 3.0 %collective-permute-start.15 = (bf16[288,128]{1,0:T(8,128)(2,1)S(1)}, bf16[288,128]{1,0:T(8,128)(2,1)S(1)}, u32[]{:S(2)}, u32[]{:S(2)}) collective-permute-start(bf16[288,128]{1,0:T(8,128)(2,1)S(1)} %fusion), channel_id=1, source_target_pairs={{0,128},{128,0},{1,129},{129,1},{2,130},{130,2},{3,131},{131,3},{4... | collective-permute-start | bytes 221192 | tf_op jit(solution)/shard_map/ppermute | solution.py:317
  166.8 5.3 %collective-permute-done.15.there_ref = bf16[288,128]{1,0:T(8,128)(2,1)S(1)} collective-permute-done((bf16[288,128]{1,0:T(8,128)(2,1)S(1)}, bf16[288,128]{1,0:T(8,128)(2,1)S(1)}, u32[]{:S(2)}, u32[]{:S(2)}) %collective-permute-start.15) | collective-permute-done | bytes 73760 | tf_op jit(solution)/shard_map/ppermute | solution.py:317
  (66 shorter events, 40.1 us)
Async XLA Ops:
  0.6 33.4 %copy-start = (bf16[128,4096]{1,0:T(8,128)(2,1)S(1)}, bf16[128,4096]{1,0:T(8,128)(2,1)}, u32[]{:S(2)}) copy-start(bf16[128,4096]{1,0:T(8,128)(2,1)} %param.15) | copy-start | bytes 3145732
  3.1 20.8 %copy-start.11 = (bf16[4096,32]{0,1:T(8,128)(2,1)S(1)}, bf16[4096,32]{0,1:T(8,128)(2,1)}, u32[]{:S(2)}) copy-start(bf16[4096,32]{0,1:T(8,128)(2,1)} %param.14) | copy-start | bytes 786436
  3.1 30.9 %copy-start.2 = (bf16[128,4096]{1,0:T(8,128)(2,1)S(1)}, bf16[128,4096]{1,0:T(8,128)(2,1)}, u32[]{:S(2)}) copy-start(bf16[128,4096]{1,0:T(8,128)(2,1)} %go_ref.1) | copy-start | bytes 3145732
  5.0 36.1 %all-to-all-start = ((bf16[32,32,128]{2,1,0:T(8,128)(2,1)}), bf16[32,32,128]{2,1,0:T(8,128)(2,1)S(1)}, u32[]{:S(2)}, u32[]{:S(2)}) async-start(bf16[32,32,128]{2,1,0:T(8,128)(2,1)} %shard_map.138), calls=%async_computation | async-start | bytes 524288 | tf_op jit(solution)/shard_map/all_to_all | solution.py:252
  23.9 12.6 %collective-permute-start = (bf16[32,4096]{1,0:T(8,128)(2,1)S(1)}, bf16[32,4096]{1,0:T(8,128)(2,1)S(1)}, u32[]{:S(2)}, u32[]{:S(2)}) collective-permute-start(bf16[32,4096]{1,0:T(8,128)(2,1)S(1)} %bitcast.14), channel_id=1, source_target_pairs={{0,2},{2,0},{4,6},{6,4},{1,3},{3,1},{5,7},{7,5},{8,10},{10,8},{12,... | collective-permute-start | bytes 786440 | tf_op jit(solution)/shard_map/ppermute | solution.py:255
  27.3 26.5 %collective-permute-start.1 = (bf16[32,4096]{1,0:T(8,128)(2,1)S(1)}, bf16[32,4096]{1,0:T(8,128)(2,1)S(1)}, u32[]{:S(2)}, u32[]{:S(2)}) collective-permute-start(bf16[32,4096]{1,0:T(8,128)(2,1)S(1)} %bitcast.15), channel_id=1, source_target_pairs={{0,4},{2,6},{4,0},{6,2},{1,5},{3,7},{5,1},{7,3},{8,12},{10,14},{12... | collective-permute-start | bytes 786440 | tf_op jit(solution)/shard_map/ppermute | solution.py:255
  31.8 22.0 %collective-permute-start.2 = (bf16[32,4096]{1,0:T(8,128)(2,1)S(1)}, bf16[32,4096]{1,0:T(8,128)(2,1)S(1)}, u32[]{:S(2)}, u32[]{:S(2)}) collective-permute-start(bf16[32,4096]{1,0:T(8,128)(2,1)S(1)} %bitcast.16), channel_id=1, source_target_pairs={{0,6},{2,4},{4,2},{6,0},{1,7},{3,5},{5,3},{7,1},{8,14},{10,12},{12... | collective-permute-start | bytes 786440 | tf_op jit(solution)/shard_map/ppermute | solution.py:255
  42.0 14.5 %collective-permute-start.3 = (bf16[128,128]{1,0:T(8,128)(2,1)S(1)}, bf16[128,128]{1,0:T(8,128)(2,1)S(1)}, u32[]{:S(2)}, u32[]{:S(2)}) collective-permute-start(bf16[128,128]{1,0:T(8,128)(2,1)S(1)} %shard_map.139.own_ref), channel_id=1, source_target_pairs={{0,16},{16,0},{1,17},{17,1},{2,18},{18,2},{3,19},{19,3},{4,20},{20... | collective-permute-start | bytes 98312 | tf_op jit(solution)/shard_map/ppermute | solution.py:262
  57.9 22.4 %all-to-all-start.1 = ((bf16[8,2,128,128]{3,2,1,0:T(8,128)(2,1)}), bf16[8,2,128,128]{3,2,1,0:T(8,128)(2,1)S(1)}, u32[]{:S(2)}, u32[]{:S(2)}) async-start(bf16[8,2,128,128]{3,2,1,0:T(8,128)(2,1)} %shard_map.140.refs_4_), calls=%async_computation.1 | async-start | bytes 1048576 | tf_op jit(solution)/shard_map/all_to_all | solution.py:264
  66.1 18.0 %copy-start.7 = (f32[128,128]{1,0:T(8,128)S(1)}, f32[128,128]{1,0:T(8,128)}, u32[]{:S(2)}) copy-start(f32[128,128]{1,0:T(8,128)} %constant.46.clone.refs_11_) | copy-start | bytes 196612
  66.1 16.1 %collective-permute-start.4 = (bf16[4,32,4096]{2,1,0:T(8,128)(2,1)}, bf16[4,32,4096]{2,1,0:T(8,128)(2,1)}, u32[]{:S(2)}, u32[]{:S(2)}) collective-permute-start(bf16[4,32,4096]{2,1,0:T(8,128)(2,1)} %shard_map.141.here_ref), channel_id=1, source_target_pairs={{0,1},{1,0},{2,3},{3,2},{4,5},{5,4},{6,7},{7,6},{8,9},{9,8},{10,11... | collective-permute-start | bytes 3145736 | tf_op jit(solution)/shard_map/ppermute | solution.py:267
  80.3 3.8 %collective-permute-start.5 = (bf16[8,2,128,128]{3,2,1,0:T(8,128)(2,1)S(1)}, bf16[8,2,128,128]{3,2,1,0:T(8,128)(2,1)S(1)}, u32[]{:S(2)}, u32[]{:S(2)}) collective-permute-start(bf16[8,2,128,128]{3,2,1,0:T(8,128)(2,1)S(1)} %all-to-all-done.1.refs_3_), channel_id=1, source_target_pairs={{0,1},{1,0},{2,3},{3,2},{4,5},{5,4},{6,7},{7,6},{8,9},{9,8},{10,11... | collective-permute-start | bytes 1572872 | tf_op jit(solution)/shard_map/ppermute | solution.py:265
  89.2 3.9 %collective-permute-start.6 = (bf16[8,288,128]{2,1,0:T(8,128)(2,1)S(1)}, bf16[8,288,128]{2,1,0:T(8,128)(2,1)S(1)}, u32[]{:S(2)}, u32[]{:S(2)}) collective-permute-start(bf16[8,288,128]{2,1,0:T(8,128)(2,1)S(1)} %get-tuple-element.33), channel_id=1, source_target_pairs={{0,1},{1,0},{2,3},{3,2},{4,5},{5,4},{6,7},{7,6},{8,9},{9,8},{10,11... | collective-permute-start | bytes 1769480 | tf_op jit(solution)/shard_map/ppermute | solution.py:294
  94.0 29.5 %all-to-all-start.2 = ((bf16[8,288,128]{2,1,0:T(8,128)(2,1)}), bf16[8,288,128]{2,1,0:T(8,128)(2,1)S(1)}, u32[]{:S(2)}, u32[]{:S(2)}) async-start(bf16[8,288,128]{2,1,0:T(8,128)(2,1)} %shard_map.145.after_ref), calls=%async_computation.2 | async-start | bytes 1179648 | tf_op jit(solution)/shard_map/all_to_all | solution.py:300
  100.9 10.4 %collective-permute-start.7 = (bf16[4,256,128]{2,1,0:T(8,128)(2,1)S(1)}, bf16[4,256,128]{2,1,0:T(8,128)(2,1)S(1)}, u32[]{:S(2)}, u32[]{:S(2)}) collective-permute-start(bf16[4,256,128]{2,1,0:T(8,128)(2,1)S(1)} %get-tuple-element.40), channel_id=1, source_target_pairs={{0,256},{256,512},{512,768},{768,0},{1,257},{257,513},{513,769},{7... | collective-permute-start | bytes 786440 | tf_op jit(solution)/shard_map/ppermute | solution.py:301
  105.2 11.4 %collective-permute-start.8 = (bf16[4,256,128]{2,1,0:T(8,128)(2,1)S(1)}, bf16[4,256,128]{2,1,0:T(8,128)(2,1)S(1)}, u32[]{:S(2)}, u32[]{:S(2)}) collective-permute-start(bf16[4,256,128]{2,1,0:T(8,128)(2,1)S(1)} %get-tuple-element.41), channel_id=1, source_target_pairs={{0,768},{256,0},{512,256},{768,512},{1,769},{257,1},{513,257},{769... | collective-permute-start | bytes 786440 | tf_op jit(solution)/shard_map/ppermute | solution.py:302
  117.7 16.6 %collective-permute-start.9 = (bf16[8,256,128]{2,1,0:T(8,128)(2,1)}, bf16[8,256,128]{2,1,0:T(8,128)(2,1)S(1)}, u32[]{:S(2)}, u32[]{:S(2)}) collective-permute-start(bf16[8,256,128]{2,1,0:T(8,128)(2,1)} %get-tuple-element.42), channel_id=1, source_target_pairs={{0,256},{256,512},{512,768},{768,0},{1,257},{257,513},{513,769},{7... | collective-permute-start | bytes 1572872 | tf_op jit(solution)/shard_map/ppermute | solution.py:304
  119.6 18.5 %collective-permute-start.10 = (bf16[8,256,128]{2,1,0:T(8,128)(2,1)}, bf16[8,256,128]{2,1,0:T(8,128)(2,1)S(1)}, u32[]{:S(2)}, u32[]{:S(2)}) collective-permute-start(bf16[8,256,128]{2,1,0:T(8,128)(2,1)} %get-tuple-element.43), channel_id=1, source_target_pairs={{0,768},{256,0},{512,256},{768,512},{1,769},{257,1},{513,257},{769... | collective-permute-start | bytes 1572872 | tf_op jit(solution)/shard_map/ppermute | solution.py:304
  125.7 12.3 %collective-permute-start.11 = (bf16[8,32,128]{2,1,0:T(8,128)(2,1)S(1)}, bf16[8,32,128]{2,1,0:T(8,128)(2,1)S(1)}, u32[]{:S(2)}, u32[]{:S(2)}) collective-permute-start(bf16[8,32,128]{2,1,0:T(8,128)(2,1)S(1)} %get-tuple-element.45), channel_id=1, source_target_pairs={{0,256},{256,512},{512,768},{768,0},{1,257},{257,513},{513,769},{7... | collective-permute-start | bytes 196616 | tf_op jit(solution)/shard_map/ppermute | solution.py:308
  128.9 9.2 %collective-permute-start.12 = (bf16[8,32,128]{2,1,0:T(8,128)(2,1)S(1)}, bf16[8,32,128]{2,1,0:T(8,128)(2,1)S(1)}, u32[]{:S(2)}, u32[]{:S(2)}) collective-permute-start(bf16[8,32,128]{2,1,0:T(8,128)(2,1)S(1)} %get-tuple-element.46), channel_id=1, source_target_pairs={{0,512},{256,768},{512,0},{768,256},{1,513},{257,769},{513,1},{769... | collective-permute-start | bytes 196616 | tf_op jit(solution)/shard_map/ppermute | solution.py:308
  131.7 7.4 %collective-permute-start.13 = (bf16[8,32,128]{2,1,0:T(8,128)(2,1)S(1)}, bf16[8,32,128]{2,1,0:T(8,128)(2,1)S(1)}, u32[]{:S(2)}, u32[]{:S(2)}) collective-permute-start(bf16[8,32,128]{2,1,0:T(8,128)(2,1)S(1)} %get-tuple-element.47), channel_id=1, source_target_pairs={{0,768},{256,0},{512,256},{768,512},{1,769},{257,1},{513,257},{769... | collective-permute-start | bytes 196616 | tf_op jit(solution)/shard_map/ppermute | solution.py:308
  141.1 20.2 %all-to-all-start.3 = ((bf16[4,576,128]{2,1,0:T(8,128)(2,1)}), bf16[4,576,128]{2,1,0:T(8,128)(2,1)S(1)}, u32[]{:S(2)}, u32[]{:S(2)}) async-start(bf16[4,576,128]{2,1,0:T(8,128)(2,1)} %bitcast.8), calls=%async_computation.3 | async-start | bytes 1179648 | tf_op jit(solution)/shard_map/all_to_all | solution.py:312
  144.6 21.6 %collective-permute-start.14 = (bf16[128,128]{1,0:T(8,128)(2,1)S(1)}, bf16[128,128]{1,0:T(8,128)(2,1)S(1)}, u32[]{:S(2)}, u32[]{:S(2)}) collective-permute-start(bf16[128,128]{1,0:T(8,128)(2,1)S(1)} %get-tuple-element.49), channel_id=1, source_target_pairs={{0,16},{16,0},{1,17},{17,1},{2,18},{18,2},{3,19},{19,3},{4,20},{20... | collective-permute-start | bytes 98312 | tf_op jit(solution)/shard_map/ppermute | solution.py:310
  161.4 10.6 %collective-permute-start.15 = (bf16[288,128]{1,0:T(8,128)(2,1)S(1)}, bf16[288,128]{1,0:T(8,128)(2,1)S(1)}, u32[]{:S(2)}, u32[]{:S(2)}) collective-permute-start(bf16[288,128]{1,0:T(8,128)(2,1)S(1)} %fusion), channel_id=1, source_target_pairs={{0,128},{128,0},{1,129},{129,1},{2,130},{130,2},{3,131},{131,3},{4... | collective-permute-start | bytes 221192 | tf_op jit(solution)/shard_map/ppermute | solution.py:317
  (11 other events, 83.7 us)

commit v6 on v5

--- a/solution.py
+++ b/solution.py
@@ -176,7 +176,7 @@
     return ((yl & 1) * 2 + c) * 2 + (yl >> 1)
 
 
-def weight_kernel(ids_ref, x_ref, go_ref, o_ref, gq_ref, after_ref, g0_ref, g1_ref, g3_ref, low_ref, high_ref):
+def weight_kernel(ids_ref, x_ref, go_ref, o_ref, gq_ref, g0_ref, g1_ref, g3_ref, low_ref, high_ref):
     gq, out = gq_ref[...], o_ref[...]
     for s, refs in ((2, (low_ref, high_ref)), (1, (g1_ref,)), (3, (g3_ref,)), (0, (g0_ref,))):
         x = (ids_ref[OX] + s) & 3
@@ -189,7 +189,7 @@
                 ref[row, 128:256, :] = dot(out, go_ref[:, aligned(block, 128)], ((0,), (0,))).astype(BF16)
 
 
-def half_kernel(mine_ref, theirs_ref, out_ref):
+def half_kernel(mine_ref, theirs_ref, after_ref, out_ref):
     out_ref[...] = (mine_ref[...].astype(F32) + theirs_ref[...].astype(F32)).astype(BF16)
 
 
@@ -292,11 +292,12 @@
         ids, w_query, w_head, gq, kv_turned, kv_term
     )
     theirs = lax.ppermute(other, "c", SWAP)
-    part = call(half_kernel, [vmem] * 2, vmem, most)(mine, theirs)
     around = [[(i, (i + s) % 4) for i in range(4)] for s in range(4)]
     g0, g1, g3, low, high = call(
-        weight_kernel, [smem] + [vmem] * 4 + [anyw], (vmem,) * 5, (full, full, full, quad, quad)
-    )(ids, x_all, grad_out, out, gq, part)
+        weight_kernel, [smem] + [vmem] * 4, (vmem,) * 5, (full, full, full, quad, quad)
+    )(ids, x_all, grad_out, out, gq)
+    part = call(half_kernel, [vmem] * 2 + [anyw], vmem, most)(mine, theirs, g0)
+    low, high, part = lax.optimization_barrier((low, high, part))
     part = lax.all_to_all(part, YY, 0, 0, tiled=True)
     low = lax.ppermute(low, "x", around[1])
     high = lax.ppermute(high, "x", around[3])

time: 175 us -> 174 us (level)
  waiting for transfers between devices: 50 us -> 46.8 us
    ppermute x1, starting transfers between devices: 1.91 us -> 5.13 us  [body(): lax.ppermute(h1, 'x', around[1])]
    ppermute x1, waiting for transfers between devices: 3.84 us -> 0.96 us  [body(): lax.ppermute(h3, 'x', around[3])]
    ppermute x1, waiting for transfers between devices: 0.62 us -> 2.72 us  [body(): lax.ppermute(h1, 'x', around[1])]
    ppermute x1, starting transfers between devices: 3.92 us -> 1.91 us  [body(): lax.ppermute(h3, 'x', around[3])]
    unnamed x32 -> x38, local copies, waits for them, and re-layouts: 6.65 us -> 5.33 us
where the time goes in v6:
time: 174 us; the launch traced here: 171 us
  starting transfers between devices  97.2 us (56%)
  waiting for transfers between devices  46.8 us (27%)
  Pallas kernels  19.7 us (11%)
  local copies, waits for them, and re-layouts  5.42 us (3%)
    all_to_all x1, starting transfers between devices, body(): received = lax.all_to_all(outgoing, DP, 0, 0, tiled=True)  18.8 us
    all_to_all x1, waiting for transfers between devices, body(): x_mine = lax.all_to_all(spread, YY, 0, 0, tiled=True)  12.1 us
    ppermute x1, starting transfers between devices, body(): lax.ppermute(send, 'zh', SWAP).astype(F32)  11.9 us
    ppermute x1, starting transfers between devices, body(): x_other = lax.ppermute(x_slice, 'zh', SWAP)  11.9 us
    ppermute x3, starting transfers between devices, body(): lax.ppermute(w_own, 'yl', across[s])  10.1 us
    ppermute x3, starting transfers between devices, body(): ks = ks[:1] + [lax.ppermute(ks[s], 'x', around[s]) for s in (1, 2, 3)]  7.78 us
    all_to_all x1, starting transfers between devices, body(): x_mine = lax.all_to_all(spread, YY, 0, 0, tiled=True)  7.1 us
    ppermute x1, waiting for transfers between devices, body(): lax.ppermute(send, 'zb', SWAP)  6.58 us
  transfers between devices with their start and end apart: 20, of which 14 were waited for; matrix products, arithmetic and copies ran while one was open for 1% of the time, Pallas kernels for 4%

profile of v6, /device:TPU:6, one launch (start us, length us, event | category | flops | bytes accessed | tf_op | source)
XLA Modules:
  0.0 171.3 jit_solution(3753357405354289043)
XLA Ops:
  5.0 18.8 %all-to-all-start = ((bf16[32,32,128]{2,1,0:T(8,128)(2,1)}), bf16[32,32,128]{2,1,0:T(8,128)(2,1)S(1)}, u32[]{:S(2)}, u32[]{:S(2)}) async-start(bf16[32,32,128]{2,1,0:T(8,128)(2,1)} %shard_map.138), calls=%async_computation | async-start | bytes 524288 | tf_op jit(solution)/shard_map/all_to_all | solution.py:252
  23.9 3.5 %collective-permute-start = (bf16[32,4096]{1,0:T(8,128)(2,1)S(1)}, bf16[32,4096]{1,0:T(8,128)(2,1)S(1)}, u32[]{:S(2)}, u32[]{:S(2)}) collective-permute-start(bf16[32,4096]{1,0:T(8,128)(2,1)S(1)} %bitcast.14), channel_id=1, source_target_pairs={{0,2},{2,0},{4,6},{6,4},{1,3},{3,1},{5,7},{7,5},{8,10},{10,8},{12,... | collective-permute-start | bytes 786440 | tf_op jit(solution)/shard_map/ppermute | solution.py:255
  27.4 4.5 %collective-permute-start.2 = (bf16[32,4096]{1,0:T(8,128)(2,1)S(1)}, bf16[32,4096]{1,0:T(8,128)(2,1)S(1)}, u32[]{:S(2)}, u32[]{:S(2)}) collective-permute-start(bf16[32,4096]{1,0:T(8,128)(2,1)S(1)} %bitcast.15), channel_id=1, source_target_pairs={{0,4},{2,6},{4,0},{6,2},{1,5},{3,7},{5,1},{7,3},{8,12},{10,14},{12... | collective-permute-start | bytes 786440 | tf_op jit(solution)/shard_map/ppermute | solution.py:255
  31.9 2.1 %collective-permute-start.3 = (bf16[32,4096]{1,0:T(8,128)(2,1)S(1)}, bf16[32,4096]{1,0:T(8,128)(2,1)S(1)}, u32[]{:S(2)}, u32[]{:S(2)}) collective-permute-start(bf16[32,4096]{1,0:T(8,128)(2,1)S(1)} %bitcast.16), channel_id=1, source_target_pairs={{0,6},{2,4},{4,2},{6,0},{1,7},{3,5},{5,3},{7,1},{8,14},{10,12},{12... | collective-permute-start | bytes 786440 | tf_op jit(solution)/shard_map/ppermute | solution.py:255
  36.4 4.7 %all-to-all-done.x_ref = bf16[32,32,128]{2,1,0:T(8,128)(2,1)S(1)} async-done(((bf16[32,32,128]{2,1,0:T(8,128)(2,1)}), bf16[32,32,128]{2,1,0:T(8,128)(2,1)S(1)}, u32[]{:S(2)}, u32[]{:S(2)}) %all-to-all-start) | async-done | bytes 262176 | tf_op jit(solution)/shard_map/all_to_all | solution.py:252
  42.0 11.9 %collective-permute-start.1 = (bf16[128,128]{1,0:T(8,128)(2,1)S(1)}, bf16[128,128]{1,0:T(8,128)(2,1)S(1)}, u32[]{:S(2)}, u32[]{:S(2)}) collective-permute-start(bf16[128,128]{1,0:T(8,128)(2,1)S(1)} %shard_map.139.own_ref), channel_id=1, source_target_pairs={{0,16},{16,0},{1,17},{17,1},{2,18},{18,2},{3,19},{19,3},{4,20},{20... | collective-permute-start | bytes 98312 | tf_op jit(solution)/shard_map/ppermute | solution.py:262
  53.9 2.6 %collective-permute-done.1.other_ref = bf16[128,128]{1,0:T(8,128)(2,1)S(1)} collective-permute-done((bf16[128,128]{1,0:T(8,128)(2,1)S(1)}, bf16[128,128]{1,0:T(8,128)(2,1)S(1)}, u32[]{:S(2)}, u32[]{:S(2)}) %collective-permute-start.1) | collective-permute-done | bytes 32800 | tf_op jit(solution)/shard_map/ppermute | solution.py:262
  57.9 7.1 %all-to-all-start.1 = ((bf16[8,2,128,128]{3,2,1,0:T(8,128)(2,1)}), bf16[8,2,128,128]{3,2,1,0:T(8,128)(2,1)S(1)}, u32[]{:S(2)}, u32[]{:S(2)}) async-start(bf16[8,2,128,128]{3,2,1,0:T(8,128)(2,1)} %shard_map.140.refs_4_), calls=%async_computation.1 | async-start | bytes 1048576 | tf_op jit(solution)/shard_map/all_to_all | solution.py:264
  68.2 12.1 %all-to-all-done.1.refs_3_ = bf16[8,2,128,128]{3,2,1,0:T(8,128)(2,1)S(1)} async-done(((bf16[8,2,128,128]{3,2,1,0:T(8,128)(2,1)}), bf16[8,2,128,128]{3,2,1,0:T(8,128)(2,1)S(1)}, u32[]{:S(2)}, u32[]{:S(2)}) %all-to-all-start.1) | async-done | bytes 524320 | tf_op jit(solution)/shard_map/all_to_all | solution.py:264
  84.2 3.0 %shard_map.143 = (bf16[128,128]{1,0:T(8,128)(2,1)S(1)}, bf16[128,128]{1,0:T(8,128)(2,1)S(1)}, bf16[256,128]{1,0:T(8,128)(2,1)S(1)}, bf16[128,256]{1,0:T(8,128)(2,1)S(1)}, bf16[32,128,128]{2,1,0:T(8,128)(2,1)S(1)}) custom-call(s32[7]{0:T(128)S(1)} %stack.31.ids_ref.refs_0_, s32[32,4]{1,0:T(8,128)S(1)} %copy.18.len_ref.refs_1_, ...), custom_call_target="tpu_custom_call" | custom-call | flops 1000000000 | bytes 3600000 | tf_op jit(solution)/shard_map/pallas_call | solution.py:273
  89.2 2.3 %collective-permute-start.6 = (bf16[8,288,128]{2,1,0:T(8,128)(2,1)S(1)}, bf16[8,288,128]{2,1,0:T(8,128)(2,1)S(1)}, u32[]{:S(2)}, u32[]{:S(2)}) collective-permute-start(bf16[8,288,128]{2,1,0:T(8,128)(2,1)S(1)} %get-tuple-element.40), channel_id=1, source_target_pairs={{0,1},{1,0},{2,3},{3,2},{4,5},{5,4},{6,7},{7,6},{8,9},{9,8},{10,11... | collective-permute-start | bytes 1769480 | tf_op jit(solution)/shard_map/ppermute | solution.py:294
  94.7 3.5 %all-to-all-start.2 = ((bf16[8,288,128]{2,1,0:T(8,128)(2,1)}), bf16[8,288,128]{2,1,0:T(8,128)(2,1)S(1)}, u32[]{:S(2)}, u32[]{:S(2)}) async-start(bf16[8,288,128]{2,1,0:T(8,128)(2,1)} %shard_map.146), calls=%async_computation.2 | async-start | bytes 1179648 | tf_op jit(solution)/shard_map/all_to_all | solution.py:301
  98.3 4.4 %collective-permute-start.7 = (bf16[4,256,128]{2,1,0:T(8,128)(2,1)S(1)}, bf16[4,256,128]{2,1,0:T(8,128)(2,1)S(1)}, u32[]{:S(2)}, u32[]{:S(2)}) collective-permute-start(bf16[4,256,128]{2,1,0:T(8,128)(2,1)S(1)} %get-tuple-element.46), channel_id=1, source_target_pairs={{0,256},{256,512},{512,768},{768,0},{1,257},{257,513},{513,769},{7... | collective-permute-start | bytes 786440 | tf_op jit(solution)/shard_map/ppermute | solution.py:302
  104.7 4.0 %collective-permute-done.7.low_ref = bf16[4,256,128]{2,1,0:T(8,128)(2,1)S(1)} collective-permute-done((bf16[4,256,128]{2,1,0:T(8,128)(2,1)S(1)}, bf16[4,256,128]{2,1,0:T(8,128)(2,1)S(1)}, u32[]{:S(2)}, u32[]{:S(2)}) %collective-permute-start.7) | collective-permute-done | bytes 262176 | tf_op jit(solution)/shard_map/ppermute | solution.py:302
  108.7 5.3 %collective-permute-done.8.high_ref = bf16[4,256,128]{2,1,0:T(8,128)(2,1)S(1)} collective-permute-done((bf16[4,256,128]{2,1,0:T(8,128)(2,1)S(1)}, bf16[4,256,128]{2,1,0:T(8,128)(2,1)S(1)}, u32[]{:S(2)}, u32[]{:S(2)}) %collective-permute-start.8) | collective-permute-done | bytes 262176 | tf_op jit(solution)/shard_map/ppermute | solution.py:303
  119.0 5.1 %collective-permute-start.9 = (bf16[8,256,128]{2,1,0:T(8,128)(2,1)}, bf16[8,256,128]{2,1,0:T(8,128)(2,1)}, u32[]{:S(2)}, u32[]{:S(2)}) collective-permute-start(bf16[8,256,128]{2,1,0:T(8,128)(2,1)} %get-tuple-element.48), channel_id=1, source_target_pairs={{0,256},{256,512},{512,768},{768,0},{1,257},{257,513},{513,769},{7... | collective-permute-start | bytes 1572872 | tf_op jit(solution)/shard_map/ppermute | solution.py:305
  127.1 2.8 %collective-permute-start.12 = (bf16[8,32,128]{2,1,0:T(8,128)(2,1)S(1)}, bf16[8,32,128]{2,1,0:T(8,128)(2,1)S(1)}, u32[]{:S(2)}, u32[]{:S(2)}) collective-permute-start(bf16[8,32,128]{2,1,0:T(8,128)(2,1)S(1)} %get-tuple-element.52), channel_id=1, source_target_pairs={{0,512},{256,768},{512,0},{768,256},{1,513},{257,769},{513,1},{769... | collective-permute-start | bytes 196616 | tf_op jit(solution)/shard_map/ppermute | solution.py:309
  129.9 3.1 %collective-permute-start.13 = (bf16[8,32,128]{2,1,0:T(8,128)(2,1)S(1)}, bf16[8,32,128]{2,1,0:T(8,128)(2,1)S(1)}, u32[]{:S(2)}, u32[]{:S(2)}) collective-permute-start(bf16[8,32,128]{2,1,0:T(8,128)(2,1)S(1)} %get-tuple-element.53), channel_id=1, source_target_pairs={{0,768},{256,0},{512,256},{768,512},{1,769},{257,1},{513,257},{769... | collective-permute-start | bytes 196616 | tf_op jit(solution)/shard_map/ppermute | solution.py:309
  133.9 2.7 %collective-permute-done.9.refs_1_ = bf16[8,256,128]{2,1,0:T(8,128)(2,1)} collective-permute-done((bf16[8,256,128]{2,1,0:T(8,128)(2,1)}, bf16[8,256,128]{2,1,0:T(8,128)(2,1)}, u32[]{:S(2)}, u32[]{:S(2)}) %collective-permute-start.9) | collective-permute-done | bytes 524320 | tf_op jit(solution)/shard_map/ppermute | solution.py:305
  140.0 3.5 %all-to-all-start.3 = ((bf16[4,576,128]{2,1,0:T(8,128)(2,1)}), bf16[4,576,128]{2,1,0:T(8,128)(2,1)S(1)}, u32[]{:S(2)}, u32[]{:S(2)}) async-start(bf16[4,576,128]{2,1,0:T(8,128)(2,1)} %bitcast.8), calls=%async_computation.3 | async-start | bytes 1179648 | tf_op jit(solution)/shard_map/all_to_all | solution.py:313
  143.5 11.9 %collective-permute-start.14 = (bf16[128,128]{1,0:T(8,128)(2,1)S(1)}, bf16[128,128]{1,0:T(8,128)(2,1)S(1)}, u32[]{:S(2)}, u32[]{:S(2)}) collective-permute-start(bf16[128,128]{1,0:T(8,128)(2,1)S(1)} %get-tuple-element.55), channel_id=1, source_target_pairs={{0,16},{16,0},{1,17},{17,1},{2,18},{18,2},{3,19},{19,3},{4,20},{20... | collective-permute-start | bytes 98312 | tf_op jit(solution)/shard_map/ppermute | solution.py:311
  155.3 3.3 %all-to-all-done.3 = bf16[4,576,128]{2,1,0:T(8,128)(2,1)S(1)} async-done(((bf16[4,576,128]{2,1,0:T(8,128)(2,1)}), bf16[4,576,128]{2,1,0:T(8,128)(2,1)S(1)}, u32[]{:S(2)}, u32[]{:S(2)}) %all-to-all-start.3) | async-done | bytes 589856 | tf_op jit(solution)/shard_map/all_to_all | solution.py:313
  158.7 3.0 %collective-permute-start.15 = (bf16[288,128]{1,0:T(8,128)(2,1)S(1)}, bf16[288,128]{1,0:T(8,128)(2,1)S(1)}, u32[]{:S(2)}, u32[]{:S(2)}) collective-permute-start(bf16[288,128]{1,0:T(8,128)(2,1)S(1)} %fusion), channel_id=1, source_target_pairs={{0,128},{128,0},{1,129},{129,1},{2,130},{130,2},{3,131},{131,3},{4... | collective-permute-start | bytes 221192 | tf_op jit(solution)/shard_map/ppermute | solution.py:318
  163.5 6.6 %collective-permute-done.15.there_ref = bf16[288,128]{1,0:T(8,128)(2,1)S(1)} collective-permute-done((bf16[288,128]{1,0:T(8,128)(2,1)S(1)}, bf16[288,128]{1,0:T(8,128)(2,1)S(1)}, u32[]{:S(2)}, u32[]{:S(2)}) %collective-permute-start.15) | collective-permute-done | bytes 73760 | tf_op jit(solution)/shard_map/ppermute | solution.py:318
  (72 shorter events, 38.5 us)
Async XLA Ops:
  0.6 33.4 %copy-start = (bf16[128,4096]{1,0:T(8,128)(2,1)S(1)}, bf16[128,4096]{1,0:T(8,128)(2,1)}, u32[]{:S(2)}) copy-start(bf16[128,4096]{1,0:T(8,128)(2,1)} %param.15) | copy-start | bytes 3145732
  3.1 20.8 %copy-start.10 = (bf16[4096,32]{0,1:T(8,128)(2,1)S(1)}, bf16[4096,32]{0,1:T(8,128)(2,1)}, u32[]{:S(2)}) copy-start(bf16[4096,32]{0,1:T(8,128)(2,1)} %param.14) | copy-start | bytes 786436
  3.1 30.9 %copy-start.2 = (bf16[128,4096]{1,0:T(8,128)(2,1)S(1)}, bf16[128,4096]{1,0:T(8,128)(2,1)}, u32[]{:S(2)}) copy-start(bf16[128,4096]{1,0:T(8,128)(2,1)} %go_ref.1) | copy-start | bytes 3145732
  5.0 36.1 %all-to-all-start = ((bf16[32,32,128]{2,1,0:T(8,128)(2,1)}), bf16[32,32,128]{2,1,0:T(8,128)(2,1)S(1)}, u32[]{:S(2)}, u32[]{:S(2)}) async-start(bf16[32,32,128]{2,1,0:T(8,128)(2,1)} %shard_map.138), calls=%async_computation | async-start | bytes 524288 | tf_op jit(solution)/shard_map/all_to_all | solution.py:252
  23.9 12.6 %collective-permute-start = (bf16[32,4096]{1,0:T(8,128)(2,1)S(1)}, bf16[32,4096]{1,0:T(8,128)(2,1)S(1)}, u32[]{:S(2)}, u32[]{:S(2)}) collective-permute-start(bf16[32,4096]{1,0:T(8,128)(2,1)S(1)} %bitcast.14), channel_id=1, source_target_pairs={{0,2},{2,0},{4,6},{6,4},{1,3},{3,1},{5,7},{7,5},{8,10},{10,8},{12,... | collective-permute-start | bytes 786440 | tf_op jit(solution)/shard_map/ppermute | solution.py:255
  27.4 26.5 %collective-permute-start.2 = (bf16[32,4096]{1,0:T(8,128)(2,1)S(1)}, bf16[32,4096]{1,0:T(8,128)(2,1)S(1)}, u32[]{:S(2)}, u32[]{:S(2)}) collective-permute-start(bf16[32,4096]{1,0:T(8,128)(2,1)S(1)} %bitcast.15), channel_id=1, source_target_pairs={{0,4},{2,6},{4,0},{6,2},{1,5},{3,7},{5,1},{7,3},{8,12},{10,14},{12... | collective-permute-start | bytes 786440 | tf_op jit(solution)/shard_map/ppermute | solution.py:255
  31.9 22.0 %collective-permute-start.3 = (bf16[32,4096]{1,0:T(8,128)(2,1)S(1)}, bf16[32,4096]{1,0:T(8,128)(2,1)S(1)}, u32[]{:S(2)}, u32[]{:S(2)}) collective-permute-start(bf16[32,4096]{1,0:T(8,128)(2,1)S(1)} %bitcast.16), channel_id=1, source_target_pairs={{0,6},{2,4},{4,2},{6,0},{1,7},{3,5},{5,3},{7,1},{8,14},{10,12},{12... | collective-permute-start | bytes 786440 | tf_op jit(solution)/shard_map/ppermute | solution.py:255
  42.0 14.5 %collective-permute-start.1 = (bf16[128,128]{1,0:T(8,128)(2,1)S(1)}, bf16[128,128]{1,0:T(8,128)(2,1)S(1)}, u32[]{:S(2)}, u32[]{:S(2)}) collective-permute-start(bf16[128,128]{1,0:T(8,128)(2,1)S(1)} %shard_map.139.own_ref), channel_id=1, source_target_pairs={{0,16},{16,0},{1,17},{17,1},{2,18},{18,2},{3,19},{19,3},{4,20},{20... | collective-permute-start | bytes 98312 | tf_op jit(solution)/shard_map/ppermute | solution.py:262
  57.9 22.4 %all-to-all-start.1 = ((bf16[8,2,128,128]{3,2,1,0:T(8,128)(2,1)}), bf16[8,2,128,128]{3,2,1,0:T(8,128)(2,1)S(1)}, u32[]{:S(2)}, u32[]{:S(2)}) async-start(bf16[8,2,128,128]{3,2,1,0:T(8,128)(2,1)} %shard_map.140.refs_4_), calls=%async_computation.1 | async-start | bytes 1048576 | tf_op jit(solution)/shard_map/all_to_all | solution.py:264
  66.1 16.1 %collective-permute-start.5 = (bf16[4,32,4096]{2,1,0:T(8,128)(2,1)}, bf16[4,32,4096]{2,1,0:T(8,128)(2,1)}, u32[]{:S(2)}, u32[]{:S(2)}) collective-permute-start(bf16[4,32,4096]{2,1,0:T(8,128)(2,1)} %shard_map.141.here_ref), channel_id=1, source_target_pairs={{0,1},{1,0},{2,3},{3,2},{4,5},{5,4},{6,7},{7,6},{8,9},{9,8},{10,11... | collective-permute-start | bytes 3145736 | tf_op jit(solution)/shard_map/ppermute | solution.py:267
  80.3 3.8 %collective-permute-start.4 = (bf16[8,2,128,128]{3,2,1,0:T(8,128)(2,1)S(1)}, bf16[8,2,128,128]{3,2,1,0:T(8,128)(2,1)S(1)}, u32[]{:S(2)}, u32[]{:S(2)}) collective-permute-start(bf16[8,2,128,128]{3,2,1,0:T(8,128)(2,1)S(1)} %all-to-all-done.1.refs_3_), channel_id=1, source_target_pairs={{0,1},{1,0},{2,3},{3,2},{4,5},{5,4},{6,7},{7,6},{8,9},{9,8},{10,11... | collective-permute-start | bytes 1572872 | tf_op jit(solution)/shard_map/ppermute | solution.py:265
  89.2 4.4 %collective-permute-start.6 = (bf16[8,288,128]{2,1,0:T(8,128)(2,1)S(1)}, bf16[8,288,128]{2,1,0:T(8,128)(2,1)S(1)}, u32[]{:S(2)}, u32[]{:S(2)}) collective-permute-start(bf16[8,288,128]{2,1,0:T(8,128)(2,1)S(1)} %get-tuple-element.40), channel_id=1, source_target_pairs={{0,1},{1,0},{2,3},{3,2},{4,5},{5,4},{6,7},{7,6},{8,9},{9,8},{10,11... | collective-permute-start | bytes 1769480 | tf_op jit(solution)/shard_map/ppermute | solution.py:294
  94.7 29.4 %all-to-all-start.2 = ((bf16[8,288,128]{2,1,0:T(8,128)(2,1)}), bf16[8,288,128]{2,1,0:T(8,128)(2,1)S(1)}, u32[]{:S(2)}, u32[]{:S(2)}) async-start(bf16[8,288,128]{2,1,0:T(8,128)(2,1)} %shard_map.146), calls=%async_computation.2 | async-start | bytes 1179648 | tf_op jit(solution)/shard_map/all_to_all | solution.py:301
  98.3 25.9 %copy-start.9 = (bf16[32,128,128]{2,1,0:T(8,128)(2,1)S(1)}, bf16[32,128,128]{2,1,0:T(8,128)(2,1)}, u32[]{:S(2)}) copy-start(bf16[32,128,128]{2,1,0:T(8,128)(2,1)} %copy-done.8) | copy-start | bytes 3145732
  98.3 10.4 %collective-permute-start.7 = (bf16[4,256,128]{2,1,0:T(8,128)(2,1)S(1)}, bf16[4,256,128]{2,1,0:T(8,128)(2,1)S(1)}, u32[]{:S(2)}, u32[]{:S(2)}) collective-permute-start(bf16[4,256,128]{2,1,0:T(8,128)(2,1)S(1)} %get-tuple-element.46), channel_id=1, source_target_pairs={{0,256},{256,512},{512,768},{768,0},{1,257},{257,513},{513,769},{7... | collective-permute-start | bytes 786440 | tf_op jit(solution)/shard_map/ppermute | solution.py:302
  102.7 11.2 %collective-permute-start.8 = (bf16[4,256,128]{2,1,0:T(8,128)(2,1)S(1)}, bf16[4,256,128]{2,1,0:T(8,128)(2,1)S(1)}, u32[]{:S(2)}, u32[]{:S(2)}) collective-permute-start(bf16[4,256,128]{2,1,0:T(8,128)(2,1)S(1)} %get-tuple-element.47), channel_id=1, source_target_pairs={{0,768},{256,0},{512,256},{768,512},{1,769},{257,1},{513,257},{769... | collective-permute-start | bytes 786440 | tf_op jit(solution)/shard_map/ppermute | solution.py:303
  117.1 16.8 %collective-permute-start.10 = (bf16[8,256,128]{2,1,0:T(8,128)(2,1)}, bf16[8,256,128]{2,1,0:T(8,128)(2,1)S(1)}, u32[]{:S(2)}, u32[]{:S(2)}) collective-permute-start(bf16[8,256,128]{2,1,0:T(8,128)(2,1)} %get-tuple-element.49), channel_id=1, source_target_pairs={{0,768},{256,0},{512,256},{768,512},{1,769},{257,1},{513,257},{769... | collective-permute-start | bytes 1572872 | tf_op jit(solution)/shard_map/ppermute | solution.py:305
  119.0 17.7 %collective-permute-start.9 = (bf16[8,256,128]{2,1,0:T(8,128)(2,1)}, bf16[8,256,128]{2,1,0:T(8,128)(2,1)}, u32[]{:S(2)}, u32[]{:S(2)}) collective-permute-start(bf16[8,256,128]{2,1,0:T(8,128)(2,1)} %get-tuple-element.48), channel_id=1, source_target_pairs={{0,256},{256,512},{512,768},{768,0},{1,257},{257,513},{513,769},{7... | collective-permute-start | bytes 1572872 | tf_op jit(solution)/shard_map/ppermute | solution.py:305
  125.2 12.0 %collective-permute-start.11 = (bf16[8,32,128]{2,1,0:T(8,128)(2,1)S(1)}, bf16[8,32,128]{2,1,0:T(8,128)(2,1)S(1)}, u32[]{:S(2)}, u32[]{:S(2)}) collective-permute-start(bf16[8,32,128]{2,1,0:T(8,128)(2,1)S(1)} %get-tuple-element.51), channel_id=1, source_target_pairs={{0,256},{256,512},{512,768},{768,0},{1,257},{257,513},{513,769},{7... | collective-permute-start | bytes 196616 | tf_op jit(solution)/shard_map/ppermute | solution.py:309
  127.1 10.1 %collective-permute-start.12 = (bf16[8,32,128]{2,1,0:T(8,128)(2,1)S(1)}, bf16[8,32,128]{2,1,0:T(8,128)(2,1)S(1)}, u32[]{:S(2)}, u32[]{:S(2)}) collective-permute-start(bf16[8,32,128]{2,1,0:T(8,128)(2,1)S(1)} %get-tuple-element.52), channel_id=1, source_target_pairs={{0,512},{256,768},{512,0},{768,256},{1,513},{257,769},{513,1},{769... | collective-permute-start | bytes 196616 | tf_op jit(solution)/shard_map/ppermute | solution.py:309
  129.9 8.0 %collective-permute-start.13 = (bf16[8,32,128]{2,1,0:T(8,128)(2,1)S(1)}, bf16[8,32,128]{2,1,0:T(8,128)(2,1)S(1)}, u32[]{:S(2)}, u32[]{:S(2)}) collective-permute-start(bf16[8,32,128]{2,1,0:T(8,128)(2,1)S(1)} %get-tuple-element.53), channel_id=1, source_target_pairs={{0,768},{256,0},{512,256},{768,512},{1,769},{257,1},{513,257},{769... | collective-permute-start | bytes 196616 | tf_op jit(solution)/shard_map/ppermute | solution.py:309
  140.0 18.6 %all-to-all-start.3 = ((bf16[4,576,128]{2,1,0:T(8,128)(2,1)}), bf16[4,576,128]{2,1,0:T(8,128)(2,1)S(1)}, u32[]{:S(2)}, u32[]{:S(2)}) async-start(bf16[4,576,128]{2,1,0:T(8,128)(2,1)} %bitcast.8), calls=%async_computation.3 | async-start | bytes 1179648 | tf_op jit(solution)/shard_map/all_to_all | solution.py:313
  143.5 19.5 %collective-permute-start.14 = (bf16[128,128]{1,0:T(8,128)(2,1)S(1)}, bf16[128,128]{1,0:T(8,128)(2,1)S(1)}, u32[]{:S(2)}, u32[]{:S(2)}) collective-permute-start(bf16[128,128]{1,0:T(8,128)(2,1)S(1)} %get-tuple-element.55), channel_id=1, source_target_pairs={{0,16},{16,0},{1,17},{17,1},{2,18},{18,2},{3,19},{19,3},{4,20},{20... | collective-permute-start | bytes 98312 | tf_op jit(solution)/shard_map/ppermute | solution.py:311
  158.7 11.4 %collective-permute-start.15 = (bf16[288,128]{1,0:T(8,128)(2,1)S(1)}, bf16[288,128]{1,0:T(8,128)(2,1)S(1)}, u32[]{:S(2)}, u32[]{:S(2)}) collective-permute-start(bf16[288,128]{1,0:T(8,128)(2,1)S(1)} %fusion), channel_id=1, source_target_pairs={{0,128},{128,0},{1,129},{129,1},{2,130},{130,2},{3,131},{131,3},{4... | collective-permute-start | bytes 221192 | tf_op jit(solution)/shard_map/ppermute | solution.py:318
  (14 other events, 118.2 us)

commit v7 on v6

--- a/solution.py
+++ b/solution.py
@@ -41,8 +41,8 @@
 
 
 def incoming(ids_ref, dest_ref):
-    groups, seq_total = dest_ref.shape
-    senders = [lax.rem(ids_ref[G] + groups - dest_ref[0, j], groups) for j in range(seq_total)]
+    seq_total, groups = dest_ref.shape
+    senders = [lax.rem(ids_ref[G] + groups - dest_ref[j, 0], groups) for j in range(seq_total)]
     ranks = []
     for j in range(seq_total):
         rank = jnp.int32(0)
@@ -52,19 +52,27 @@
     return senders, ranks
 
 
-def outgoing_kernel(ids_ref, len_ref, dest_ref, x_ref, out_ref):
-    groups, seq_total = dest_ref.shape
+def outgoing_kernel(ids_ref, len_any, dest_any, x_any, out_ref, len_ref, dest_ref, x_ref, sem):
+    copies = [
+        pltpu.make_async_copy(source, target, sem.at[n])
+        for n, (source, target) in enumerate(((len_any, len_ref), (dest_any, dest_ref), (x_any, x_ref)))
+    ]
+    for copy in copies:
+        copy.start()
+    seq_total, groups = dest_ref.shape
     longest = out_ref.shape[1]
     tokens = x_ref.shape[0]
     group = ids_ref[G]
     out_ref[...] = jnp.zeros_like(out_ref)
     place = lax.broadcasted_iota(jnp.int32, (longest, tokens), 0)
     token = lax.broadcasted_iota(jnp.int32, (longest, tokens), 1)
+    for copy in copies:
+        copy.wait()
     start = jnp.int32(0)
     for j in range(seq_total):
-        size = len_ref[group, j]
+        size = len_ref[j, group]
         chosen = jnp.where((token == place + start) & (place < size), 1.0, 0.0).astype(BF16)
-        to = lax.rem(group + dest_ref[0, j], groups)
+        to = lax.rem(group + dest_ref[j, 0], groups)
         out_ref[to] = dot(chosen, x_ref[...], ((1,), (0,))).astype(BF16)
         start = start + size
 
@@ -137,7 +145,7 @@
         first = ranks[j] * longest
         here = (qi >= first) & (qi < first + longest)
         starts = jnp.where(here, first, starts)
-        ends = jnp.where(here, first + len_ref[senders[j], j], ends)
+        ends = jnp.where(here, first + len_ref[j, senders[j]], ends)
     allowed = (ki >= starts) & (ki <= qi) & (ki < ends)
     scores = jnp.where(allowed, dot(q, k, ((1,), (0,))) * inv_scale, -1e30)
     highest = jnp.max(scores, axis=1, keepdims=True)
@@ -206,11 +214,23 @@
                 k_refs[s][row_of(yl, c)] = dot(kvg, x_ref[x * 8 + yl * 2 + c], ((1,), (0,))).astype(BF16)
 
 
-def fold_kernel(g1_ref, g3_ref, low_ref, high_ref, h1_ref, h3_ref):
-    h1_ref[0:4] = (g1_ref[0:4].astype(F32) + low_ref[...].astype(F32)).astype(BF16)
-    h1_ref[4:8] = g1_ref[4:8]
-    h3_ref[0:4] = g3_ref[0:4]
-    h3_ref[4:8] = (g3_ref[4:8].astype(F32) + high_ref[...].astype(F32)).astype(BF16)
+def fold_kernel(g1_ref, g3_ref, low_ref, high_ref, h1_ref, h3_ref, one_ref, three_ref, sem):
+    loads = [
+        pltpu.make_async_copy(g1_ref.at[0:4], one_ref, sem.at[0]),
+        pltpu.make_async_copy(g3_ref.at[4:8], three_ref, sem.at[1]),
+    ]
+    rest = [
+        pltpu.make_async_copy(g1_ref.at[4:8], h1_ref.at[4:8], sem.at[2]),
+        pltpu.make_async_copy(g3_ref.at[0:4], h3_ref.at[0:4], sem.at[3]),
+    ]
+    for copy in loads + rest:
+        copy.start()
+    loads[0].wait()
+    h1_ref[0:4] = (one_ref[...].astype(F32) + low_ref[...].astype(F32)).astype(BF16)
+    loads[1].wait()
+    h3_ref[4:8] = (three_ref[...].astype(F32) + high_ref[...].astype(F32)).astype(BF16)
+    for copy in rest:
+        copy.wait()
 
 
 def sum_kernel(*refs):
@@ -229,26 +249,35 @@
 
 def body(x_source, grad_out, w_query, w_kv, w_out, lengths, dest):
     groups, seq_total = dest.shape
+    lengths, dest = lengths.T, dest.T
     rows = grad_out.shape[0]
     longest = rows // seq_total
     vmem = pl.BlockSpec(memory_space=pltpu.VMEM)
     smem = pl.BlockSpec(memory_space=pltpu.SMEM)
     anyw = pl.BlockSpec(memory_space=pl.ANY)
-    params = pltpu.CompilerParams(vmem_limit_bytes=32 * 1024 * 1024)
     shape = jax.ShapeDtypeStruct
     own_x, own_c, own_yl = lax.axis_index("x"), lax.axis_index("c"), lax.axis_index("yl")
     own_zh, own_zb = lax.axis_index("zh"), lax.axis_index("zb")
     ids = jnp.stack([lax.axis_index(DP), own_x, own_c, own_yl, own_zh, lax.axis_index("yh"), own_zb]).astype(jnp.int32)
 
-    def call(kernel, ins, outs, out_shape, micros=1):
+    def call(kernel, ins, outs, out_shape, micros=1, scratch=(), mib=32):
+        params = pltpu.CompilerParams(vmem_limit_bytes=mib * 1024 * 1024)
         cost = pl.CostEstimate(flops=micros * 10**9, bytes_accessed=micros * 3_600_000, transcendentals=0)
         return pl.pallas_call(
-            kernel, out_shape=out_shape, in_specs=ins, out_specs=outs, compiler_params=params, cost_estimate=cost
+            kernel, out_shape=out_shape, in_specs=ins, out_specs=outs, compiler_params=params, cost_estimate=cost,
+            scratch_shapes=scratch,
         )
 
-    outgoing = call(outgoing_kernel, [smem] * 3 + [vmem], vmem, shape((groups, longest, 128), BF16))(
-        ids, lengths, dest, x_source
-    )
+    outgoing = call(
+        outgoing_kernel, [smem] + [anyw] * 3, vmem, shape((groups, longest, 128), BF16),
+        scratch=[
+            pltpu.SMEM(lengths.shape, jnp.int32),
+            pltpu.SMEM(dest.shape, jnp.int32),
+            pltpu.VMEM(x_source.shape, BF16),
+            pltpu.SemaphoreType.DMA((3,)),
+        ],
+        mib=60,
+    )(ids, lengths, dest, x_source)
     received = lax.all_to_all(outgoing, DP, 0, 0, tiled=True)
     w_own = w_kv.T
     across = [[(i, i ^ s) for i in range(4)] for s in range(4)]
@@ -301,7 +330,11 @@
     part = lax.all_to_all(part, YY, 0, 0, tiled=True)
     low = lax.ppermute(low, "x", around[1])
     high = lax.ppermute(high, "x", around[3])
-    h1, h3 = call(fold_kernel, [vmem] * 4, (vmem,) * 2, (full, full))(g1, g3, low, high)
+    h1, h3 = call(
+        fold_kernel, [anyw] * 2 + [vmem] * 2, (vmem,) * 2, (full, full),
+        scratch=[pltpu.VMEM((4, 256, 128), BF16)] * 2 + [pltpu.SemaphoreType.DMA((4,))],
+        mib=60,
+    )(g1, g3, low, high)
     h1, h3 = lax.ppermute(h1, "x", around[1]), lax.ppermute(h3, "x", around[3])
     keep, send, *ks = call(
         collect_kernel, [smem] + [vmem] * 2, (vmem,) * 6, (shape(block, F32), shape(block, BF16)) + (slim,) * 4

time: 174 us -> 174 us (level)
  local copies, waits for them, and re-layouts: 5.42 us -> 3.25 us
    unnamed x38 -> x44, local copies, waits for them, and re-layouts: 5.33 us -> 2.58 us
    pallas_call x2, Pallas kernels: 3 us -> 5.59 us  [the longest x1 3.21 us: body(): call(fold_kernel, [anyw] * 2 + [vmem] * 2, (vmem,) * 2, (full, full), scr...]
where the time goes in v7:
time: 174 us; the launch traced here: 170 us
  starting transfers between devices  97.2 us (56%)
  waiting for transfers between devices  47.5 us (27%)
  Pallas kernels  20.3 us (12%)
  local copies, waits for them, and re-layouts  3.25 us (2%)
    all_to_all x1, starting transfers between devices, body(): received = lax.all_to_all(outgoing, DP, 0, 0, tiled=True)  18.9 us
    all_to_all x1, waiting for transfers between devices, body(): x_mine = lax.all_to_all(spread, YY, 0, 0, tiled=True)  12.2 us
    ppermute x1, starting transfers between devices, body(): x_other = lax.ppermute(x_slice, 'zh', SWAP)  11.9 us
    ppermute x1, starting transfers between devices, body(): lax.ppermute(send, 'zh', SWAP).astype(F32)  11.9 us
    ppermute x3, starting transfers between devices, body(): lax.ppermute(w_own, 'yl', across[s])  10.1 us
    ppermute x3, starting transfers between devices, body(): ks = ks[:1] + [lax.ppermute(ks[s], 'x', around[s]) for s in (1, 2, 3)]  7.78 us
    all_to_all x1, starting transfers between devices, body(): x_mine = lax.all_to_all(spread, YY, 0, 0, tiled=True)  7.1 us
    ppermute x1, waiting for transfers between devices, body(): lax.ppermute(send, 'zb', SWAP)  6.64 us
  transfers between devices with their start and end apart: 20, of which 14 were waited for; matrix products, arithmetic and copies ran while one was open for 1% of the time, Pallas kernels for 4%

profile of v7, /device:TPU:6, one launch (start us, length us, event | category | flops | bytes accessed | tf_op | source)
XLA Modules:
  0.0 170.5 jit_solution(11667035522944666615)
XLA Ops:
  1.3 2.4 %shard_map.138 = bf16[32,32,128]{2,1,0:T(8,128)(2,1)} custom-call(s32[7]{0:T(128)} %stack.31.ids_ref.refs_0_, s32[4,32]{1,0:T(4,128)} %bitcast.19, s32[4,32]{1,0:T(4,128)} %bitcast.16, bf16[64,128]{1,0:T(8,128)(2,1)} %x_any.1), custom_call_target="tpu_custom_call" | custom-call | flops 1000000000 | bytes 3600000 | tf_op jit(solution)/shard_map/pallas_call | solution.py:271
  3.7 18.9 %all-to-all-start = ((bf16[32,32,128]{2,1,0:T(8,128)(2,1)}), bf16[32,32,128]{2,1,0:T(8,128)(2,1)S(1)}, u32[]{:S(2)}, u32[]{:S(2)}) async-start(bf16[32,32,128]{2,1,0:T(8,128)(2,1)} %shard_map.138), calls=%async_computation | async-start | bytes 524288 | tf_op jit(solution)/shard_map/all_to_all | solution.py:281
  22.6 3.5 %collective-permute-start = (bf16[32,4096]{1,0:T(8,128)(2,1)S(1)}, bf16[32,4096]{1,0:T(8,128)(2,1)S(1)}, u32[]{:S(2)}, u32[]{:S(2)}) collective-permute-start(bf16[32,4096]{1,0:T(8,128)(2,1)S(1)} %bitcast.21), channel_id=1, source_target_pairs={{0,2},{2,0},{4,6},{6,4},{1,3},{3,1},{5,7},{7,5},{8,10},{10,8},{12,... | collective-permute-start | bytes 786440 | tf_op jit(solution)/shard_map/ppermute | solution.py:284
  26.1 4.5 %collective-permute-start.2 = (bf16[32,4096]{1,0:T(8,128)(2,1)S(1)}, bf16[32,4096]{1,0:T(8,128)(2,1)S(1)}, u32[]{:S(2)}, u32[]{:S(2)}) collective-permute-start(bf16[32,4096]{1,0:T(8,128)(2,1)S(1)} %bitcast.22), channel_id=1, source_target_pairs={{0,4},{2,6},{4,0},{6,2},{1,5},{3,7},{5,1},{7,3},{8,12},{10,14},{12... | collective-permute-start | bytes 786440 | tf_op jit(solution)/shard_map/ppermute | solution.py:284
  35.2 4.7 %all-to-all-done.x_ref = bf16[32,32,128]{2,1,0:T(8,128)(2,1)S(1)} async-done(((bf16[32,32,128]{2,1,0:T(8,128)(2,1)}), bf16[32,32,128]{2,1,0:T(8,128)(2,1)S(1)}, u32[]{:S(2)}, u32[]{:S(2)}) %all-to-all-start) | async-done | bytes 262176 | tf_op jit(solution)/shard_map/all_to_all | solution.py:281
  40.5 11.9 %collective-permute-start.1 = (bf16[128,128]{1,0:T(8,128)(2,1)S(1)}, bf16[128,128]{1,0:T(8,128)(2,1)S(1)}, u32[]{:S(2)}, u32[]{:S(2)}) collective-permute-start(bf16[128,128]{1,0:T(8,128)(2,1)S(1)} %shard_map.139.own_ref), channel_id=1, source_target_pairs={{0,16},{16,0},{1,17},{17,1},{2,18},{18,2},{3,19},{19,3},{4,20},{20... | collective-permute-start | bytes 98312 | tf_op jit(solution)/shard_map/ppermute | solution.py:291
  52.4 2.6 %collective-permute-done.1.other_ref = bf16[128,128]{1,0:T(8,128)(2,1)S(1)} collective-permute-done((bf16[128,128]{1,0:T(8,128)(2,1)S(1)}, bf16[128,128]{1,0:T(8,128)(2,1)S(1)}, u32[]{:S(2)}, u32[]{:S(2)}) %collective-permute-start.1) | collective-permute-done | bytes 32800 | tf_op jit(solution)/shard_map/ppermute | solution.py:291
  56.5 7.1 %all-to-all-start.1 = ((bf16[8,2,128,128]{3,2,1,0:T(8,128)(2,1)}), bf16[8,2,128,128]{3,2,1,0:T(8,128)(2,1)S(1)}, u32[]{:S(2)}, u32[]{:S(2)}) async-start(bf16[8,2,128,128]{3,2,1,0:T(8,128)(2,1)} %shard_map.140.refs_4_), calls=%async_computation.1 | async-start | bytes 1048576 | tf_op jit(solution)/shard_map/all_to_all | solution.py:293
  66.7 12.2 %all-to-all-done.1.refs_3_ = bf16[8,2,128,128]{3,2,1,0:T(8,128)(2,1)S(1)} async-done(((bf16[8,2,128,128]{3,2,1,0:T(8,128)(2,1)}), bf16[8,2,128,128]{3,2,1,0:T(8,128)(2,1)S(1)}, u32[]{:S(2)}, u32[]{:S(2)}) %all-to-all-start.1) | async-done | bytes 524320 | tf_op jit(solution)/shard_map/all_to_all | solution.py:293
  82.8 2.5 %shard_map.143 = (bf16[128,128]{1,0:T(8,128)(2,1)S(1)}, bf16[128,128]{1,0:T(8,128)(2,1)S(1)}, bf16[256,128]{1,0:T(8,128)(2,1)S(1)}, bf16[128,256]{1,0:T(8,128)(2,1)S(1)}, bf16[32,128,128]{2,1,0:T(8,128)(2,1)S(1)}) custom-call(s32[7]{0:T(128)S(1)} %copy-done.8, s32[4,32]{1,0:T(4,128)S(1)} %bitcast.20, s32[4,32]{1,0:T(4,128)S(1)} %bitcast.18, ...), custom_call_target="tpu_custom_call" | custom-call | flops 1000000000 | bytes 3600000 | tf_op jit(solution)/shard_map/pallas_call | solution.py:302
  92.7 3.5 %all-to-all-start.2 = ((bf16[8,288,128]{2,1,0:T(8,128)(2,1)}), bf16[8,288,128]{2,1,0:T(8,128)(2,1)S(1)}, u32[]{:S(2)}, u32[]{:S(2)}) async-start(bf16[8,288,128]{2,1,0:T(8,128)(2,1)} %shard_map.146), calls=%async_computation.2 | async-start | bytes 1179648 | tf_op jit(solution)/shard_map/all_to_all | solution.py:330
  96.3 4.5 %collective-permute-start.7 = (bf16[4,256,128]{2,1,0:T(8,128)(2,1)S(1)}, bf16[4,256,128]{2,1,0:T(8,128)(2,1)S(1)}, u32[]{:S(2)}, u32[]{:S(2)}) collective-permute-start(bf16[4,256,128]{2,1,0:T(8,128)(2,1)S(1)} %get-tuple-element.46), channel_id=1, source_target_pairs={{0,256},{256,512},{512,768},{768,0},{1,257},{257,513},{513,769},{7... | collective-permute-start | bytes 786440 | tf_op jit(solution)/shard_map/ppermute | solution.py:331
  102.7 4.2 %collective-permute-done.7.low_ref = bf16[4,256,128]{2,1,0:T(8,128)(2,1)S(1)} collective-permute-done((bf16[4,256,128]{2,1,0:T(8,128)(2,1)S(1)}, bf16[4,256,128]{2,1,0:T(8,128)(2,1)S(1)}, u32[]{:S(2)}, u32[]{:S(2)}) %collective-permute-start.7) | collective-permute-done | bytes 262176 | tf_op jit(solution)/shard_map/ppermute | solution.py:331
  106.9 5.2 %collective-permute-done.8.high_ref = bf16[4,256,128]{2,1,0:T(8,128)(2,1)S(1)} collective-permute-done((bf16[4,256,128]{2,1,0:T(8,128)(2,1)S(1)}, bf16[4,256,128]{2,1,0:T(8,128)(2,1)S(1)}, u32[]{:S(2)}, u32[]{:S(2)}) %collective-permute-start.8) | collective-permute-done | bytes 262176 | tf_op jit(solution)/shard_map/ppermute | solution.py:332
  112.9 3.2 %shard_map.148 = (bf16[8,256,128]{2,1,0:T(8,128)(2,1)}, bf16[8,256,128]{2,1,0:T(8,128)(2,1)}) custom-call(bf16[8,256,128]{2,1,0:T(8,128)(2,1)} %copy-done.18, bf16[8,256,128]{2,1,0:T(8,128)(2,1)} %copy-done.19, bf16[4,256,128]{2,1,0:T(8,128)(2,1)} %copy-done.20, bf16[4,256,128]{2,1,0:T(8,128)(2,1)} %copy-done.21), custom_call_target="tpu_custom_call" | custom-call | flops 1000000000 | bytes 3600000 | tf_op jit(solution)/shard_map/pallas_call | solution.py:333
  118.0 5.1 %collective-permute-start.9 = (bf16[8,256,128]{2,1,0:T(8,128)(2,1)}, bf16[8,256,128]{2,1,0:T(8,128)(2,1)}, u32[]{:S(2)}, u32[]{:S(2)}) collective-permute-start(bf16[8,256,128]{2,1,0:T(8,128)(2,1)} %get-tuple-element.48), channel_id=1, source_target_pairs={{0,256},{256,512},{512,768},{768,0},{1,257},{257,513},{513,769},{7... | collective-permute-start | bytes 1572872 | tf_op jit(solution)/shard_map/ppermute | solution.py:338
  126.1 2.8 %collective-permute-start.12 = (bf16[8,32,128]{2,1,0:T(8,128)(2,1)S(1)}, bf16[8,32,128]{2,1,0:T(8,128)(2,1)S(1)}, u32[]{:S(2)}, u32[]{:S(2)}) collective-permute-start(bf16[8,32,128]{2,1,0:T(8,128)(2,1)S(1)} %get-tuple-element.52), channel_id=1, source_target_pairs={{0,512},{256,768},{512,0},{768,256},{1,513},{257,769},{513,1},{769... | collective-permute-start | bytes 196616 | tf_op jit(solution)/shard_map/ppermute | solution.py:342
  128.9 3.1 %collective-permute-start.13 = (bf16[8,32,128]{2,1,0:T(8,128)(2,1)S(1)}, bf16[8,32,128]{2,1,0:T(8,128)(2,1)S(1)}, u32[]{:S(2)}, u32[]{:S(2)}) collective-permute-start(bf16[8,32,128]{2,1,0:T(8,128)(2,1)S(1)} %get-tuple-element.53), channel_id=1, source_target_pairs={{0,768},{256,0},{512,256},{768,512},{1,769},{257,1},{513,257},{769... | collective-permute-start | bytes 196616 | tf_op jit(solution)/shard_map/ppermute | solution.py:342
  133.2 2.7 %collective-permute-done.9.refs_1_ = bf16[8,256,128]{2,1,0:T(8,128)(2,1)} collective-permute-done((bf16[8,256,128]{2,1,0:T(8,128)(2,1)}, bf16[8,256,128]{2,1,0:T(8,128)(2,1)}, u32[]{:S(2)}, u32[]{:S(2)}) %collective-permute-start.9) | collective-permute-done | bytes 524320 | tf_op jit(solution)/shard_map/ppermute | solution.py:338
  139.0 3.5 %all-to-all-start.3 = ((bf16[4,576,128]{2,1,0:T(8,128)(2,1)}), bf16[4,576,128]{2,1,0:T(8,128)(2,1)S(1)}, u32[]{:S(2)}, u32[]{:S(2)}) async-start(bf16[4,576,128]{2,1,0:T(8,128)(2,1)} %bitcast.10), calls=%async_computation.3 | async-start | bytes 1179648 | tf_op jit(solution)/shard_map/all_to_all | solution.py:346
  142.5 11.9 %collective-permute-start.14 = (bf16[128,128]{1,0:T(8,128)(2,1)S(1)}, bf16[128,128]{1,0:T(8,128)(2,1)S(1)}, u32[]{:S(2)}, u32[]{:S(2)}) collective-permute-start(bf16[128,128]{1,0:T(8,128)(2,1)S(1)} %get-tuple-element.55), channel_id=1, source_target_pairs={{0,16},{16,0},{1,17},{17,1},{2,18},{18,2},{3,19},{19,3},{4,20},{20... | collective-permute-start | bytes 98312 | tf_op jit(solution)/shard_map/ppermute | solution.py:344
  154.3 3.4 %all-to-all-done.3 = bf16[4,576,128]{2,1,0:T(8,128)(2,1)S(1)} async-done(((bf16[4,576,128]{2,1,0:T(8,128)(2,1)}), bf16[4,576,128]{2,1,0:T(8,128)(2,1)S(1)}, u32[]{:S(2)}, u32[]{:S(2)}) %all-to-all-start.3) | async-done | bytes 589856 | tf_op jit(solution)/shard_map/all_to_all | solution.py:346
  157.8 3.0 %collective-permute-start.15 = (bf16[288,128]{1,0:T(8,128)(2,1)S(1)}, bf16[288,128]{1,0:T(8,128)(2,1)S(1)}, u32[]{:S(2)}, u32[]{:S(2)}) collective-permute-start(bf16[288,128]{1,0:T(8,128)(2,1)S(1)} %fusion), channel_id=1, source_target_pairs={{0,128},{128,0},{1,129},{129,1},{2,130},{130,2},{3,131},{131,3},{4... | collective-permute-start | bytes 221192 | tf_op jit(solution)/shard_map/ppermute | solution.py:351
  162.6 6.6 %collective-permute-done.15.there_ref = bf16[288,128]{1,0:T(8,128)(2,1)S(1)} collective-permute-done((bf16[288,128]{1,0:T(8,128)(2,1)S(1)}, bf16[288,128]{1,0:T(8,128)(2,1)S(1)}, u32[]{:S(2)}, u32[]{:S(2)}) %collective-permute-start.15) | collective-permute-done | bytes 73760 | tf_op jit(solution)/shard_map/ppermute | solution.py:351
  (78 shorter events, 36.4 us)
Async XLA Ops:
  0.6 32.1 %copy-start = (bf16[128,4096]{1,0:T(8,128)(2,1)S(1)}, bf16[128,4096]{1,0:T(8,128)(2,1)}, u32[]{:S(2)}) copy-start(bf16[128,4096]{1,0:T(8,128)(2,1)} %param.15) | copy-start | bytes 3145732
  1.3 31.4 %copy-start.1 = (bf16[128,4096]{1,0:T(8,128)(2,1)S(1)}, bf16[128,4096]{1,0:T(8,128)(2,1)}, u32[]{:S(2)}) copy-start(bf16[128,4096]{1,0:T(8,128)(2,1)} %go_ref.1) | copy-start | bytes 3145732
  3.7 36.2 %copy-start.8 = (s32[7]{0:T(128)S(1)}, s32[7]{0:T(128)}, u32[]{:S(2)}) copy-start(s32[7]{0:T(128)} %stack.31.ids_ref.refs_0_) | copy-start | bytes 88
  3.7 36.2 %copy-start.9 = (s32[32,4]{0,1:T(4,128)S(1)}, s32[32,4]{0,1:T(4,128)}, u32[]{:S(2)}) copy-start(s32[32,4]{0,1:T(4,128)} %param.17) | copy-start | bytes 1540
  3.7 36.2 %all-to-all-start = ((bf16[32,32,128]{2,1,0:T(8,128)(2,1)}), bf16[32,32,128]{2,1,0:T(8,128)(2,1)S(1)}, u32[]{:S(2)}, u32[]{:S(2)}) async-start(bf16[32,32,128]{2,1,0:T(8,128)(2,1)} %shard_map.138), calls=%async_computation | async-start | bytes 524288 | tf_op jit(solution)/shard_map/all_to_all | solution.py:281
  22.6 12.6 %collective-permute-start = (bf16[32,4096]{1,0:T(8,128)(2,1)S(1)}, bf16[32,4096]{1,0:T(8,128)(2,1)S(1)}, u32[]{:S(2)}, u32[]{:S(2)}) collective-permute-start(bf16[32,4096]{1,0:T(8,128)(2,1)S(1)} %bitcast.21), channel_id=1, source_target_pairs={{0,2},{2,0},{4,6},{6,4},{1,3},{3,1},{5,7},{7,5},{8,10},{10,8},{12,... | collective-permute-start | bytes 786440 | tf_op jit(solution)/shard_map/ppermute | solution.py:284
  26.1 26.3 %collective-permute-start.2 = (bf16[32,4096]{1,0:T(8,128)(2,1)S(1)}, bf16[32,4096]{1,0:T(8,128)(2,1)S(1)}, u32[]{:S(2)}, u32[]{:S(2)}) collective-permute-start(bf16[32,4096]{1,0:T(8,128)(2,1)S(1)} %bitcast.22), channel_id=1, source_target_pairs={{0,4},{2,6},{4,0},{6,2},{1,5},{3,7},{5,1},{7,3},{8,12},{10,14},{12... | collective-permute-start | bytes 786440 | tf_op jit(solution)/shard_map/ppermute | solution.py:284
  30.6 21.8 %collective-permute-start.3 = (bf16[32,4096]{1,0:T(8,128)(2,1)S(1)}, bf16[32,4096]{1,0:T(8,128)(2,1)S(1)}, u32[]{:S(2)}, u32[]{:S(2)}) collective-permute-start(bf16[32,4096]{1,0:T(8,128)(2,1)S(1)} %bitcast.23), channel_id=1, source_target_pairs={{0,6},{2,4},{4,2},{6,0},{1,7},{3,5},{5,3},{7,1},{8,14},{10,12},{12... | collective-permute-start | bytes 786440 | tf_op jit(solution)/shard_map/ppermute | solution.py:284
  40.5 14.5 %collective-permute-start.1 = (bf16[128,128]{1,0:T(8,128)(2,1)S(1)}, bf16[128,128]{1,0:T(8,128)(2,1)S(1)}, u32[]{:S(2)}, u32[]{:S(2)}) collective-permute-start(bf16[128,128]{1,0:T(8,128)(2,1)S(1)} %shard_map.139.own_ref), channel_id=1, source_target_pairs={{0,16},{16,0},{1,17},{17,1},{2,18},{18,2},{3,19},{19,3},{4,20},{20... | collective-permute-start | bytes 98312 | tf_op jit(solution)/shard_map/ppermute | solution.py:291
  56.5 22.4 %all-to-all-start.1 = ((bf16[8,2,128,128]{3,2,1,0:T(8,128)(2,1)}), bf16[8,2,128,128]{3,2,1,0:T(8,128)(2,1)S(1)}, u32[]{:S(2)}, u32[]{:S(2)}) async-start(bf16[8,2,128,128]{3,2,1,0:T(8,128)(2,1)} %shard_map.140.refs_4_), calls=%async_computation.1 | async-start | bytes 1048576 | tf_op jit(solution)/shard_map/all_to_all | solution.py:293
  64.7 16.3 %collective-permute-start.5 = (bf16[4,32,4096]{2,1,0:T(8,128)(2,1)S(1)}, bf16[4,32,4096]{2,1,0:T(8,128)(2,1)}, u32[]{:S(2)}, u32[]{:S(2)}) collective-permute-start(bf16[4,32,4096]{2,1,0:T(8,128)(2,1)S(1)} %shard_map.141.here_ref), channel_id=1, source_target_pairs={{0,1},{1,0},{2,3},{3,2},{4,5},{5,4},{6,7},{7,6},{8,9},{9,8},{10,11... | collective-permute-start | bytes 3145736 | tf_op jit(solution)/shard_map/ppermute | solution.py:296
  78.9 3.9 %collective-permute-start.4 = (bf16[8,2,128,128]{3,2,1,0:T(8,128)(2,1)S(1)}, bf16[8,2,128,128]{3,2,1,0:T(8,128)(2,1)S(1)}, u32[]{:S(2)}, u32[]{:S(2)}) collective-permute-start(bf16[8,2,128,128]{3,2,1,0:T(8,128)(2,1)S(1)} %all-to-all-done.1.refs_3_), channel_id=1, source_target_pairs={{0,1},{1,0},{2,3},{3,2},{4,5},{5,4},{6,7},{7,6},{8,9},{9,8},{10,11... | collective-permute-start | bytes 1572872 | tf_op jit(solution)/shard_map/ppermute | solution.py:294
  87.4 4.2 %collective-permute-start.6 = (bf16[8,288,128]{2,1,0:T(8,128)(2,1)S(1)}, bf16[8,288,128]{2,1,0:T(8,128)(2,1)S(1)}, u32[]{:S(2)}, u32[]{:S(2)}) collective-permute-start(bf16[8,288,128]{2,1,0:T(8,128)(2,1)S(1)} %get-tuple-element.40), channel_id=1, source_target_pairs={{0,1},{1,0},{2,3},{3,2},{4,5},{5,4},{6,7},{7,6},{8,9},{9,8},{10,11... | collective-permute-start | bytes 1769480 | tf_op jit(solution)/shard_map/ppermute | solution.py:323
  92.7 30.4 %all-to-all-start.2 = ((bf16[8,288,128]{2,1,0:T(8,128)(2,1)}), bf16[8,288,128]{2,1,0:T(8,128)(2,1)S(1)}, u32[]{:S(2)}, u32[]{:S(2)}) async-start(bf16[8,288,128]{2,1,0:T(8,128)(2,1)} %shard_map.146), calls=%async_computation.2 | async-start | bytes 1179648 | tf_op jit(solution)/shard_map/all_to_all | solution.py:330
  96.3 10.6 %collective-permute-start.7 = (bf16[4,256,128]{2,1,0:T(8,128)(2,1)S(1)}, bf16[4,256,128]{2,1,0:T(8,128)(2,1)S(1)}, u32[]{:S(2)}, u32[]{:S(2)}) collective-permute-start(bf16[4,256,128]{2,1,0:T(8,128)(2,1)S(1)} %get-tuple-element.46), channel_id=1, source_target_pairs={{0,256},{256,512},{512,768},{768,0},{1,257},{257,513},{513,769},{7... | collective-permute-start | bytes 786440 | tf_op jit(solution)/shard_map/ppermute | solution.py:331
  100.8 11.4 %collective-permute-start.8 = (bf16[4,256,128]{2,1,0:T(8,128)(2,1)S(1)}, bf16[4,256,128]{2,1,0:T(8,128)(2,1)S(1)}, u32[]{:S(2)}, u32[]{:S(2)}) collective-permute-start(bf16[4,256,128]{2,1,0:T(8,128)(2,1)S(1)} %get-tuple-element.47), channel_id=1, source_target_pairs={{0,768},{256,0},{512,256},{768,512},{1,769},{257,1},{513,257},{769... | collective-permute-start | bytes 786440 | tf_op jit(solution)/shard_map/ppermute | solution.py:332
  116.1 17.1 %collective-permute-start.10 = (bf16[8,256,128]{2,1,0:T(8,128)(2,1)}, bf16[8,256,128]{2,1,0:T(8,128)(2,1)S(1)}, u32[]{:S(2)}, u32[]{:S(2)}) collective-permute-start(bf16[8,256,128]{2,1,0:T(8,128)(2,1)} %get-tuple-element.49), channel_id=1, source_target_pairs={{0,768},{256,0},{512,256},{768,512},{1,769},{257,1},{513,257},{769... | collective-permute-start | bytes 1572872 | tf_op jit(solution)/shard_map/ppermute | solution.py:338
  118.0 17.9 %collective-permute-start.9 = (bf16[8,256,128]{2,1,0:T(8,128)(2,1)}, bf16[8,256,128]{2,1,0:T(8,128)(2,1)}, u32[]{:S(2)}, u32[]{:S(2)}) collective-permute-start(bf16[8,256,128]{2,1,0:T(8,128)(2,1)} %get-tuple-element.48), channel_id=1, source_target_pairs={{0,256},{256,512},{512,768},{768,0},{1,257},{257,513},{513,769},{7... | collective-permute-start | bytes 1572872 | tf_op jit(solution)/shard_map/ppermute | solution.py:338
  124.2 12.3 %collective-permute-start.11 = (bf16[8,32,128]{2,1,0:T(8,128)(2,1)S(1)}, bf16[8,32,128]{2,1,0:T(8,128)(2,1)S(1)}, u32[]{:S(2)}, u32[]{:S(2)}) collective-permute-start(bf16[8,32,128]{2,1,0:T(8,128)(2,1)S(1)} %get-tuple-element.51), channel_id=1, source_target_pairs={{0,256},{256,512},{512,768},{768,0},{1,257},{257,513},{513,769},{7... | collective-permute-start | bytes 196616 | tf_op jit(solution)/shard_map/ppermute | solution.py:342
  126.1 10.3 %collective-permute-start.12 = (bf16[8,32,128]{2,1,0:T(8,128)(2,1)S(1)}, bf16[8,32,128]{2,1,0:T(8,128)(2,1)S(1)}, u32[]{:S(2)}, u32[]{:S(2)}) collective-permute-start(bf16[8,32,128]{2,1,0:T(8,128)(2,1)S(1)} %get-tuple-element.52), channel_id=1, source_target_pairs={{0,512},{256,768},{512,0},{768,256},{1,513},{257,769},{513,1},{769... | collective-permute-start | bytes 196616 | tf_op jit(solution)/shard_map/ppermute | solution.py:342
  128.9 8.0 %collective-permute-start.13 = (bf16[8,32,128]{2,1,0:T(8,128)(2,1)S(1)}, bf16[8,32,128]{2,1,0:T(8,128)(2,1)S(1)}, u32[]{:S(2)}, u32[]{:S(2)}) collective-permute-start(bf16[8,32,128]{2,1,0:T(8,128)(2,1)S(1)} %get-tuple-element.53), channel_id=1, source_target_pairs={{0,768},{256,0},{512,256},{768,512},{1,769},{257,1},{513,257},{769... | collective-permute-start | bytes 196616 | tf_op jit(solution)/shard_map/ppermute | solution.py:342
  139.0 18.7 %all-to-all-start.3 = ((bf16[4,576,128]{2,1,0:T(8,128)(2,1)}), bf16[4,576,128]{2,1,0:T(8,128)(2,1)S(1)}, u32[]{:S(2)}, u32[]{:S(2)}) async-start(bf16[4,576,128]{2,1,0:T(8,128)(2,1)} %bitcast.10), calls=%async_computation.3 | async-start | bytes 1179648 | tf_op jit(solution)/shard_map/all_to_all | solution.py:346
  142.5 19.5 %collective-permute-start.14 = (bf16[128,128]{1,0:T(8,128)(2,1)S(1)}, bf16[128,128]{1,0:T(8,128)(2,1)S(1)}, u32[]{:S(2)}, u32[]{:S(2)}) collective-permute-start(bf16[128,128]{1,0:T(8,128)(2,1)S(1)} %get-tuple-element.55), channel_id=1, source_target_pairs={{0,16},{16,0},{1,17},{17,1},{2,18},{18,2},{3,19},{19,3},{4,20},{20... | collective-permute-start | bytes 98312 | tf_op jit(solution)/shard_map/ppermute | solution.py:344
  157.8 11.5 %collective-permute-start.15 = (bf16[288,128]{1,0:T(8,128)(2,1)S(1)}, bf16[288,128]{1,0:T(8,128)(2,1)S(1)}, u32[]{:S(2)}, u32[]{:S(2)}) collective-permute-start(bf16[288,128]{1,0:T(8,128)(2,1)S(1)} %fusion), channel_id=1, source_target_pairs={{0,128},{128,0},{1,129},{129,1},{2,130},{130,2},{3,131},{131,3},{4... | collective-permute-start | bytes 221192 | tf_op jit(solution)/shard_map/ppermute | solution.py:351
  (18 other events, 179.0 us)

commit v8 on v7

--- a/solution.py
+++ b/solution.py
@@ -184,15 +184,20 @@
     return ((yl & 1) * 2 + c) * 2 + (yl >> 1)
 
 
-def weight_kernel(ids_ref, x_ref, go_ref, o_ref, gq_ref, g0_ref, g1_ref, g3_ref, low_ref, high_ref):
+def weight_kernel(ids_ref, x_ref, go_ref, o_ref, gq_ref, g0_ref, plus_ref, minus_ref, one_ref, three_ref):
     gq, out = gq_ref[...], o_ref[...]
-    for s, refs in ((2, (low_ref, high_ref)), (1, (g1_ref,)), (3, (g3_ref,)), (0, (g0_ref,))):
+    places = (
+        lambda row: (g0_ref, row),
+        lambda row: (plus_ref, row) if row >= 4 else (one_ref, row),
+        lambda row: (minus_ref, row) if row >= 4 else (plus_ref, row),
+        lambda row: (three_ref, row - 4) if row >= 4 else (minus_ref, row),
+    )
+    for s in (2, 1, 3, 0):
         x = (ids_ref[OX] + s) & 3
         for yl in range(4):
             for c in range(2):
-                row, block = row_of(yl, c), x * 8 + yl * 2 + c
-                ref = refs[row // 4 if s == 2 else 0]
-                row = row % 4 if s == 2 else row
+                ref, row = places[s](row_of(yl, c))
+                block = x * 8 + yl * 2 + c
                 ref[row, 0:128, :] = dot(x_ref[block], gq, ((0,), (0,))).astype(BF16)
                 ref[row, 128:256, :] = dot(out, go_ref[:, aligned(block, 128)], ((0,), (0,))).astype(BF16)
 
@@ -214,29 +219,21 @@
                 k_refs[s][row_of(yl, c)] = dot(kvg, x_ref[x * 8 + yl * 2 + c], ((1,), (0,))).astype(BF16)
 
 
-def fold_kernel(g1_ref, g3_ref, low_ref, high_ref, h1_ref, h3_ref, one_ref, three_ref, sem):
-    loads = [
-        pltpu.make_async_copy(g1_ref.at[0:4], one_ref, sem.at[0]),
-        pltpu.make_async_copy(g3_ref.at[4:8], three_ref, sem.at[1]),
-    ]
-    rest = [
-        pltpu.make_async_copy(g1_ref.at[4:8], h1_ref.at[4:8], sem.at[2]),
-        pltpu.make_async_copy(g3_ref.at[0:4], h3_ref.at[0:4], sem.at[3]),
-    ]
-    for copy in loads + rest:
-        copy.start()
-    loads[0].wait()
-    h1_ref[0:4] = (one_ref[...].astype(F32) + low_ref[...].astype(F32)).astype(BF16)
-    loads[1].wait()
-    h3_ref[4:8] = (three_ref[...].astype(F32) + high_ref[...].astype(F32)).astype(BF16)
-    for copy in rest:
-        copy.wait()
-
-
-def sum_kernel(*refs):
-    send_ref, out_ref, late_ref = refs[7:]
-    out_ref[:, 0:256, :] = sum(ref[...].astype(F32) for ref in refs[:3]).astype(BF16)
-    out_ref[:, 256:288, :] = sum(ref[...].astype(F32) for ref in refs[3:7]).astype(BF16)
+def fold_kernel(one_ref, three_ref, plus_ref, minus_ref, k1_ref, k3_ref, h1_ref, h3_ref):
+    h1_ref[0:4] = (one_ref[...].astype(F32) + plus_ref[0:4].astype(F32)).astype(BF16)
+    h3_ref[0:4] = (three_ref[...].astype(F32) + minus_ref[4:8].astype(F32)).astype(BF16)
+    for row in range(8):
+        h1_ref[4, row * 32 : row * 32 + 32, :] = k1_ref[row]
+        h3_ref[4, row * 32 : row * 32 + 32, :] = k3_ref[row]
+
+
+def sum_kernel(g0_ref, plus_ref, minus_ref, h1_ref, h3_ref, k0_ref, k2_ref, send_ref, out_ref, late_ref):
+    out_ref[0:4, 0:256, :] = sum(v.astype(F32) for v in (g0_ref[0:4], minus_ref[0:4], h1_ref[0:4])).astype(BF16)
+    out_ref[4:8, 0:256, :] = sum(v.astype(F32) for v in (g0_ref[4:8], plus_ref[4:8], h3_ref[0:4])).astype(BF16)
+    for row in range(8):
+        rows = slice(row * 32, row * 32 + 32)
+        parts = (k0_ref[row], k2_ref[row], h1_ref[4, rows, :], h3_ref[4, rows, :])
+        out_ref[row, 256:288, :] = sum(v.astype(F32) for v in parts).astype(BF16)
     late_ref[...] = send_ref[...]
 
 
@@ -322,25 +319,23 @@
     )
     theirs = lax.ppermute(other, "c", SWAP)
     around = [[(i, (i + s) % 4) for i in range(4)] for s in range(4)]
-    g0, g1, g3, low, high = call(
+    g0, plus, minus, one, three = call(
         weight_kernel, [smem] + [vmem] * 4, (vmem,) * 5, (full, full, full, quad, quad)
     )(ids, x_all, grad_out, out, gq)
     part = call(half_kernel, [vmem] * 2 + [anyw], vmem, most)(mine, theirs, g0)
-    low, high, part = lax.optimization_barrier((low, high, part))
+    plus, minus, part = lax.optimization_barrier((plus, minus, part))
     part = lax.all_to_all(part, YY, 0, 0, tiled=True)
-    low = lax.ppermute(low, "x", around[1])
-    high = lax.ppermute(high, "x", around[3])
-    h1, h3 = call(
-        fold_kernel, [anyw] * 2 + [vmem] * 2, (vmem,) * 2, (full, full),
-        scratch=[pltpu.VMEM((4, 256, 128), BF16)] * 2 + [pltpu.SemaphoreType.DMA((4,))],
-        mib=60,
-    )(g1, g3, low, high)
-    h1, h3 = lax.ppermute(h1, "x", around[1]), lax.ppermute(h3, "x", around[3])
-    keep, send, *ks = call(
+    plus, minus = lax.ppermute(plus, "x", around[1]), lax.ppermute(minus, "x", around[3])
+    keep, send, k0, k1, k2, k3 = call(
         collect_kernel, [smem] + [vmem] * 2, (vmem,) * 6, (shape(block, F32), shape(block, BF16)) + (slim,) * 4
     )(ids, part, x_all)
-    ks = ks[:1] + [lax.ppermute(ks[s], "x", around[s]) for s in (1, 2, 3)]
-    total, send = call(sum_kernel, [vmem] * 8, (vmem,) * 2, (most, shape(block, BF16)))(g0, h1, h3, *ks, send)
+    five = shape((5, 256, 128), BF16)
+    h1, h3 = call(fold_kernel, [vmem] * 6, (vmem,) * 2, (five, five))(one, three, plus, minus, k1, k3)
+    h1, h3 = lax.ppermute(h1, "x", around[1]), lax.ppermute(h3, "x", around[3])
+    k2 = lax.ppermute(k2, "x", around[2])
+    total, send = call(sum_kernel, [vmem] * 8, (vmem,) * 2, (most, shape(block, BF16)))(
+        g0, plus, minus, h1, h3, k0, k2, send
+    )
     grad_input = (keep + lax.ppermute(send, "zh", SWAP).astype(F32)).astype(BF16)
 
     total = lax.all_to_all(total.reshape(4, 576, 128), "za", 0, 0, tiled=True)

time: 174 us -> 172 us (0.989)
  starting transfers between devices: 97.2 us -> 93 us
  waiting for transfers between devices: 47.5 us -> 50.3 us
  Pallas kernels: 20.3 us -> 18.1 us
    all_to_all x1, waiting for transfers between devices: 0.01 us -> 13.4 us  [body(): part = lax.all_to_all(part, YY, 0, 0, tiled=True)]
    ppermute x5 -> x3, starting transfers between devices: 14.2 us -> 8.17 us  [the longest x1 4.33 us: body(): lax.ppermute(plus, 'x', around[1])]
    ppermute x5 -> x3, waiting for transfers between devices: 10.4 us -> 6.69 us  [the longest x1 5.74 us: body(): k2 = lax.ppermute(k2, 'x', around[2])]
    ppermute x1, waiting for transfers between devices: 2.71 us -> 0.01 us  [body(): lax.ppermute(h1, 'x', around[1])]
    pallas_call x1, Pallas kernels: 3.21 us -> 1.18 us  [body(): call(fold_kernel, [vmem] * 6, (vmem,) * 2, (five, five))]
    ppermute x1, starting transfers between devices: 3.04 us -> 4.8 us  [body(): lax.ppermute(send, 'zb', SWAP)]
    unnamed x44 -> x48, local copies, waits for them, and re-layouts: 2.58 us -> 4.31 us
  transfers between devices with their start and end apart: 20 -> 18, of which waited for: 14 -> 10; matrix products, arithmetic and copies ran while one was open for 1% -> 1% of each run, Pallas kernels for 4% -> 3%
where the time goes in v8:
time: 172 us; the launch traced here: 169 us
  starting transfers between devices  93 us (54%)
  waiting for transfers between devices  50.3 us (29%)
  Pallas kernels  18.1 us (11%)
  local copies, waits for them, and re-layouts  4.98 us (3%)
    all_to_all x1, starting transfers between devices, body(): received = lax.all_to_all(outgoing, DP, 0, 0, tiled=True)  18.9 us
    all_to_all x1, waiting for transfers between devices, body(): part = lax.all_to_all(part, YY, 0, 0, tiled=True)  13.4 us
    ppermute x1, starting transfers between devices, body(): lax.ppermute(send, 'zh', SWAP).astype(F32)  11.9 us
    ppermute x1, starting transfers between devices, body(): x_other = lax.ppermute(x_slice, 'zh', SWAP)  11.9 us
    all_to_all x1, waiting for transfers between devices, body(): x_mine = lax.all_to_all(spread, YY, 0, 0, tiled=True)  11.2 us
    ppermute x3, starting transfers between devices, body(): lax.ppermute(w_own, 'yl', across[s])  10.1 us
    all_to_all x1, starting transfers between devices, body(): x_mine = lax.all_to_all(spread, YY, 0, 0, tiled=True)  7.1 us
    ppermute x1, waiting for transfers between devices, body(): k2 = lax.ppermute(k2, 'x', around[2])  5.74 us
  transfers between devices with their start and end apart: 18, of which 10 were waited for; matrix products, arithmetic and copies ran while one was open for 1% of the time, Pallas kernels for 3%

profile of v8, /device:TPU:6, one launch (start us, length us, event | category | flops | bytes accessed | tf_op | source)
XLA Modules:
  0.0 168.6 jit_solution(15663650665939335797)
XLA Ops:
  1.3 2.4 %shard_map.138 = bf16[32,32,128]{2,1,0:T(8,128)(2,1)} custom-call(s32[7]{0:T(128)} %stack.31.ids_ref.refs_0_, s32[4,32]{1,0:T(4,128)} %bitcast.19, s32[4,32]{1,0:T(4,128)} %bitcast.16, bf16[64,128]{1,0:T(8,128)(2,1)} %x_any.1), custom_call_target="tpu_custom_call" | custom-call | flops 1000000000 | bytes 3600000 | tf_op jit(solution)/shard_map/pallas_call | solution.py:268
  3.7 18.9 %all-to-all-start = ((bf16[32,32,128]{2,1,0:T(8,128)(2,1)}), bf16[32,32,128]{2,1,0:T(8,128)(2,1)S(1)}, u32[]{:S(2)}, u32[]{:S(2)}) async-start(bf16[32,32,128]{2,1,0:T(8,128)(2,1)} %shard_map.138), calls=%async_computation | async-start | bytes 524288 | tf_op jit(solution)/shard_map/all_to_all | solution.py:278
  22.6 3.5 %collective-permute-start = (bf16[32,4096]{1,0:T(8,128)(2,1)S(1)}, bf16[32,4096]{1,0:T(8,128)(2,1)S(1)}, u32[]{:S(2)}, u32[]{:S(2)}) collective-permute-start(bf16[32,4096]{1,0:T(8,128)(2,1)S(1)} %bitcast.21), channel_id=1, source_target_pairs={{0,2},{2,0},{4,6},{6,4},{1,3},{3,1},{5,7},{7,5},{8,10},{10,8},{12,... | collective-permute-start | bytes 786440 | tf_op jit(solution)/shard_map/ppermute | solution.py:281
  26.1 4.5 %collective-permute-start.2 = (bf16[32,4096]{1,0:T(8,128)(2,1)S(1)}, bf16[32,4096]{1,0:T(8,128)(2,1)S(1)}, u32[]{:S(2)}, u32[]{:S(2)}) collective-permute-start(bf16[32,4096]{1,0:T(8,128)(2,1)S(1)} %bitcast.22), channel_id=1, source_target_pairs={{0,4},{2,6},{4,0},{6,2},{1,5},{3,7},{5,1},{7,3},{8,12},{10,14},{12... | collective-permute-start | bytes 786440 | tf_op jit(solution)/shard_map/ppermute | solution.py:281
  30.6 2.1 %collective-permute-start.3 = (bf16[32,4096]{1,0:T(8,128)(2,1)S(1)}, bf16[32,4096]{1,0:T(8,128)(2,1)S(1)}, u32[]{:S(2)}, u32[]{:S(2)}) collective-permute-start(bf16[32,4096]{1,0:T(8,128)(2,1)S(1)} %bitcast.23), channel_id=1, source_target_pairs={{0,6},{2,4},{4,2},{6,0},{1,7},{3,5},{5,3},{7,1},{8,14},{10,12},{12... | collective-permute-start | bytes 786440 | tf_op jit(solution)/shard_map/ppermute | solution.py:281
  35.2 4.7 %all-to-all-done.x_ref = bf16[32,32,128]{2,1,0:T(8,128)(2,1)S(1)} async-done(((bf16[32,32,128]{2,1,0:T(8,128)(2,1)}), bf16[32,32,128]{2,1,0:T(8,128)(2,1)S(1)}, u32[]{:S(2)}, u32[]{:S(2)}) %all-to-all-start) | async-done | bytes 262176 | tf_op jit(solution)/shard_map/all_to_all | solution.py:278
  40.5 11.9 %collective-permute-start.1 = (bf16[128,128]{1,0:T(8,128)(2,1)S(1)}, bf16[128,128]{1,0:T(8,128)(2,1)S(1)}, u32[]{:S(2)}, u32[]{:S(2)}) collective-permute-start(bf16[128,128]{1,0:T(8,128)(2,1)S(1)} %shard_map.139.own_ref), channel_id=1, source_target_pairs={{0,16},{16,0},{1,17},{17,1},{2,18},{18,2},{3,19},{19,3},{4,20},{20... | collective-permute-start | bytes 98312 | tf_op jit(solution)/shard_map/ppermute | solution.py:288
  52.4 2.6 %collective-permute-done.1.other_ref = bf16[128,128]{1,0:T(8,128)(2,1)S(1)} collective-permute-done((bf16[128,128]{1,0:T(8,128)(2,1)S(1)}, bf16[128,128]{1,0:T(8,128)(2,1)S(1)}, u32[]{:S(2)}, u32[]{:S(2)}) %collective-permute-start.1) | collective-permute-done | bytes 32800 | tf_op jit(solution)/shard_map/ppermute | solution.py:288
  56.5 7.1 %all-to-all-start.1 = ((bf16[8,2,128,128]{3,2,1,0:T(8,128)(2,1)}), bf16[8,2,128,128]{3,2,1,0:T(8,128)(2,1)S(1)}, u32[]{:S(2)}, u32[]{:S(2)}) async-start(bf16[8,2,128,128]{3,2,1,0:T(8,128)(2,1)} %shard_map.140.refs_4_), calls=%async_computation.1 | async-start | bytes 1048576 | tf_op jit(solution)/shard_map/all_to_all | solution.py:290
  65.6 2.1 %collective-permute-start.5 = (bf16[4,32,4096]{2,1,0:T(8,128)(2,1)S(1)}, bf16[4,32,4096]{2,1,0:T(8,128)(2,1)}, u32[]{:S(2)}, u32[]{:S(2)}) collective-permute-start(bf16[4,32,4096]{2,1,0:T(8,128)(2,1)S(1)} %shard_map.141.here_ref), channel_id=1, source_target_pairs={{0,1},{1,0},{2,3},{3,2},{4,5},{5,4},{6,7},{7,6},{8,9},{9,8},{10,11... | collective-permute-start | bytes 3145736 | tf_op jit(solution)/shard_map/ppermute | solution.py:293
  67.7 11.2 %all-to-all-done.1.refs_3_ = bf16[8,2,128,128]{3,2,1,0:T(8,128)(2,1)S(1)} async-done(((bf16[8,2,128,128]{3,2,1,0:T(8,128)(2,1)}), bf16[8,2,128,128]{3,2,1,0:T(8,128)(2,1)S(1)}, u32[]{:S(2)}, u32[]{:S(2)}) %all-to-all-start.1) | async-done | bytes 524320 | tf_op jit(solution)/shard_map/all_to_all | solution.py:290
  78.9 2.0 %collective-permute-start.4 = (bf16[8,2,128,128]{3,2,1,0:T(8,128)(2,1)S(1)}, bf16[8,2,128,128]{3,2,1,0:T(8,128)(2,1)S(1)}, u32[]{:S(2)}, u32[]{:S(2)}) collective-permute-start(bf16[8,2,128,128]{3,2,1,0:T(8,128)(2,1)S(1)} %all-to-all-done.1.refs_3_), channel_id=1, source_target_pairs={{0,1},{1,0},{2,3},{3,2},{4,5},{5,4},{6,7},{7,6},{8,9},{9,8},{10,11... | collective-permute-start | bytes 1572872 | tf_op jit(solution)/shard_map/ppermute | solution.py:291
  82.8 2.5 %shard_map.143 = (bf16[128,128]{1,0:T(8,128)(2,1)S(1)}, bf16[128,128]{1,0:T(8,128)(2,1)S(1)}, bf16[256,128]{1,0:T(8,128)(2,1)S(1)}, bf16[128,256]{1,0:T(8,128)(2,1)S(1)}, bf16[32,128,128]{2,1,0:T(8,128)(2,1)S(1)}) custom-call(s32[7]{0:T(128)S(1)} %copy-done.8, s32[4,32]{1,0:T(4,128)S(1)} %bitcast.20, s32[4,32]{1,0:T(4,128)S(1)} %bitcast.18, ...), custom_call_target="tpu_custom_call" | custom-call | flops 1000000000 | bytes 3600000 | tf_op jit(solution)/shard_map/pallas_call | solution.py:299
  94.0 3.5 %all-to-all-start.2 = ((bf16[8,288,128]{2,1,0:T(8,128)(2,1)}), bf16[8,288,128]{2,1,0:T(8,128)(2,1)S(1)}, u32[]{:S(2)}, u32[]{:S(2)}) async-start(bf16[8,288,128]{2,1,0:T(8,128)(2,1)} %shard_map.146), calls=%async_computation.2 | async-start | bytes 1179648 | tf_op jit(solution)/shard_map/all_to_all | solution.py:327
  97.6 4.3 %collective-permute-start.7 = (bf16[8,256,128]{2,1,0:T(8,128)(2,1)}, bf16[8,256,128]{2,1,0:T(8,128)(2,1)S(1)}, u32[]{:S(2)}, u32[]{:S(2)}) collective-permute-start(bf16[8,256,128]{2,1,0:T(8,128)(2,1)} %copy-done.14), channel_id=1, source_target_pairs={{0,256},{256,512},{512,768},{768,0},{1,257},{257,513},{513,769},{7... | collective-permute-start | bytes 1572872 | tf_op jit(solution)/shard_map/ppermute | solution.py:328
  103.8 13.4 %all-to-all-done.2.part_ref = bf16[8,288,128]{2,1,0:T(8,128)(2,1)S(1)} async-done(((bf16[8,288,128]{2,1,0:T(8,128)(2,1)}), bf16[8,288,128]{2,1,0:T(8,128)(2,1)S(1)}, u32[]{:S(2)}, u32[]{:S(2)}) %all-to-all-start.2) | async-done | bytes 589856 | tf_op jit(solution)/shard_map/all_to_all | solution.py:327
  122.4 5.1 %collective-permute-start.9 = (bf16[5,256,128]{2,1,0:T(8,128)(2,1)S(1)}, bf16[5,256,128]{2,1,0:T(8,128)(2,1)S(1)}, u32[]{:S(2)}, u32[]{:S(2)}) collective-permute-start(bf16[5,256,128]{2,1,0:T(8,128)(2,1)S(1)} %get-tuple-element.50), channel_id=1, source_target_pairs={{0,256},{256,512},{512,768},{768,0},{1,257},{257,513},{513,769},{7... | collective-permute-start | bytes 983048 | tf_op jit(solution)/shard_map/ppermute | solution.py:334
  129.4 5.7 %collective-permute-done.11.k2_ref = bf16[8,32,128]{2,1,0:T(8,128)(2,1)S(1)} collective-permute-done((bf16[8,32,128]{2,1,0:T(8,128)(2,1)S(1)}, bf16[8,32,128]{2,1,0:T(8,128)(2,1)S(1)}, u32[]{:S(2)}, u32[]{:S(2)}) %collective-permute-start.11) | collective-permute-done | bytes 65568 | tf_op jit(solution)/shard_map/ppermute | solution.py:335
  135.2 2.1 %shard_map.149 = (bf16[8,288,128]{2,1,0:T(8,128)(2,1)}, bf16[128,128]{1,0:T(8,128)(2,1)S(1)}) custom-call(bf16[8,256,128]{2,1,0:T(8,128)(2,1)S(1)} %copy-done.21, bf16[8,256,128]{2,1,0:T(8,128)(2,1)S(1)} %collective-permute-done.7.plus_ref, bf16[8,256,128]{2,1,0:T(8,128)(2,1)} %collective-permute-done.8.minus_ref, ...), custom_call_target="tpu_custom_call" | custom-call | flops 1000000000 | bytes 3600000 | tf_op jit(solution)/shard_map/pallas_call | solution.py:336
  137.3 3.5 %all-to-all-start.3 = ((bf16[4,576,128]{2,1,0:T(8,128)(2,1)}), bf16[4,576,128]{2,1,0:T(8,128)(2,1)S(1)}, u32[]{:S(2)}, u32[]{:S(2)}) async-start(bf16[4,576,128]{2,1,0:T(8,128)(2,1)} %bitcast.10), calls=%async_computation.3 | async-start | bytes 1179648 | tf_op jit(solution)/shard_map/all_to_all | solution.py:341
  140.8 11.9 %collective-permute-start.12 = (bf16[128,128]{1,0:T(8,128)(2,1)S(1)}, bf16[128,128]{1,0:T(8,128)(2,1)S(1)}, u32[]{:S(2)}, u32[]{:S(2)}) collective-permute-start(bf16[128,128]{1,0:T(8,128)(2,1)S(1)} %get-tuple-element.55), channel_id=1, source_target_pairs={{0,16},{16,0},{1,17},{17,1},{2,18},{18,2},{3,19},{19,3},{4,20},{20... | collective-permute-start | bytes 98312 | tf_op jit(solution)/shard_map/ppermute | solution.py:339
  152.7 3.8 %all-to-all-done.3 = bf16[4,576,128]{2,1,0:T(8,128)(2,1)S(1)} async-done(((bf16[4,576,128]{2,1,0:T(8,128)(2,1)}), bf16[4,576,128]{2,1,0:T(8,128)(2,1)S(1)}, u32[]{:S(2)}, u32[]{:S(2)}) %all-to-all-start.3) | async-done | bytes 589856 | tf_op jit(solution)/shard_map/all_to_all | solution.py:341
  156.6 4.8 %collective-permute-start.13 = (bf16[288,128]{1,0:T(8,128)(2,1)S(1)}, bf16[288,128]{1,0:T(8,128)(2,1)S(1)}, u32[]{:S(2)}, u32[]{:S(2)}) collective-permute-start(bf16[288,128]{1,0:T(8,128)(2,1)S(1)} %fusion), channel_id=1, source_target_pairs={{0,128},{128,0},{1,129},{129,1},{2,130},{130,2},{3,131},{131,3},{4... | collective-permute-start | bytes 221192 | tf_op jit(solution)/shard_map/ppermute | solution.py:346
  162.0 5.4 %collective-permute-done.13.there_ref = bf16[288,128]{1,0:T(8,128)(2,1)S(1)} collective-permute-done((bf16[288,128]{1,0:T(8,128)(2,1)S(1)}, bf16[288,128]{1,0:T(8,128)(2,1)S(1)}, u32[]{:S(2)}, u32[]{:S(2)}) %collective-permute-start.13) | collective-permute-done | bytes 73760 | tf_op jit(solution)/shard_map/ppermute | solution.py:346
  (78 shorter events, 28.5 us)
Async XLA Ops:
  0.6 32.1 %copy-start = (bf16[128,4096]{1,0:T(8,128)(2,1)S(1)}, bf16[128,4096]{1,0:T(8,128)(2,1)}, u32[]{:S(2)}) copy-start(bf16[128,4096]{1,0:T(8,128)(2,1)} %param.15) | copy-start | bytes 3145732
  1.3 21.3 %copy-start.15 = (bf16[4096,32]{0,1:T(8,128)(2,1)S(1)}, bf16[4096,32]{0,1:T(8,128)(2,1)}, u32[]{:S(2)}) copy-start(bf16[4096,32]{0,1:T(8,128)(2,1)} %param.14) | copy-start | bytes 786436
  1.3 31.4 %copy-start.1 = (bf16[128,4096]{1,0:T(8,128)(2,1)S(1)}, bf16[128,4096]{1,0:T(8,128)(2,1)}, u32[]{:S(2)}) copy-start(bf16[128,4096]{1,0:T(8,128)(2,1)} %go_ref.1) | copy-start | bytes 3145732
  3.7 36.2 %copy-start.8 = (s32[7]{0:T(128)S(1)}, s32[7]{0:T(128)}, u32[]{:S(2)}) copy-start(s32[7]{0:T(128)} %stack.31.ids_ref.refs_0_) | copy-start | bytes 88
  3.7 36.2 %copy-start.9 = (s32[32,4]{0,1:T(4,128)S(1)}, s32[32,4]{0,1:T(4,128)}, u32[]{:S(2)}) copy-start(s32[32,4]{0,1:T(4,128)} %param.17) | copy-start | bytes 1540
  3.7 36.2 %all-to-all-start = ((bf16[32,32,128]{2,1,0:T(8,128)(2,1)}), bf16[32,32,128]{2,1,0:T(8,128)(2,1)S(1)}, u32[]{:S(2)}, u32[]{:S(2)}) async-start(bf16[32,32,128]{2,1,0:T(8,128)(2,1)} %shard_map.138), calls=%async_computation | async-start | bytes 524288 | tf_op jit(solution)/shard_map/all_to_all | solution.py:278
  22.6 12.6 %collective-permute-start = (bf16[32,4096]{1,0:T(8,128)(2,1)S(1)}, bf16[32,4096]{1,0:T(8,128)(2,1)S(1)}, u32[]{:S(2)}, u32[]{:S(2)}) collective-permute-start(bf16[32,4096]{1,0:T(8,128)(2,1)S(1)} %bitcast.21), channel_id=1, source_target_pairs={{0,2},{2,0},{4,6},{6,4},{1,3},{3,1},{5,7},{7,5},{8,10},{10,8},{12,... | collective-permute-start | bytes 786440 | tf_op jit(solution)/shard_map/ppermute | solution.py:281
  26.1 26.3 %collective-permute-start.2 = (bf16[32,4096]{1,0:T(8,128)(2,1)S(1)}, bf16[32,4096]{1,0:T(8,128)(2,1)S(1)}, u32[]{:S(2)}, u32[]{:S(2)}) collective-permute-start(bf16[32,4096]{1,0:T(8,128)(2,1)S(1)} %bitcast.22), channel_id=1, source_target_pairs={{0,4},{2,6},{4,0},{6,2},{1,5},{3,7},{5,1},{7,3},{8,12},{10,14},{12... | collective-permute-start | bytes 786440 | tf_op jit(solution)/shard_map/ppermute | solution.py:281
  30.6 21.8 %collective-permute-start.3 = (bf16[32,4096]{1,0:T(8,128)(2,1)S(1)}, bf16[32,4096]{1,0:T(8,128)(2,1)S(1)}, u32[]{:S(2)}, u32[]{:S(2)}) collective-permute-start(bf16[32,4096]{1,0:T(8,128)(2,1)S(1)} %bitcast.23), channel_id=1, source_target_pairs={{0,6},{2,4},{4,2},{6,0},{1,7},{3,5},{5,3},{7,1},{8,14},{10,12},{12... | collective-permute-start | bytes 786440 | tf_op jit(solution)/shard_map/ppermute | solution.py:281
  40.5 14.5 %collective-permute-start.1 = (bf16[128,128]{1,0:T(8,128)(2,1)S(1)}, bf16[128,128]{1,0:T(8,128)(2,1)S(1)}, u32[]{:S(2)}, u32[]{:S(2)}) collective-permute-start(bf16[128,128]{1,0:T(8,128)(2,1)S(1)} %shard_map.139.own_ref), channel_id=1, source_target_pairs={{0,16},{16,0},{1,17},{17,1},{2,18},{18,2},{3,19},{19,3},{4,20},{20... | collective-permute-start | bytes 98312 | tf_op jit(solution)/shard_map/ppermute | solution.py:288
  56.5 22.4 %all-to-all-start.1 = ((bf16[8,2,128,128]{3,2,1,0:T(8,128)(2,1)}), bf16[8,2,128,128]{3,2,1,0:T(8,128)(2,1)S(1)}, u32[]{:S(2)}, u32[]{:S(2)}) async-start(bf16[8,2,128,128]{3,2,1,0:T(8,128)(2,1)} %shard_map.140.refs_4_), calls=%async_computation.1 | async-start | bytes 1048576 | tf_op jit(solution)/shard_map/all_to_all | solution.py:290
  65.6 15.3 %collective-permute-start.5 = (bf16[4,32,4096]{2,1,0:T(8,128)(2,1)S(1)}, bf16[4,32,4096]{2,1,0:T(8,128)(2,1)}, u32[]{:S(2)}, u32[]{:S(2)}) collective-permute-start(bf16[4,32,4096]{2,1,0:T(8,128)(2,1)S(1)} %shard_map.141.here_ref), channel_id=1, source_target_pairs={{0,1},{1,0},{2,3},{3,2},{4,5},{5,4},{6,7},{7,6},{8,9},{9,8},{10,11... | collective-permute-start | bytes 3145736 | tf_op jit(solution)/shard_map/ppermute | solution.py:293
  78.9 3.9 %collective-permute-start.4 = (bf16[8,2,128,128]{3,2,1,0:T(8,128)(2,1)S(1)}, bf16[8,2,128,128]{3,2,1,0:T(8,128)(2,1)S(1)}, u32[]{:S(2)}, u32[]{:S(2)}) collective-permute-start(bf16[8,2,128,128]{3,2,1,0:T(8,128)(2,1)S(1)} %all-to-all-done.1.refs_3_), channel_id=1, source_target_pairs={{0,1},{1,0},{2,3},{3,2},{4,5},{5,4},{6,7},{7,6},{8,9},{9,8},{10,11... | collective-permute-start | bytes 1572872 | tf_op jit(solution)/shard_map/ppermute | solution.py:291
  87.4 5.7 %collective-permute-start.6 = (bf16[8,288,128]{2,1,0:T(8,128)(2,1)S(1)}, bf16[8,288,128]{2,1,0:T(8,128)(2,1)S(1)}, u32[]{:S(2)}, u32[]{:S(2)}) collective-permute-start(bf16[8,288,128]{2,1,0:T(8,128)(2,1)S(1)} %get-tuple-element.40), channel_id=1, source_target_pairs={{0,1},{1,0},{2,3},{3,2},{4,5},{5,4},{6,7},{7,6},{8,9},{9,8},{10,11... | collective-permute-start | bytes 1769480 | tf_op jit(solution)/shard_map/ppermute | solution.py:320
  93.0 24.2 %copy-start.12 = (bf16[32,128,128]{2,1,0:T(8,128)(2,1)S(1)}, bf16[32,128,128]{2,1,0:T(8,128)(2,1)}, u32[]{:S(2)}) copy-start(bf16[32,128,128]{2,1,0:T(8,128)(2,1)} %copy-done.11) | copy-start | bytes 3145732
  94.0 23.2 %all-to-all-start.2 = ((bf16[8,288,128]{2,1,0:T(8,128)(2,1)}), bf16[8,288,128]{2,1,0:T(8,128)(2,1)S(1)}, u32[]{:S(2)}, u32[]{:S(2)}) async-start(bf16[8,288,128]{2,1,0:T(8,128)(2,1)} %shard_map.146), calls=%async_computation.2 | async-start | bytes 1179648 | tf_op jit(solution)/shard_map/all_to_all | solution.py:327
  97.6 20.7 %collective-permute-start.7 = (bf16[8,256,128]{2,1,0:T(8,128)(2,1)}, bf16[8,256,128]{2,1,0:T(8,128)(2,1)S(1)}, u32[]{:S(2)}, u32[]{:S(2)}) collective-permute-start(bf16[8,256,128]{2,1,0:T(8,128)(2,1)} %copy-done.14), channel_id=1, source_target_pairs={{0,256},{256,512},{512,768},{768,0},{1,257},{257,513},{513,769},{7... | collective-permute-start | bytes 1572872 | tf_op jit(solution)/shard_map/ppermute | solution.py:328
  101.9 17.3 %collective-permute-start.8 = (bf16[8,256,128]{2,1,0:T(8,128)(2,1)}, bf16[8,256,128]{2,1,0:T(8,128)(2,1)}, u32[]{:S(2)}, u32[]{:S(2)}) collective-permute-start(bf16[8,256,128]{2,1,0:T(8,128)(2,1)} %copy-done.13), channel_id=1, source_target_pairs={{0,768},{256,0},{512,256},{768,512},{1,769},{257,1},{513,257},{769... | collective-permute-start | bytes 1572872 | tf_op jit(solution)/shard_map/ppermute | solution.py:328
  120.4 14.7 %collective-permute-start.10 = (bf16[5,256,128]{2,1,0:T(8,128)(2,1)S(1)}, bf16[5,256,128]{2,1,0:T(8,128)(2,1)S(1)}, u32[]{:S(2)}, u32[]{:S(2)}) collective-permute-start(bf16[5,256,128]{2,1,0:T(8,128)(2,1)S(1)} %get-tuple-element.51), channel_id=1, source_target_pairs={{0,768},{256,0},{512,256},{768,512},{1,769},{257,1},{513,257},{769... | collective-permute-start | bytes 983048 | tf_op jit(solution)/shard_map/ppermute | solution.py:334
  122.4 12.8 %collective-permute-start.9 = (bf16[5,256,128]{2,1,0:T(8,128)(2,1)S(1)}, bf16[5,256,128]{2,1,0:T(8,128)(2,1)S(1)}, u32[]{:S(2)}, u32[]{:S(2)}) collective-permute-start(bf16[5,256,128]{2,1,0:T(8,128)(2,1)S(1)} %get-tuple-element.50), channel_id=1, source_target_pairs={{0,256},{256,512},{512,768},{768,0},{1,257},{257,513},{513,769},{7... | collective-permute-start | bytes 983048 | tf_op jit(solution)/shard_map/ppermute | solution.py:334
  127.5 7.7 %collective-permute-start.11 = (bf16[8,32,128]{2,1,0:T(8,128)(2,1)S(1)}, bf16[8,32,128]{2,1,0:T(8,128)(2,1)S(1)}, u32[]{:S(2)}, u32[]{:S(2)}) collective-permute-start(bf16[8,32,128]{2,1,0:T(8,128)(2,1)S(1)} %get-tuple-element.53), channel_id=1, source_target_pairs={{0,512},{256,768},{512,0},{768,256},{1,513},{257,769},{513,1},{769... | collective-permute-start | bytes 196616 | tf_op jit(solution)/shard_map/ppermute | solution.py:335
  137.3 19.2 %all-to-all-start.3 = ((bf16[4,576,128]{2,1,0:T(8,128)(2,1)}), bf16[4,576,128]{2,1,0:T(8,128)(2,1)S(1)}, u32[]{:S(2)}, u32[]{:S(2)}) async-start(bf16[4,576,128]{2,1,0:T(8,128)(2,1)} %bitcast.10), calls=%async_computation.3 | async-start | bytes 1179648 | tf_op jit(solution)/shard_map/all_to_all | solution.py:341
  140.8 20.6 %collective-permute-start.12 = (bf16[128,128]{1,0:T(8,128)(2,1)S(1)}, bf16[128,128]{1,0:T(8,128)(2,1)S(1)}, u32[]{:S(2)}, u32[]{:S(2)}) collective-permute-start(bf16[128,128]{1,0:T(8,128)(2,1)S(1)} %get-tuple-element.55), channel_id=1, source_target_pairs={{0,16},{16,0},{1,17},{17,1},{2,18},{18,2},{3,19},{19,3},{4,20},{20... | collective-permute-start | bytes 98312 | tf_op jit(solution)/shard_map/ppermute | solution.py:339
  156.6 10.9 %collective-permute-start.13 = (bf16[288,128]{1,0:T(8,128)(2,1)S(1)}, bf16[288,128]{1,0:T(8,128)(2,1)S(1)}, u32[]{:S(2)}, u32[]{:S(2)}) collective-permute-start(bf16[288,128]{1,0:T(8,128)(2,1)S(1)} %fusion), channel_id=1, source_target_pairs={{0,128},{128,0},{1,129},{129,1},{2,130},{130,2},{3,131},{131,3},{4... | collective-permute-start | bytes 221192 | tf_op jit(solution)/shard_map/ppermute | solution.py:346
  (18 other events, 130.5 us)
